TPU v7x, 32 devices: a whole 2x2x4 slice. The times are simulated.
32 devices in a mesh: ang: 8 (over y, x, core), row: 4 (over z).
Axes of the slice: x: 2, y: 2, z: 4, core: 2. Of those that a mesh axis runs over, the one named last changes fastest.
Arguments:
- sinogram: float32 [256, 8, 4096], P('ang', 'row'), may hold values from -3 to 16
- col_weights: bfloat16 [32, 256, 128], replicated
- col_start: int32 [32], replicated, may hold values from 0 to 3840, as said below
- view_offset: int32 [32], replicated, may hold values from -32 to 29, as said below
- row_offset: int32 [32], replicated, may hold values from -2 to 1, as said below
- conj_offset: int32 [32], replicated, may hold values from -16 to 16, as said below
- ang_weights: float32 [4, 4096], replicated, may hold values from -0.5 to 1
- row_weights: float32 [2, 4096], replicated, may hold values from 0 to 1
Outputs:
- filtered: float32 [256, 8, 8192], P('ang', 'row')
Inputs may be any that keep to these rules, and one draw needn't show every extreme that they name: `col_start`: both ends are taken by some column tile in every draw. `view_offset`: both ends are taken by some column tile in every draw. `row_offset`: both ends are taken by some column tile in every draw. `conj_offset`: both ends are taken by some column tile in every draw.
All inputs are finite; a program needn't handle non-finite values.
Results may differ from a plain program's by a relative error of at most 0.0003.
Values sent between devices are 32-bit elements; how exact they have to be, the bound alone decides.
No kernel may reach another device: no remote copies, remote signals or barrier semaphores. Data moves between devices by JAX's collectives and lax.ppermute only.
A program may use at most 64 MiB of HBM per device.

v0:
```python
import math

import jax
import jax.numpy as jnp
from jax import lax
from jax.sharding import PartitionSpec as P

KR = 256


highest = lax.Precision.HIGHEST


def padded(x, sides, width, wrap):
    for axis, dim in sides:
        count, length = (lax.axis_size(axis), x.shape[dim])
        up = [(i, (i + 1) % count) for i in range(count if wrap else count - 1)]
        down = [(j, i) for i, j in up]
        last = lax.slice_in_dim(x, length - width, length, axis=dim)
        initial = lax.slice_in_dim(x, 0, width, axis=dim)
        before = lax.ppermute(last, axis, up)
        after = lax.ppermute(initial, axis, down)
        x = jnp.concatenate([before, x, after], axis=dim)
    return x


def passed_along(value, axis, steps):
    count = lax.axis_size(axis)
    pairs = [(source, (source + steps) % count) for source in range(count)]
    return lax.ppermute(value, axis, pairs)


def ramp_kernel(lag, reach):
    lag_float = lag.astype(jnp.float32)
    odd_lag = lag % 2 != 0
    inverse = -1.0 / (math.pi * math.pi * jnp.maximum(lag_float * lag_float, 1.0))
    values = jnp.where(lag == 0, 0.25, jnp.where(odd_lag, inverse, 0.0))
    values = jnp.where(jnp.abs(lag) <= reach, values, 0.0)
    return values


def resample_columns(block, col_weights, col_start):
    tile_count = col_weights.shape[0]
    band_width = col_weights.shape[1]
    pieces = []
    for tile_index in range(tile_count):
        slab = lax.dynamic_slice_in_dim(block, col_start[tile_index], band_width, axis=2)
        weights = col_weights[tile_index].astype(jnp.float32)
        pieces.append(
            jnp.einsum(
                "vrb,bc->vrc", slab, weights, precision=highest, preferred_element_type=jnp.float32
            )
        )
    return jnp.concatenate(pieces, axis=2)


def interpolate_rows(widened, row_offset, row_weights, row_count, width_tile):
    pieces = []
    for tile_index in range(row_offset.shape[0]):
        first = tile_index * width_tile
        columns = widened[:, :, first : first + width_tile]
        start = row_count + row_offset[tile_index]
        lower = lax.dynamic_slice_in_dim(columns, start, row_count, axis=1)
        upper = lax.dynamic_slice_in_dim(columns, start + 1, row_count, axis=1)
        mixed = (
            row_weights[0, first : first + width_tile] * lower
            + row_weights[1, first : first + width_tile] * upper
        )
        pieces.append(mixed)
    return jnp.concatenate(pieces, axis=2)


def interpolate_views(beside_all, view_offset, ang_weights, view_count, width_tile):
    pieces = []
    for tile_index in range(view_offset.shape[0]):
        first = tile_index * width_tile
        columns = beside_all[:, :, first : first + width_tile]
        total = jnp.zeros((view_count, beside_all.shape[1], width_tile), jnp.float32)
        for angle_tap in range(ang_weights.shape[0]):
            picked = lax.dynamic_slice_in_dim(
                columns, view_count + view_offset[tile_index] + angle_tap, view_count, axis=0
            )
            total = total + ang_weights[angle_tap, first : first + width_tile] * picked
        pieces.append(total)
    return jnp.concatenate(pieces, axis=2)


def conjugate_views(partner, conj_offset, margin_views, view_count, width_tile):
    tile_count = conj_offset.shape[0]
    pieces = []
    for tile_index in range(tile_count):
        mirror = (tile_count - 1 - tile_index) * width_tile
        columns = partner[:, :, mirror : mirror + width_tile][:, :, ::-1]
        pieces.append(
            lax.dynamic_slice_in_dim(
                columns, margin_views + conj_offset[tile_index], view_count, axis=0
            )
        )
    return jnp.concatenate(pieces, axis=2)


def ramp_filter(parallel, conjugate, width_tile):
    sections = 1 + KR // width_tile
    leading = jnp.arange(width_tile, dtype=jnp.int32)[None, :, None]
    trailing = jnp.arange(2 * width_tile, dtype=jnp.int32)[None, None, :]
    section_ids = jnp.arange(sections, dtype=jnp.int32)[:, None, None]
    lag_even = trailing - 2 * width_tile * section_ids - 2 * leading + KR
    kernel_even = ramp_kernel(lag_even, KR)
    kernel_odd = ramp_kernel(lag_even - 1, KR)
    tile_count = parallel.shape[2] // width_tile
    margin = ((0, 0), (0, 0), (KR // 2, KR // 2))
    par_blocks = jnp.pad(parallel, margin).reshape(
        parallel.shape[0], parallel.shape[1], -1, width_tile
    )
    conj_blocks = jnp.pad(conjugate, margin).reshape(
        parallel.shape[0], parallel.shape[1], -1, width_tile
    )
    total = jnp.zeros(
        (parallel.shape[0], parallel.shape[1], tile_count, 2 * width_tile), jnp.float32
    )
    for section_index in range(sections):
        total = total + jnp.einsum(
            "vrqa,ab->vrqb",
            par_blocks[:, :, section_index : section_index + tile_count],
            kernel_even[section_index],
            precision=highest,
            preferred_element_type=jnp.float32,
        )
        total = total + jnp.einsum(
            "vrqa,ab->vrqb",
            conj_blocks[:, :, section_index : section_index + tile_count],
            kernel_odd[section_index],
            precision=highest,
            preferred_element_type=jnp.float32,
        )
    return total.reshape(parallel.shape[0], parallel.shape[1], -1)


def on_device(
    sinogram, col_weights, col_start, view_offset, row_offset, conj_offset, ang_weights, row_weights
):
    view_count = sinogram.shape[0]
    row_count = sinogram.shape[1]
    width_tile = col_weights.shape[2]
    own_rows = resample_columns(sinogram, col_weights, col_start)
    widened = padded(own_rows, (("row", 1),), row_count, False)
    rowed = interpolate_rows(widened, row_offset, row_weights, row_count, width_tile)
    beside_all = padded(rowed, (("ang", 0),), view_count, True)
    parallel = interpolate_views(beside_all, view_offset, ang_weights, view_count, width_tile)
    halfway = lax.axis_size("ang") // 2
    margin_views = view_count // 2
    extended = padded(parallel, (("ang", 0),), margin_views, True)
    partner = passed_along(extended, "ang", halfway)
    conjugate = conjugate_views(partner, conj_offset, margin_views, view_count, width_tile)
    return ramp_filter(parallel, conjugate, width_tile)


def solution(mesh):
    return jax.shard_map(
        on_device,
        mesh=mesh,
        in_specs=(P("ang", "row", None), P(), P(), P(), P(), P(), P(), P()),
        out_specs=P("ang", "row", None),
        check_vma=False,
    )
```

profile of v0, /device:TPU:11, one launch (start us, length us, event | category | flops | bytes accessed | tf_op | source)
XLA Modules:
  0.0 486.9 jit_solution(15994426701091513885)
XLA Ops:
  0.0 1.8 fusion.471
  18.2 2.1 fusion.470
  64.1 2.5 constant_dynamic-slice_fusion.242
  93.0 2.1 collective-permute-start.1
  95.1 3.2 collective-permute-start
  348.8 22.8 %collective-permute-done.3 = f32[32,2,4096]{2,0,1:T(8,128)S(1)} collective-permute-done((f32[32,2,4096]{2,0,1:T(8,128)S(1)}, f32[32,2,4096]{2,0,1:T(8,128)S(1)}, u32[]{:S(2)}, u32[]{:S(2)}) %collective-permute-start.3) | collective-permute-done | bytes 1048608 | tf_op jit(solution)/shard_map/ppermute | solution.py:22
  373.7 2.3 collective-permute-start.4
  422.4 1.8 fusion.9
  424.2 3.1 fusion.5
  427.3 3.1 fusion.1
  430.4 10.6 %collective-permute-done.6 = f32[64,2,4096]{2,0,1:T(8,128)} collective-permute-done((f32[64,2,4096]{2,0,1:T(8,128)}, f32[64,2,4096]{2,0,1:T(8,128)}, u32[]{:S(2)}, u32[]{:S(2)}) %collective-permute-start.6) | collective-permute-done | bytes 2097184 | tf_op jit(solution)/shard_map/ppermute | solution.py:30
  443.2 2.0 fusion.460
  445.2 1.6 rev.108
  446.8 1.5 rev.107
  448.3 1.5 rev.106
  449.9 1.5 rev.105
  451.4 1.6 rev.104
  452.9 1.5 rev.103
  456.0 1.5 rev.101
  457.6 1.6 rev.100
  476.2 1.8 fusion.3
  478.0 1.8 fusion.7
  479.9 3.5 add_add_fusion
  483.4 3.6 reshape.1131
  (224 shorter events, 63.1 us)
Async XLA Ops:
  0.0 66.6 %copy-start.3 = (bf16[32,256,128]{2,1,0:T(8,128)(2,1)S(1)}, bf16[32,256,128]{2,1,0:T(8,128)(2,1)}, u32[]{:S(2)}) copy-start(bf16[32,256,128]{2,1,0:T(8,128)(2,1)} %param.9) | copy-start | bytes 6291460
  54.5 23.0 %copy-start.2 = (f32[32,2,4096]{2,1,0:T(2,128)S(1)}, f32[32,2,4096]{2,1,0:T(2,128)}, u32[]{:S(2)}) copy-start(f32[32,2,4096]{2,1,0:T(2,128)} %param.8) | copy-start | bytes 3145732
  77.5 20.8 %copy-start.5 = (s32[32]{0:T(128)S(1)}, s32[32]{0:T(128)}, u32[]{:S(2)}) copy-start(s32[32]{0:T(128)} %param.11) | copy-start | bytes 388
  78.9 85.9 %copy-start.6 = (s32[32]{0:T(128)S(1)}, s32[32]{0:T(128)}, u32[]{:S(2)}) copy-start(s32[32]{0:T(128)} %param.12) | copy-start | bytes 388
  81.3 260.5 %copy-start.12 = (f32[2,4096]{1,0:T(2,128)S(1)}, f32[2,4096]{1,0:T(2,128)}, u32[]{:S(2)}) copy-start(f32[2,4096]{1,0:T(2,128)} %param.15) | copy-start | bytes 98308
  85.2 258.1 %copy-start.11 = (f32[4,4096]{1,0:T(4,128)S(1)}, f32[4,4096]{1,0:T(4,128)}, u32[]{:S(2)}) copy-start(f32[4,4096]{1,0:T(4,128)} %param.14) | copy-start | bytes 196612
  93.0 250.3 %collective-permute-start.1 = (f32[32,2,4096]{2,0,1:T(8,128)}, f32[32,2,4096]{2,0,1:T(8,128)S(1)}, u32[]{:S(2)}, u32[]{:S(2)}) collective-permute-start(f32[32,2,4096]{2,0,1:T(8,128)} %convolution_dynamic-update-slice_fusion), channel_id=1, source_target_pairs={{1,0},{2,1},{3,2},{5,4},{6,5},{7,6},{9,8},{10,9},{11,10},{13,12},{... | collective-permute-start | bytes 3145736 | tf_op jit(solution)/shard_map/ppermute | solution.py:22
  95.1 248.3 %collective-permute-start = (f32[32,2,4096]{2,0,1:T(8,128)}, f32[32,2,4096]{2,0,1:T(8,128)S(1)}, u32[]{:S(2)}, u32[]{:S(2)}) collective-permute-start(f32[32,2,4096]{2,0,1:T(8,128)} %convolution_dynamic-update-slice_fusion), channel_id=1, source_target_pairs={{0,1},{1,2},{2,3},{4,5},{5,6},{6,7},{8,9},{9,10},{10,11},{12,13},{... | collective-permute-start | bytes 3145736 | tf_op jit(solution)/shard_map/ppermute | solution.py:21
  346.0 25.6 %collective-permute-start.3 = (f32[32,2,4096]{2,0,1:T(8,128)S(1)}, f32[32,2,4096]{2,0,1:T(8,128)S(1)}, u32[]{:S(2)}, u32[]{:S(2)}) collective-permute-start(f32[32,2,4096]{2,0,1:T(8,128)S(1)} %constant_dynamic-update-slice_fusion), channel_id=1, source_target_pairs={{4,0},{8,4},{12,8},{16,12},{20,16},{24,20},{28,24},{0,28},{5,1},{9... | collective-permute-start | bytes 3145736 | tf_op jit(solution)/shard_map/ppermute | solution.py:22
  347.3 24.3 %collective-permute-start.2 = (f32[32,2,4096]{2,0,1:T(8,128)S(1)}, f32[32,2,4096]{2,0,1:T(8,128)S(1)}, u32[]{:S(2)}, u32[]{:S(2)}) collective-permute-start(f32[32,2,4096]{2,0,1:T(8,128)S(1)} %constant_dynamic-update-slice_fusion), channel_id=1, source_target_pairs={{0,4},{4,8},{8,12},{12,16},{16,20},{20,24},{24,28},{28,0},{1,5},{5... | collective-permute-start | bytes 3145736 | tf_op jit(solution)/shard_map/ppermute | solution.py:21
  373.1 2.9 copy-start.7
  373.7 19.1 %collective-permute-start.4 = (f32[16,2,4096]{2,0,1:T(8,128)S(1)}, f32[16,2,4096]{2,0,1:T(8,128)S(1)}, u32[]{:S(2)}, u32[]{:S(2)}) collective-permute-start(f32[16,2,4096]{2,0,1:T(8,128)S(1)} %get-tuple-element.107), channel_id=1, source_target_pairs={{0,4},{4,8},{8,12},{12,16},{16,20},{20,24},{24,28},{28,0},{1,5},{5... | collective-permute-start | bytes 1572872 | tf_op jit(solution)/shard_map/ppermute | solution.py:21
  376.0 16.8 %collective-permute-start.5 = (f32[16,2,4096]{2,0,1:T(8,128)S(1)}, f32[16,2,4096]{2,0,1:T(8,128)S(1)}, u32[]{:S(2)}, u32[]{:S(2)}) collective-permute-start(f32[16,2,4096]{2,0,1:T(8,128)S(1)} %get-tuple-element.108), channel_id=1, source_target_pairs={{4,0},{8,4},{12,8},{16,12},{20,16},{24,20},{28,24},{0,28},{5,1},{9... | collective-permute-start | bytes 1572872 | tf_op jit(solution)/shard_map/ppermute | solution.py:22
  394.3 46.7 %collective-permute-start.6 = (f32[64,2,4096]{2,0,1:T(8,128)}, f32[64,2,4096]{2,0,1:T(8,128)}, u32[]{:S(2)}, u32[]{:S(2)}) collective-permute-start(f32[64,2,4096]{2,0,1:T(8,128)} %pad_maximum_fusion.2), channel_id=1, source_target_pairs={{0,16},{4,20},{8,24},{12,28},{16,0},{20,4},{24,8},{28,12},{1,17},{... | collective-permute-start | bytes 6291464 | tf_op jit(solution)/shard_map/ppermute | solution.py:30
  459.9 12.4 %copy-start.9 = (f32[64,2,128]{2,0,1:T(8,128)S(1)}, f32[64,2,128]{2,0,1:T(8,128)}, u32[]{:S(2)}) copy-start(f32[64,2,128]{2,0,1:T(8,128)} %rev.108) | copy-start | bytes 196612
  460.6 11.6 %copy-start.10 = (f32[64,2,128]{2,0,1:T(8,128)S(1)}, f32[64,2,128]{2,0,1:T(8,128)}, u32[]{:S(2)}) copy-start(f32[64,2,128]{2,0,1:T(8,128)} %rev.107) | copy-start | bytes 196612
  462.1 10.5 %copy-start.8 = (f32[64,2,128]{2,0,1:T(8,128)S(1)}, f32[64,2,128]{2,0,1:T(8,128)}, u32[]{:S(2)}) copy-start(f32[64,2,128]{2,0,1:T(8,128)} %rev.127) | copy-start | bytes 196612
  475.2 1.0 copy-start.4
  476.2 3.6 copy-start.1
  478.0 1.8 copy-start
where the time goes:
time: 496 us; the launch traced here: 487 us
  between operations  343 us (69%)
  local copies, waits for them, and re-layouts  52.1 us (11%)
  matrix products  40.2 us (8%)
  waiting for transfers between devices  33.4 us (7%)
  starting transfers between devices  11.5 us (2%)
  other arithmetic  6.46 us (1%)
    dot_general x32, matrix products, resample_columns(): jnp.einsum('vrb,bc->vrc', slab, weights, precision=highest, preferred_ele...  25 us
    ppermute x3, waiting for transfers between devices, padded(): after = lax.ppermute(initial, axis, down)  22.8 us
    rev x32, local copies, waits for them, and re-layouts, conjugate_views(): columns = partner[:, :, mirror:mirror + width_tile][:, :, ::-1]  19 us
    ppermute x1, waiting for transfers between devices, passed_along(): return lax.ppermute(value, axis, pairs)  10.6 us
  transfers between devices with their start and end apart: 7, of which 2 were waited for; matrix products, arithmetic and copies ran while one was open for 3% of the time, Pallas kernels for 0%

commit v1 on v0

v1 whole, which is shorter than its diff:
```python
import functools
import math

import jax
import jax.numpy as jnp
import numpy as np
from jax import lax
from jax.experimental import pallas as pl
from jax.experimental.pallas import tpu as pltpu
from jax.sharding import PartitionSpec as P

KR = 256
LANES = 128
WINDOW = 3 * LANES
WRAP = 72
VMEM = pl.BlockSpec(memory_space=pltpu.VMEM)
SMEM = pl.BlockSpec(memory_space=pltpu.SMEM)
PARAMS = pltpu.CompilerParams(vmem_limit_bytes=48 * 1024 * 1024)


def call(body, outs, scratch, args, flops, moved):
    smem = [a.dtype == jnp.int32 for a in args]
    return pl.pallas_call(
        body,
        out_shape=outs,
        in_specs=[SMEM if s else VMEM for s in smem],
        out_specs=[VMEM] * len(outs),
        scratch_shapes=scratch,
        compiler_params=PARAMS,
        cost_estimate=pl.CostEstimate(flops=flops, bytes_accessed=moved, transcendentals=0),
    )(*args)


def f32(*shape):
    return jax.ShapeDtypeStruct(shape, jnp.float32)


def tile_of(index, group, tiles):
    first, half = group
    return jnp.where(index < half, first + index, tiles - first - 2 * half + index)


def split(x):
    high = x.astype(jnp.bfloat16)
    low = (x - high.astype(jnp.float32)).astype(jnp.bfloat16)
    return high, low


def dot(a, b):
    return jnp.dot(a, b, preferred_element_type=jnp.float32)


def resample_body(group, start_ref, sino_ref, weights_ref, out_ref):
    tiles, band, _ = weights_ref.shape
    views, rows, cols = sino_ref.shape

    def step(index, carry):
        tile = tile_of(index, group, tiles)
        start = start_ref[tile]
        base = jnp.minimum(start // LANES * LANES, cols - WINDOW)
        shift = start - base
        slab = sino_ref[:, :, pl.ds(pl.multiple_of(base, LANES), WINDOW)]
        slab = slab.reshape(views * rows, WINDOW)
        slab = pltpu.roll(slab, WINDOW - shift, 1)[:, :band]
        high, low = split(slab)
        weights = weights_ref[tile]
        out_ref[index] = dot(high, weights) + dot(low, weights)
        return carry

    lax.fori_loop(0, 2 * group[1], step, 0, unroll=2)


def resample(group, start, sino, weights):
    views, rows, cols = sino.shape
    count = 2 * group[1]
    flops = 4 * count * views * rows * weights.shape[1] * LANES
    return call(
        functools.partial(resample_body, group),
        [f32(count, views * rows, LANES)],
        [],
        (start, sino, weights),
        flops,
        6 << 20,
    )[0]


def rows_body(group, tiles, offset_ref, prev_ref, own_ref, next_ref, weights_ref, keep_ref, send_ref, stack):
    count, height, _ = own_ref.shape
    views = height // 2
    core = lax.axis_index("ang") % 2

    def step(index, slot):
        tile = tile_of(index, group, tiles)
        offset = offset_ref[tile]
        stack[slot, 0:height] = prev_ref[index]
        stack[slot, height : 2 * height] = own_ref[index]
        stack[slot, 2 * height : 3 * height] = next_ref[index]
        weights = weights_ref[:, pl.ds(pl.multiple_of(tile * LANES, LANES), LANES)]

        def picked(row):
            lifted = row + 2
            first = lifted // 2 * height + lifted % 2
            return stack[slot, pl.ds(first, views, stride=2), :]

        for out_ref, row in ((keep_ref, core), (send_ref, 1 - core)):
            lower = picked(row + offset)
            upper = picked(row + offset + 1)
            out_ref[index] = weights[0:1] * lower + weights[1:2] * upper

    def pair(index, carry):
        step(2 * index, 0)
        step(2 * index + 1, 1)
        return carry

    lax.fori_loop(0, count // 2, pair, 0)


def interpolate_rows(group, tiles, offset, prev, own, after, weights):
    count, height, _ = own.shape
    return call(
        functools.partial(rows_body, group, tiles),
        [f32(count, height // 2, LANES)] * 2,
        [pltpu.VMEM((2, 3 * height, LANES), jnp.float32)],
        (offset, prev, own, after, weights),
        count * height * LANES * 4,
        count * height * LANES * 16,
    )


def views_body(group, tiles, chips, places, view_ref, conj_ref, weights_ref, *refs):
    blocks = refs[: len(places)]
    keep_ref, send_ref, stack = refs[len(places) :]
    count, chip_views = keep_ref.shape[0], 2 * keep_ref.shape[2]
    views = chip_views // 2
    turn = chips * chip_views
    index_ang = lax.axis_index("ang")
    chip, core = index_ang // 2, index_ang % 2
    taps = weights_ref.shape[0]

    def step(index, slot):
        tile = tile_of(index, group, tiles)
        for ref, (place, low, high) in zip(blocks, places):

            def put(ref=ref, place=place, low=low):
                at = place(chip) * chip_views
                mine = pl.multiple_of(at + core * views, 8)
                other = pl.multiple_of(at + (1 - core) * views, 8)
                stack[slot, pl.ds(mine, views)] = ref[index - low, 0:views]
                stack[slot, pl.ds(other, views)] = ref[index - low, views:chip_views]

            if low == 0 and high == count:
                put()
            else:
                pl.when((index >= low) & (index < high))(put)
        stack[slot, turn : turn + WRAP] = stack[slot, 0:WRAP]
        weights = weights_ref[:, pl.ds(pl.multiple_of(tile * LANES, LANES), LANES)]
        shift = view_ref[tile]
        opposite = shift + conj_ref[tiles - 1 - tile] + turn // 2
        for part, by in ((0, shift), (1, opposite)):
            for out_ref, first in ((keep_ref, core), (send_ref, 1 - core)):
                begin = lax.rem(chip * chip_views + first * views + by + turn, turn)
                total = weights[0:1] * stack[slot, pl.ds(begin, views)]
                for tap in range(1, taps):
                    total = total + weights[tap : tap + 1] * stack[slot, pl.ds(begin + tap, views)]
                out_ref[index, part] = total

    def pair(index, carry):
        step(2 * index, 0)
        step(2 * index + 1, 1)
        return carry

    lax.fori_loop(0, count // 2, pair, 0)


def interpolate_views(group, tiles, chips, view_offset, conj_offset, weights, blocks):
    places = tuple(place for _, place in blocks)
    arrays = [array for array, _ in blocks]
    count = 2 * group[1]
    views = arrays[0].shape[1] // 2
    return call(
        functools.partial(views_body, group, tiles, chips, places),
        [f32(count, 2, views, LANES)] * 2,
        [pltpu.VMEM((2, chips * 2 * views + WRAP, LANES), jnp.float32)],
        (view_offset, conj_offset, weights, *arrays),
        count * views * LANES * 32,
        count * views * LANES * 64,
    )


def ramp(lag):
    lag = lag.astype(np.float64)
    odd = np.abs(lag) % 2 == 1
    values = np.where(lag == 0, 0.25, np.where(odd, -1.0 / (math.pi**2 * np.maximum(lag * lag, 1.0)), 0.0))
    return np.where(np.abs(lag) <= KR, values, 0.0).astype(np.float32)


def filter_matrix():
    column = np.arange(WINDOW)[:, None]
    place = np.arange(2 * LANES)[None, :]
    lag = place - 2 * (column - LANES)
    even = ramp(lag)
    odd = ramp(lag - 1)[::-1]
    whole = jnp.asarray(np.concatenate([even, odd], axis=0))
    return split(whole)


def filter_body(groups, tiles, high_ref, low_ref, *refs):
    number = len(groups)
    keeps, gots = refs[:number], refs[number : 2 * number]
    out_ref, mixed, high_all, low_all = refs[2 * number :]
    views = out_ref.shape[0]
    core = lax.axis_index("ang") % 2
    for ref in (high_all, low_all):
        for part in range(2):
            ref[part, 0] = jnp.zeros(ref.shape[2:], ref.dtype)
            ref[part, tiles + 1] = jnp.zeros(ref.shape[2:], ref.dtype)
    for group, keep, got in zip(groups, keeps, gots):

        def gather(index, carry, group=group, keep=keep, got=got):
            tile = tile_of(index, group, tiles)
            for part in range(2):
                mixed[part, pl.ds(core, views, stride=2), :] = keep[index, part]
                mixed[part, pl.ds(1 - core, views, stride=2), :] = got[index, part]
                high, low = split(mixed[part])
                high_all[part, tile + 1] = high
                low_all[part, tile + 1] = low
            return carry

        lax.fori_loop(0, 2 * group[1], gather, 0, unroll=2)

    batch = 4

    def produce(index, carry):
        first = index * batch

        def window(ref):
            pieces = []
            for part in range(2):
                begin = first if part == 0 else tiles - first - batch
                for section in range(3):
                    if part == 0:
                        piece = ref[0, pl.ds(begin + section, batch)]
                    else:
                        piece = jnp.stack(
                            [ref[1, begin + section + batch - 1 - i] for i in range(batch)]
                        )
                    pieces.append(piece.reshape(batch * 2 * views, LANES))
            return jnp.concatenate(pieces, axis=1)

        high, low = window(high_all), window(low_all)
        total = dot(high, high_ref[...]) + dot(low, high_ref[...]) + dot(high, low_ref[...])
        for i in range(batch):
            block = total[2 * views * i : 2 * views * (i + 1)].reshape(views, 2, 2 * LANES)
            at = pl.multiple_of((first + i) * 2 * LANES, 2 * LANES)
            out_ref[:, :, pl.ds(at, 2 * LANES)] = block
        return carry

    lax.fori_loop(0, tiles // batch, produce, 0)


def ramp_filter(groups, tiles, keeps, gots):
    views = keeps[0].shape[2]
    high, low = filter_matrix()
    stored = pltpu.VMEM((2, tiles + 2, 2 * views, LANES), jnp.bfloat16)
    return call(
        functools.partial(filter_body, groups, tiles),
        [f32(views, 2, 2 * tiles * LANES)],
        [pltpu.VMEM((2, 2 * views, LANES), jnp.float32), stored, stored],
        (high, low, *keeps, *gots),
        6 * tiles * 2 * views * 2 * WINDOW * 2 * LANES,
        5 << 20,
    )[0]


def permuted(value, axis, target):
    count = lax.axis_size(axis)
    pairs = [(i, target(i)) for i in range(count)]
    return lax.ppermute(value, axis, [(i, j) for i, j in pairs if 0 <= j < count])


def chip_blocks(block):
    devices = lax.axis_size("ang")
    chips = devices // 2
    count = block.shape[0]
    if chips == 4:
        by_x = permuted(block, "ang", lambda i: i ^ 2)
        by_y = permuted(block, "ang", lambda i: i ^ 4)
        half = count // 2
        lower = permuted(by_x[:half], "ang", lambda i: i ^ 4)
        upper = permuted(by_y[half:], "ang", lambda i: i ^ 2)
        return [
            (block, (lambda p: p, 0, count)),
            (by_x, (lambda p: p ^ 1, 0, count)),
            (by_y, (lambda p: p ^ 2, 0, count)),
            (lower, (lambda p: p ^ 3, 0, half)),
            (upper, (lambda p: p ^ 3, half, count)),
        ]
    found = [(block, (lambda p: p, 0, count))]
    ahead = {d % chips for d in (-1, 1, chips // 2 - 1, chips // 2, chips // 2 + 1)} - {0}
    for steps in sorted(ahead):
        got = permuted(block, "ang", lambda i, steps=steps: (i - 2 * steps) % devices)
        found.append((got, (lambda p, steps=steps: lax.rem(p + steps, chips), 0, count)))
    return found


def on_device(
    sinogram, col_weights, col_start, view_offset, row_offset, conj_offset, ang_weights, row_weights
):
    tiles = col_weights.shape[0]
    chips = lax.axis_size("ang") // 2
    groups = ((0, tiles // 4), (tiles // 4, tiles // 4))
    keeps, gots = [], []
    for group in groups:
        own = resample(group, col_start, sinogram, col_weights)
        prev = permuted(own, "row", lambda i: i + 1)
        after = permuted(own, "row", lambda i: i - 1)
        keep, send = interpolate_rows(group, tiles, row_offset, prev, own, after, row_weights)
        got = permuted(send, "ang", lambda i: i ^ 1)
        block = jnp.concatenate([keep, got], axis=1)
        blocks = chip_blocks(block)
        keep, send = interpolate_views(
            group, tiles, chips, view_offset, conj_offset, ang_weights, blocks
        )
        keeps.append(keep)
        gots.append(permuted(send, "ang", lambda i: i ^ 1))
    return ramp_filter(groups, tiles, keeps, gots)


def solution(mesh):
    return jax.shard_map(
        on_device,
        mesh=mesh,
        in_specs=(P("ang", "row", None), P(), P(), P(), P(), P(), P(), P()),
        out_specs=P("ang", "row", None),
        check_vma=False,
    )
```

time: 496 us -> 84.6 us (0.17); the launches traced: 487 us -> 84.1 us
  between operations: 343 us -> 0.19 us
  local copies, waits for them, and re-layouts: 52.1 us -> 3.65 us
  matrix products: 40.2 us -> 0 us
  Pallas kernels: 0 us -> 16.2 us
  starting transfers between devices: 11.5 us -> 23.9 us
  waiting for transfers between devices: 33.4 us -> 40.1 us
  other arithmetic: 6.46 us -> 0 us
    dot_general x38 -> x0, matrix products: 40.2 us -> none  [the longest x32 25 us: resample_columns(): jnp.einsum('vrb,bc->vrc', slab, weights, precision=highest, preferred_ele...]
    rev x32 -> x0, local copies, waits for them, and re-layouts: 19 us -> none  [conjugate_views(): columns = partner[:, :, mirror:mirror + width_tile][:, :, ::-1]]
    pallas_call x0 -> x7, Pallas kernels: none -> 16.2 us  [call(): pl.pallas_call(body, out_shape=outs, in_specs=[SMEM if s else VMEM for s...]
    slice x17 -> x4, local copies, waits for them, and re-layouts: 13.1 us -> 0.07 us  [the longest x2 0.04 us: chip_blocks(): upper = permuted(by_y[half:], 'ang', lambda i: i ^ 2)]
    ppermute x7 -> x16, starting transfers between devices: 11.5 us -> 23.9 us  [permuted(): lax.ppermute(value, axis, [(i, j) for i, j in pairs if 0 <= j < count])]
    ppermute x7 -> x16, waiting for transfers between devices: 33.4 us -> 40.1 us  [permuted(): lax.ppermute(value, axis, [(i, j) for i, j in pairs if 0 <= j < count])]
    unnamed x57 -> x22, local copies, waits for them, and re-layouts: 9.65 us -> 3.54 us
    reshape x3 -> x0, local copies, waits for them, and re-layouts: 5.16 us -> none  [the longest x1 3.59 us: ramp_filter(): return total.reshape(parallel.shape[0], parallel.shape[1], -1)]
  transfers between devices with their start and end apart: 7 -> 16, of which waited for: 2 -> 11; matrix products, arithmetic and copies ran while one was open for 3% -> 0% of each run, Pallas kernels for 0% -> 9%
where the time goes in v1:
time: 84.6 us; the launch traced here: 84.1 us
  waiting for transfers between devices  40.1 us (47%)
  starting transfers between devices  23.9 us (28%)
  Pallas kernels  16.2 us (19%)
  local copies, waits for them, and re-layouts  3.65 us (4%)
    ppermute x16, waiting for transfers between devices, permuted(): lax.ppermute(value, axis, [(i, j) for i, j in pairs if 0 <= j < count])  40.1 us
    ppermute x16, starting transfers between devices, permuted(): lax.ppermute(value, axis, [(i, j) for i, j in pairs if 0 <= j < count])  23.9 us
    pallas_call x7, Pallas kernels, call(): pl.pallas_call(body, out_shape=outs, in_specs=[SMEM if s else VMEM for s...  16.2 us
    unnamed x22, local copies, waits for them, and re-layouts  3.54 us
  transfers between devices with their start and end apart: 16, of which 11 were waited for; matrix products, arithmetic and copies ran while one was open for 0% of the time, Pallas kernels for 9%

profile of v1, /device:TPU:11, one launch (start us, length us, event | category | flops | bytes accessed | tf_op | source)
XLA Modules:
  0.0 84.1 jit_solution(2546403518225400642)
XLA Ops:
  0.0 1.6 %copy-done = bf16[32,256,128]{2,1,0:T(8,128)(2,1)S(1)} copy-done((bf16[32,256,128]{2,1,0:T(8,128)(2,1)S(1)}, bf16[32,256,128]{2,1,0:T(8,128)(2,1)}, u32[]{:S(2)}) %copy-start) | copy-done | bytes 2097176
  1.6 1.2 %copy-done.1 = f32[32,2,4096]{2,1,0:T(2,128)S(1)} copy-done((f32[32,2,4096]{2,1,0:T(2,128)S(1)}, f32[32,2,4096]{2,1,0:T(2,128)}, u32[]{:S(2)}) %copy-start.1) | copy-done | bytes 1048600
  3.5 2.7 %shard_map.91.own_ref = f32[16,64,128]{2,1,0:T(8,128)S(1)} custom-call(s32[32]{0:T(128)S(1)} %copy-done.7, f32[32,2,4096]{2,1,0:T(2,128)S(1)} %copy-done.1, bf16[32,256,128]{2,1,0:T(8,128)(2,1)S(1)} %copy-done), custom_call_target="tpu_custom_call" | custom-call | flops 134217728 | bytes 6291456 | tf_op jit(solution)/shard_map/pallas_call | solution.py:23
  6.2 2.1 %collective-permute-start.1 = (f32[16,64,128]{2,1,0:T(8,128)S(1)}, f32[16,64,128]{2,1,0:T(8,128)S(1)}, u32[]{:S(2)}, u32[]{:S(2)}) collective-permute-start(f32[16,64,128]{2,1,0:T(8,128)S(1)} %shard_map.91.own_ref), channel_id=1, source_target_pairs={{1,0},{2,1},{3,2},{5,4},{6,5},{7,6},{9,8},{10,9},{11,10},{13,12},{... | collective-permute-start | bytes 1572872 | tf_op jit(solution)/shard_map/ppermute | solution.py:278
  8.3 3.2 %collective-permute-start = (f32[16,64,128]{2,1,0:T(8,128)S(1)}, f32[16,64,128]{2,1,0:T(8,128)S(1)}, u32[]{:S(2)}, u32[]{:S(2)}) collective-permute-start(f32[16,64,128]{2,1,0:T(8,128)S(1)} %shard_map.91.own_ref), channel_id=1, source_target_pairs={{0,1},{1,2},{2,3},{4,5},{5,6},{6,7},{8,9},{9,10},{10,11},{12,13},{... | collective-permute-start | bytes 1572872 | tf_op jit(solution)/shard_map/ppermute | solution.py:278
  11.5 2.7 %shard_map.94.own_ref = f32[16,64,128]{2,1,0:T(8,128)S(1)} custom-call(s32[32]{0:T(128)S(1)} %copy-done.7, f32[32,2,4096]{2,1,0:T(2,128)S(1)} %copy-done.1, bf16[32,256,128]{2,1,0:T(8,128)(2,1)S(1)} %copy-done), custom_call_target="tpu_custom_call" | custom-call | flops 134217728 | bytes 6291456 | tf_op jit(solution)/shard_map/pallas_call | solution.py:23
  14.2 2.1 %collective-permute-start.8 = (f32[16,64,128]{2,1,0:T(8,128)S(1)}, f32[16,64,128]{2,1,0:T(8,128)S(1)}, u32[]{:S(2)}, u32[]{:S(2)}) collective-permute-start(f32[16,64,128]{2,1,0:T(8,128)S(1)} %shard_map.94.own_ref), channel_id=1, source_target_pairs={{1,0},{2,1},{3,2},{5,4},{6,5},{7,6},{9,8},{10,9},{11,10},{13,12},{... | collective-permute-start | bytes 1572872 | tf_op jit(solution)/shard_map/ppermute | solution.py:278
  16.4 3.2 %collective-permute-start.7 = (f32[16,64,128]{2,1,0:T(8,128)S(1)}, f32[16,64,128]{2,1,0:T(8,128)S(1)}, u32[]{:S(2)}, u32[]{:S(2)}) collective-permute-start(f32[16,64,128]{2,1,0:T(8,128)S(1)} %shard_map.94.own_ref), channel_id=1, source_target_pairs={{0,1},{1,2},{2,3},{4,5},{5,6},{6,7},{8,9},{9,10},{10,11},{12,13},{... | collective-permute-start | bytes 1572872 | tf_op jit(solution)/shard_map/ppermute | solution.py:278
  19.5 1.4 %collective-permute-done.1.next_ref = f32[16,64,128]{2,1,0:T(8,128)S(1)} collective-permute-done((f32[16,64,128]{2,1,0:T(8,128)S(1)}, f32[16,64,128]{2,1,0:T(8,128)S(1)}, u32[]{:S(2)}, u32[]{:S(2)}) %collective-permute-start.1) | collective-permute-done | bytes 524320 | tf_op jit(solution)/shard_map/ppermute | solution.py:278
  20.9 1.8 %collective-permute-done.prev_ref = f32[16,64,128]{2,1,0:T(8,128)S(1)} collective-permute-done((f32[16,64,128]{2,1,0:T(8,128)S(1)}, f32[16,64,128]{2,1,0:T(8,128)S(1)}, u32[]{:S(2)}, u32[]{:S(2)}) %collective-permute-start) | collective-permute-done | bytes 524320 | tf_op jit(solution)/shard_map/ppermute | solution.py:278
  23.7 3.4 %collective-permute-start.2 = (f32[16,32,128]{2,1,0:T(8,128)S(1)}, f32[16,32,128]{2,1,0:T(8,128)S(1)}, u32[]{:S(2)}, u32[]{:S(2)}) collective-permute-start(f32[16,32,128]{2,1,0:T(8,128)S(1)} %get-tuple-element.14), channel_id=1, source_target_pairs={{0,4},{4,0},{8,12},{12,8},{16,20},{20,16},{24,28},{28,24},{1,5},{5... | collective-permute-start | bytes 786440 | tf_op jit(solution)/shard_map/ppermute | solution.py:278
  27.2 5.0 %collective-permute-done.8.next_ref = f32[16,64,128]{2,1,0:T(8,128)S(1)} collective-permute-done((f32[16,64,128]{2,1,0:T(8,128)S(1)}, f32[16,64,128]{2,1,0:T(8,128)S(1)}, u32[]{:S(2)}, u32[]{:S(2)}) %collective-permute-start.8) | collective-permute-done | bytes 524320 | tf_op jit(solution)/shard_map/ppermute | solution.py:278
  32.1 1.8 %collective-permute-done.7.prev_ref = f32[16,64,128]{2,1,0:T(8,128)S(1)} collective-permute-done((f32[16,64,128]{2,1,0:T(8,128)S(1)}, f32[16,64,128]{2,1,0:T(8,128)S(1)}, u32[]{:S(2)}, u32[]{:S(2)}) %collective-permute-start.7) | collective-permute-done | bytes 524320 | tf_op jit(solution)/shard_map/ppermute | solution.py:278
  35.0 1.9 %collective-permute-start.9 = (f32[16,32,128]{2,1,0:T(8,128)S(1)}, f32[16,32,128]{2,1,0:T(8,128)S(1)}, u32[]{:S(2)}, u32[]{:S(2)}) collective-permute-start(f32[16,32,128]{2,1,0:T(8,128)S(1)} %get-tuple-element.17), channel_id=1, source_target_pairs={{0,4},{4,0},{8,12},{12,8},{16,20},{20,16},{24,28},{28,24},{1,5},{5... | collective-permute-start | bytes 786440 | tf_op jit(solution)/shard_map/ppermute | solution.py:278
  37.0 1.3 %collective-permute-start.4 = (f32[16,64,128]{2,1,0:T(8,128)S(1)}, f32[16,64,128]{2,1,0:T(8,128)S(1)}, u32[]{:S(2)}, u32[]{:S(2)}) collective-permute-start(f32[16,64,128]{2,1,0:T(8,128)S(1)} %constant_dynamic-update-slice_fusion.refs_0_), channel_id=1, source_target_pairs={{0,16},{4,20},{8,24},{12,28},{16,0},{20,4},{24,8},{28,12},{1,17},{... | collective-permute-start | bytes 1572872 | tf_op jit(solution)/shard_map/ppermute | solution.py:278
  40.1 10.5 %collective-permute-done.4.refs_2_ = f32[16,64,128]{2,1,0:T(8,128)S(1)} collective-permute-done((f32[16,64,128]{2,1,0:T(8,128)S(1)}, f32[16,64,128]{2,1,0:T(8,128)S(1)}, u32[]{:S(2)}, u32[]{:S(2)}) %collective-permute-start.4) | collective-permute-done | bytes 524320 | tf_op jit(solution)/shard_map/ppermute | solution.py:278
  52.2 9.6 %collective-permute-done.11.refs_2_ = f32[16,64,128]{2,1,0:T(8,128)S(1)} collective-permute-done((f32[16,64,128]{2,1,0:T(8,128)S(1)}, f32[16,64,128]{2,1,0:T(8,128)S(1)}, u32[]{:S(2)}, u32[]{:S(2)}) %collective-permute-start.11) | collective-permute-done | bytes 524320 | tf_op jit(solution)/shard_map/ppermute | solution.py:278
  63.5 4.8 %collective-permute-done.6.refs_4_ = f32[8,64,128]{2,1,0:T(8,128)S(1)} collective-permute-done((f32[8,64,128]{2,1,0:T(8,128)S(1)}, f32[8,64,128]{2,1,0:T(8,128)S(1)}, u32[]{:S(2)}, u32[]{:S(2)}) %collective-permute-start.6) | collective-permute-done | bytes 262176 | tf_op jit(solution)/shard_map/ppermute | solution.py:278
  68.4 1.3 %shard_map.93 = (f32[16,2,32,128]{3,2,1,0:T(8,128)S(1)}, f32[16,2,32,128]{3,2,1,0:T(8,128)S(1)}) custom-call(s32[32]{0:T(128)S(1)} %copy-done.5, s32[32]{0:T(128)S(1)} %copy-done.6, f32[4,4096]{1,0:T(4,128)S(1)} %copy-done.2, f32[16,64,128]{2,1,0:T(8,128)S(1)} %constant_dynamic-update-slice_fusion.refs_0_, ...), custom_call_target="tpu_custom_call" | custom-call | flops 2097152 | bytes 4194304 | tf_op jit(solution)/shard_map/pallas_call | solution.py:23
  69.7 2.0 %collective-permute-start.14 = (f32[16,2,32,128]{3,2,1,0:T(8,128)S(1)}, f32[16,2,32,128]{3,2,1,0:T(8,128)S(1)}, u32[]{:S(2)}, u32[]{:S(2)}) collective-permute-start(f32[16,2,32,128]{3,2,1,0:T(8,128)S(1)} %get-tuple-element.19), channel_id=1, source_target_pairs={{0,4},{4,0},{8,12},{12,8},{16,20},{20,16},{24,28},{28,24},{1,5},{5... | collective-permute-start | bytes 1572872 | tf_op jit(solution)/shard_map/ppermute | solution.py:278
  71.7 2.3 %collective-permute-done.13.refs_4_ = f32[8,64,128]{2,1,0:T(8,128)S(1)} collective-permute-done((f32[8,64,128]{2,1,0:T(8,128)S(1)}, f32[8,64,128]{2,1,0:T(8,128)S(1)}, u32[]{:S(2)}, u32[]{:S(2)}) %collective-permute-start.13) | collective-permute-done | bytes 262176 | tf_op jit(solution)/shard_map/ppermute | solution.py:278
  74.0 1.3 %shard_map.96 = (f32[16,2,32,128]{3,2,1,0:T(8,128)S(1)}, f32[16,2,32,128]{3,2,1,0:T(8,128)S(1)}) custom-call(s32[32]{0:T(128)S(1)} %copy-done.5, s32[32]{0:T(128)S(1)} %copy-done.6, f32[4,4096]{1,0:T(4,128)S(1)} %copy-done.2, f32[16,64,128]{2,1,0:T(8,128)S(1)} %constant_dynamic-update-slice_fusion.2.refs_0_, ...), custom_call_target="tpu_custom_call" | custom-call | flops 2097152 | bytes 4194304 | tf_op jit(solution)/shard_map/pallas_call | solution.py:23
  76.5 1.5 %collective-permute-done.15.refs_3_ = f32[16,2,32,128]{3,2,1,0:T(8,128)S(1)} collective-permute-done((f32[16,2,32,128]{3,2,1,0:T(8,128)S(1)}, f32[16,2,32,128]{3,2,1,0:T(8,128)S(1)}, u32[]{:S(2)}, u32[]{:S(2)}) %collective-permute-start.15) | collective-permute-done | bytes 524320 | tf_op jit(solution)/shard_map/ppermute | solution.py:278
  78.0 6.1 %shard_map.97 = f32[32,2,8192]{2,1,0:T(2,128)} custom-call(bf16[768,256]{1,0:T(8,128)(2,1)S(1)} %copy-done.9, bf16[768,256]{1,0:T(8,128)(2,1)S(1)} %copy-done.8, f32[16,2,32,128]{3,2,1,0:T(8,128)S(1)} %get-tuple-element.15.refs_0_, f32[16,2,32,128]{3,2,1,0:T(8,128)S(1)} %get-tuple-element.18.refs_1_, f32[16,2,32,128]{3,2,1,0:T(8,128)S(1)} %collective-permute-done.14.refs_2_, ...), custom_call_target="tpu_custom_call" | custom-call | flops 2415919104 | bytes 5242880 | tf_op jit(solution)/shard_map/pallas_call | solution.py:23
  (43 shorter events, 9.2 us)
Async XLA Ops:
  0.0 1.6 %copy-start = (bf16[32,256,128]{2,1,0:T(8,128)(2,1)S(1)}, bf16[32,256,128]{2,1,0:T(8,128)(2,1)}, u32[]{:S(2)}) copy-start(bf16[32,256,128]{2,1,0:T(8,128)(2,1)} %weights_ref.9) | copy-start | bytes 6291460
  6.2 16.5 %copy-start.3 = (f32[2,4096]{1,0:T(2,128)S(1)}, f32[2,4096]{1,0:T(2,128)}, u32[]{:S(2)}) copy-start(f32[2,4096]{1,0:T(2,128)} %weights_ref.10) | copy-start | bytes 98308
  6.2 16.5 %copy-start.4 = (s32[32]{0:T(128)S(1)}, s32[32]{0:T(128)}, u32[]{:S(2)}) copy-start(s32[32]{0:T(128)} %offset_ref.3) | copy-start | bytes 388
  6.2 14.7 %collective-permute-start.1 = (f32[16,64,128]{2,1,0:T(8,128)S(1)}, f32[16,64,128]{2,1,0:T(8,128)S(1)}, u32[]{:S(2)}, u32[]{:S(2)}) collective-permute-start(f32[16,64,128]{2,1,0:T(8,128)S(1)} %shard_map.91.own_ref), channel_id=1, source_target_pairs={{1,0},{2,1},{3,2},{5,4},{6,5},{7,6},{9,8},{10,9},{11,10},{13,12},{... | collective-permute-start | bytes 1572872 | tf_op jit(solution)/shard_map/ppermute | solution.py:278
  8.3 14.4 %collective-permute-start = (f32[16,64,128]{2,1,0:T(8,128)S(1)}, f32[16,64,128]{2,1,0:T(8,128)S(1)}, u32[]{:S(2)}, u32[]{:S(2)}) collective-permute-start(f32[16,64,128]{2,1,0:T(8,128)S(1)} %shard_map.91.own_ref), channel_id=1, source_target_pairs={{0,1},{1,2},{2,3},{4,5},{5,6},{6,7},{8,9},{9,10},{10,11},{12,13},{... | collective-permute-start | bytes 1572872 | tf_op jit(solution)/shard_map/ppermute | solution.py:278
  14.2 17.9 %collective-permute-start.8 = (f32[16,64,128]{2,1,0:T(8,128)S(1)}, f32[16,64,128]{2,1,0:T(8,128)S(1)}, u32[]{:S(2)}, u32[]{:S(2)}) collective-permute-start(f32[16,64,128]{2,1,0:T(8,128)S(1)} %shard_map.94.own_ref), channel_id=1, source_target_pairs={{1,0},{2,1},{3,2},{5,4},{6,5},{7,6},{9,8},{10,9},{11,10},{13,12},{... | collective-permute-start | bytes 1572872 | tf_op jit(solution)/shard_map/ppermute | solution.py:278
  16.4 17.6 %collective-permute-start.7 = (f32[16,64,128]{2,1,0:T(8,128)S(1)}, f32[16,64,128]{2,1,0:T(8,128)S(1)}, u32[]{:S(2)}, u32[]{:S(2)}) collective-permute-start(f32[16,64,128]{2,1,0:T(8,128)S(1)} %shard_map.94.own_ref), channel_id=1, source_target_pairs={{0,1},{1,2},{2,3},{4,5},{5,6},{6,7},{8,9},{9,10},{10,11},{12,13},{... | collective-permute-start | bytes 1572872 | tf_op jit(solution)/shard_map/ppermute | solution.py:278
  23.7 13.2 %collective-permute-start.2 = (f32[16,32,128]{2,1,0:T(8,128)S(1)}, f32[16,32,128]{2,1,0:T(8,128)S(1)}, u32[]{:S(2)}, u32[]{:S(2)}) collective-permute-start(f32[16,32,128]{2,1,0:T(8,128)S(1)} %get-tuple-element.14), channel_id=1, source_target_pairs={{0,4},{4,0},{8,12},{12,8},{16,20},{20,16},{24,28},{28,24},{1,5},{5... | collective-permute-start | bytes 786440 | tf_op jit(solution)/shard_map/ppermute | solution.py:278
  35.0 3.6 %collective-permute-start.9 = (f32[16,32,128]{2,1,0:T(8,128)S(1)}, f32[16,32,128]{2,1,0:T(8,128)S(1)}, u32[]{:S(2)}, u32[]{:S(2)}) collective-permute-start(f32[16,32,128]{2,1,0:T(8,128)S(1)} %get-tuple-element.17), channel_id=1, source_target_pairs={{0,4},{4,0},{8,12},{12,8},{16,20},{20,16},{24,28},{28,24},{1,5},{5... | collective-permute-start | bytes 786440 | tf_op jit(solution)/shard_map/ppermute | solution.py:278
  36.9 31.4 %copy-start.2 = (f32[4,4096]{1,0:T(4,128)S(1)}, f32[4,4096]{1,0:T(4,128)}, u32[]{:S(2)}) copy-start(f32[4,4096]{1,0:T(4,128)} %weights_ref.11) | copy-start | bytes 196612
  36.9 31.4 %copy-start.5 = (s32[32]{0:T(128)S(1)}, s32[32]{0:T(128)}, u32[]{:S(2)}) copy-start(s32[32]{0:T(128)} %view_ref.3) | copy-start | bytes 388
  36.9 31.4 %copy-start.6 = (s32[32]{0:T(128)S(1)}, s32[32]{0:T(128)}, u32[]{:S(2)}) copy-start(s32[32]{0:T(128)} %conj_ref.3) | copy-start | bytes 388
  37.0 13.6 %collective-permute-start.4 = (f32[16,64,128]{2,1,0:T(8,128)S(1)}, f32[16,64,128]{2,1,0:T(8,128)S(1)}, u32[]{:S(2)}, u32[]{:S(2)}) collective-permute-start(f32[16,64,128]{2,1,0:T(8,128)S(1)} %constant_dynamic-update-slice_fusion.refs_0_), channel_id=1, source_target_pairs={{0,16},{4,20},{8,24},{12,28},{16,0},{20,4},{24,8},{28,12},{1,17},{... | collective-permute-start | bytes 1572872 | tf_op jit(solution)/shard_map/ppermute | solution.py:278
  38.3 13.2 %collective-permute-start.3 = (f32[16,64,128]{2,1,0:T(8,128)S(1)}, f32[16,64,128]{2,1,0:T(8,128)S(1)}, u32[]{:S(2)}, u32[]{:S(2)}) collective-permute-start(f32[16,64,128]{2,1,0:T(8,128)S(1)} %constant_dynamic-update-slice_fusion.refs_0_), channel_id=1, source_target_pairs={{0,8},{4,12},{8,0},{12,4},{16,24},{20,28},{24,16},{28,20},{1,9},{5... | collective-permute-start | bytes 1572872 | tf_op jit(solution)/shard_map/ppermute | solution.py:278
  38.6 23.2 %collective-permute-start.11 = (f32[16,64,128]{2,1,0:T(8,128)S(1)}, f32[16,64,128]{2,1,0:T(8,128)S(1)}, u32[]{:S(2)}, u32[]{:S(2)}) collective-permute-start(f32[16,64,128]{2,1,0:T(8,128)S(1)} %constant_dynamic-update-slice_fusion.2.refs_0_), channel_id=1, source_target_pairs={{0,16},{4,20},{8,24},{12,28},{16,0},{20,4},{24,8},{28,12},{1,17},{... | collective-permute-start | bytes 1572872 | tf_op jit(solution)/shard_map/ppermute | solution.py:278
  39.4 23.3 %collective-permute-start.10 = (f32[16,64,128]{2,1,0:T(8,128)S(1)}, f32[16,64,128]{2,1,0:T(8,128)S(1)}, u32[]{:S(2)}, u32[]{:S(2)}) collective-permute-start(f32[16,64,128]{2,1,0:T(8,128)S(1)} %constant_dynamic-update-slice_fusion.2.refs_0_), channel_id=1, source_target_pairs={{0,8},{4,12},{8,0},{12,4},{16,24},{20,28},{24,16},{28,20},{1,9},{5... | collective-permute-start | bytes 1572872 | tf_op jit(solution)/shard_map/ppermute | solution.py:278
  50.6 17.8 %collective-permute-start.6 = (f32[8,64,128]{2,1,0:T(8,128)S(1)}, f32[8,64,128]{2,1,0:T(8,128)S(1)}, u32[]{:S(2)}, u32[]{:S(2)}) collective-permute-start(f32[8,64,128]{2,1,0:T(8,128)S(1)} %slice.17), channel_id=1, source_target_pairs={{0,8},{4,12},{8,0},{12,4},{16,24},{20,28},{24,16},{28,20},{1,9},{5... | collective-permute-start | bytes 786440 | tf_op jit(solution)/shard_map/ppermute | solution.py:278
  51.5 16.8 %collective-permute-start.5 = (f32[8,64,128]{2,1,0:T(8,128)S(1)}, f32[8,64,128]{2,1,0:T(8,128)S(1)}, u32[]{:S(2)}, u32[]{:S(2)}) collective-permute-start(f32[8,64,128]{2,1,0:T(8,128)S(1)} %slice.16), channel_id=1, source_target_pairs={{0,16},{4,20},{8,24},{12,28},{16,0},{20,4},{24,8},{28,12},{1,17},{... | collective-permute-start | bytes 786440 | tf_op jit(solution)/shard_map/ppermute | solution.py:278
  61.8 12.1 %collective-permute-start.13 = (f32[8,64,128]{2,1,0:T(8,128)S(1)}, f32[8,64,128]{2,1,0:T(8,128)S(1)}, u32[]{:S(2)}, u32[]{:S(2)}) collective-permute-start(f32[8,64,128]{2,1,0:T(8,128)S(1)} %slice.19), channel_id=1, source_target_pairs={{0,8},{4,12},{8,0},{12,4},{16,24},{20,28},{24,16},{28,20},{1,9},{5... | collective-permute-start | bytes 786440 | tf_op jit(solution)/shard_map/ppermute | solution.py:278
  62.7 15.3 %copy-start.8 = (bf16[768,256]{1,0:T(8,128)(2,1)S(1)}, bf16[768,256]{1,0:T(8,128)(2,1)}, u32[]{:S(2)}) copy-start(bf16[768,256]{1,0:T(8,128)(2,1)} %constant.7.low_ref) | copy-start | bytes 1179652
  62.8 15.3 %copy-start.9 = (bf16[768,256]{1,0:T(8,128)(2,1)S(1)}, bf16[768,256]{1,0:T(8,128)(2,1)}, u32[]{:S(2)}) copy-start(bf16[768,256]{1,0:T(8,128)(2,1)} %constant.4.high_ref) | copy-start | bytes 1179652
  62.8 11.2 %collective-permute-start.12 = (f32[8,64,128]{2,1,0:T(8,128)S(1)}, f32[8,64,128]{2,1,0:T(8,128)S(1)}, u32[]{:S(2)}, u32[]{:S(2)}) collective-permute-start(f32[8,64,128]{2,1,0:T(8,128)S(1)} %slice.18), channel_id=1, source_target_pairs={{0,16},{4,20},{8,24},{12,28},{16,0},{20,4},{24,8},{28,12},{1,17},{... | collective-permute-start | bytes 786440 | tf_op jit(solution)/shard_map/ppermute | solution.py:278
  69.7 6.8 %collective-permute-start.14 = (f32[16,2,32,128]{3,2,1,0:T(8,128)S(1)}, f32[16,2,32,128]{3,2,1,0:T(8,128)S(1)}, u32[]{:S(2)}, u32[]{:S(2)}) collective-permute-start(f32[16,2,32,128]{3,2,1,0:T(8,128)S(1)} %get-tuple-element.19), channel_id=1, source_target_pairs={{0,4},{4,0},{8,12},{12,8},{16,20},{20,16},{24,28},{28,24},{1,5},{5... | collective-permute-start | bytes 1572872 | tf_op jit(solution)/shard_map/ppermute | solution.py:278
  75.3 2.8 %collective-permute-start.15 = (f32[16,2,32,128]{3,2,1,0:T(8,128)S(1)}, f32[16,2,32,128]{3,2,1,0:T(8,128)S(1)}, u32[]{:S(2)}, u32[]{:S(2)}) collective-permute-start(f32[16,2,32,128]{3,2,1,0:T(8,128)S(1)} %get-tuple-element.20), channel_id=1, source_target_pairs={{0,4},{4,0},{8,12},{12,8},{16,20},{20,16},{24,28},{28,24},{1,5},{5... | collective-permute-start | bytes 1572872 | tf_op jit(solution)/shard_map/ppermute | solution.py:278
  (2 other events, 1.9 us)

commit v2 on v1

--- a/solution.py
+++ b/solution.py
@@ -12,7 +12,6 @@
 KR = 256
 LANES = 128
 WINDOW = 3 * LANES
-WRAP = 72
 VMEM = pl.BlockSpec(memory_space=pltpu.VMEM)
 SMEM = pl.BlockSpec(memory_space=pltpu.SMEM)
 PARAMS = pltpu.CompilerParams(vmem_limit_bytes=48 * 1024 * 1024)
@@ -105,7 +104,11 @@
         for out_ref, row in ((keep_ref, core), (send_ref, 1 - core)):
             lower = picked(row + offset)
             upper = picked(row + offset + 1)
-            out_ref[index] = weights[0:1] * lower + weights[1:2] * upper
+            mixed = weights[0:1] * lower + weights[1:2] * upper
+            if out_ref is send_ref:
+                out_ref[index] = mixed
+            else:
+                out_ref[index, pl.ds(pl.multiple_of(core * views, 8), views)] = mixed
 
     def pair(index, carry):
         step(2 * index, 0)
@@ -119,7 +122,7 @@
     count, height, _ = own.shape
     return call(
         functools.partial(rows_body, group, tiles),
-        [f32(count, height // 2, LANES)] * 2,
+        [f32(count, height, LANES), f32(count, height // 2, LANES)],
         [pltpu.VMEM((2, 3 * height, LANES), jnp.float32)],
         (offset, prev, own, after, weights),
         count * height * LANES * 4,
@@ -127,61 +130,149 @@
     )
 
 
-def views_body(group, tiles, chips, places, view_ref, conj_ref, weights_ref, *refs):
-    blocks = refs[: len(places)]
-    keep_ref, send_ref, stack = refs[len(places) :]
-    count, chip_views = keep_ref.shape[0], 2 * keep_ref.shape[2]
-    views = chip_views // 2
-    turn = chips * chip_views
+def select_body(group, tiles, view_ref, conj_ref, own_ref, by_y_ref, by_x_ref, for_x_ref, for_y_ref, stack):
+    half = group[1]
+    chip_views = own_ref.shape[1]
+    side = lax.axis_index("ang") // 2 % 2
+    lanes = own_ref.shape[2]
+
+    def shifts(index):
+        tile = tile_of(index, group, tiles)
+        shift = view_ref[tile]
+        return shift, shift + conj_ref[tiles - 1 - tile]
+
+    def slots(low, high):
+        return low + lax.broadcasted_iota(jnp.int32, (high - low, lanes), 0)
+
+    def across_x(index, slot):
+        shift, opposite = shifts(index)
+        own_at = pl.multiple_of((1 - side) * chip_views, 8)
+        got_at = pl.multiple_of(side * chip_views, 8)
+        stack[slot, pl.ds(own_at, chip_views)] = own_ref[index]
+        stack[slot, pl.ds(got_at, chip_views)] = by_y_ref[index]
+        near, far = stack.at[slot, 0:64], stack.at[slot, 64:128]
+        for_x_ref[index, 0:32] = jnp.where(slots(0, 32) >= shift + 32, far[32:64], near[0:32])
+        for_x_ref[index, 32:80] = jnp.where(slots(0, 48) >= opposite + 48, near[16:64], far[0:48])
+
+    def across_y_first(index, slot):
+        shift, opposite = shifts(half + index)
+        stack[slot, 0:64] = own_ref[half + index]
+        stack[slot, 64:128] = by_x_ref[index]
+        both = stack.at[slot]
+        for_y_ref[index, 0:40] = jnp.where(slots(0, 40) >= opposite, both[0:40], both[72:112])
+        for_y_ref[index, 40:56] = both[40:56]
+        for_y_ref[index, 56:72] = jnp.where(slots(56, 72) >= 88 + shift, both[96:112], both[56:72])
+        for_y_ref[index, 72:88] = both[112:128]
+
+    def across_y_last(index, slot):
+        shift, opposite = shifts(half + index)
+        stack[slot, 0:64] = by_x_ref[index]
+        stack[slot, 64:128] = own_ref[half + index]
+        both = stack.at[slot]
+        for_y_ref[index, 0:16] = both[0:16]
+        for_y_ref[index, 16:32] = jnp.where(slots(16, 32) < shift + 3, both[16:32], both[56:72])
+        for_y_ref[index, 32:48] = both[72:88]
+        for_y_ref[index, 48:88] = jnp.where(slots(48, 88) < 91 + opposite, both[88:128], both[16:56])
+
+    paired(across_x, half)
+    pl.when(side == 0)(lambda: paired(across_y_first, half))
+    pl.when(side == 1)(lambda: paired(across_y_last, half))
+
+
+def paired(step, count):
+    def pair(index, carry):
+        step(2 * index, 0)
+        step(2 * index + 1, 1)
+        return carry
+
+    lax.fori_loop(0, count // 2, pair, 0)
+
+
+def select_views(group, tiles, view_offset, conj_offset, own, by_y, by_x):
+    half = group[1]
+    return call(
+        functools.partial(select_body, group, tiles),
+        [f32(half, 80, LANES), f32(half, 88, LANES)],
+        [pltpu.VMEM((2, 128, LANES), jnp.float32)],
+        (view_offset, conj_offset, own, by_y, by_x),
+        half * LANES * 1000,
+        half * LANES * 2000,
+    )
+
+
+def views_body(group, tiles, exchanged, view_ref, conj_ref, weights_ref, *refs):
+    *blocks, keep_ref, send_ref, stack = refs
+    half = group[1]
+    views = keep_ref.shape[2]
     index_ang = lax.axis_index("ang")
-    chip, core = index_ang // 2, index_ang % 2
+    side, core = index_ang // 2 % 2, index_ang % 2
     taps = weights_ref.shape[0]
 
-    def step(index, slot):
+    def interpolate(index, slot):
         tile = tile_of(index, group, tiles)
-        for ref, (place, low, high) in zip(blocks, places):
-
-            def put(ref=ref, place=place, low=low):
-                at = place(chip) * chip_views
-                mine = pl.multiple_of(at + core * views, 8)
-                other = pl.multiple_of(at + (1 - core) * views, 8)
-                stack[slot, pl.ds(mine, views)] = ref[index - low, 0:views]
-                stack[slot, pl.ds(other, views)] = ref[index - low, views:chip_views]
-
-            if low == 0 and high == count:
-                put()
-            else:
-                pl.when((index >= low) & (index < high))(put)
-        stack[slot, turn : turn + WRAP] = stack[slot, 0:WRAP]
         weights = weights_ref[:, pl.ds(pl.multiple_of(tile * LANES, LANES), LANES)]
         shift = view_ref[tile]
-        opposite = shift + conj_ref[tiles - 1 - tile] + turn // 2
-        for part, by in ((0, shift), (1, opposite)):
+        opposite = shift + conj_ref[tiles - 1 - tile]
+        for part, by in ((0, 32 + shift), (1, 176 + opposite)):
             for out_ref, first in ((keep_ref, core), (send_ref, 1 - core)):
-                begin = lax.rem(chip * chip_views + first * views + by + turn, turn)
+                begin = by + first * views
                 total = weights[0:1] * stack[slot, pl.ds(begin, views)]
                 for tap in range(1, taps):
                     total = total + weights[tap : tap + 1] * stack[slot, pl.ds(begin + tap, views)]
                 out_ref[index, part] = total
 
-    def pair(index, carry):
-        step(2 * index, 0)
-        step(2 * index + 1, 1)
-        return carry
-
-    lax.fori_loop(0, count // 2, pair, 0)
-
-
-def interpolate_views(group, tiles, chips, view_offset, conj_offset, weights, blocks):
-    places = tuple(place for _, place in blocks)
-    arrays = [array for array, _ in blocks]
+    def filled(slot, *parts):
+        at = 0
+        for part in parts:
+            stack[slot, at : at + part.shape[0]] = part[...]
+            at += part.shape[0]
+
+    if not exchanged:
+        own, before, after, early, middle, late = blocks
+
+        def whole(index, slot):
+            parts = (before, own, after, early, middle, late)
+            filled(slot, *(ref.at[index] for ref in parts))
+            interpolate(index, slot)
+
+        paired(whole, 2 * half)
+        return
+    own, by_y, by_x, from_x, from_y = blocks
+
+    def first_half(index, slot):
+        near, far = from_x.at[index, 0:32], from_x.at[index, 32:80]
+        filled(slot, near, own.at[index], near, far, by_y.at[index], far)
+        interpolate(index, slot)
+
+    def last_half_first(index, slot):
+        got = from_y.at[index]
+        beside = by_x.at[index]
+        filled(
+            slot, got.at[56:88], own.at[half + index], beside.at[0:32], beside.at[16:64], got.at[0:72], got.at[0:40]
+        )
+        interpolate(half + index, slot)
+
+    def last_half_last(index, slot):
+        got = from_y.at[index]
+        beside = by_x.at[index]
+        filled(
+            slot, beside.at[32:64], own.at[half + index], got.at[0:32], got.at[48:88], got.at[16:88], beside.at[0:48]
+        )
+        interpolate(half + index, slot)
+
+    paired(first_half, half)
+    pl.when(side == 0)(lambda: paired(last_half_first, half))
+    pl.when(side == 1)(lambda: paired(last_half_last, half))
+
+
+def interpolate_views(group, tiles, exchanged, view_offset, conj_offset, weights, blocks):
     count = 2 * group[1]
-    views = arrays[0].shape[1] // 2
+    views = blocks[0].shape[1] // 2
     return call(
-        functools.partial(views_body, group, tiles, chips, places),
+        functools.partial(views_body, group, tiles, exchanged),
         [f32(count, 2, views, LANES)] * 2,
-        [pltpu.VMEM((2, chips * 2 * views + WRAP, LANES), jnp.float32)],
-        (view_offset, conj_offset, weights, *arrays),
+        [pltpu.VMEM((2, 288, LANES), jnp.float32)],
+        (view_offset, conj_offset, weights, *blocks),
         count * views * LANES * 32,
         count * views * LANES * 64,
     )
@@ -278,48 +369,58 @@
     return lax.ppermute(value, axis, [(i, j) for i, j in pairs if 0 <= j < count])
 
 
-def chip_blocks(block):
+def exchanged_blocks(group, tiles, view_offset, conj_offset, own):
     devices = lax.axis_size("ang")
-    chips = devices // 2
-    count = block.shape[0]
-    if chips == 4:
-        by_x = permuted(block, "ang", lambda i: i ^ 2)
-        by_y = permuted(block, "ang", lambda i: i ^ 4)
-        half = count // 2
-        lower = permuted(by_x[:half], "ang", lambda i: i ^ 4)
-        upper = permuted(by_y[half:], "ang", lambda i: i ^ 2)
-        return [
-            (block, (lambda p: p, 0, count)),
-            (by_x, (lambda p: p ^ 1, 0, count)),
-            (by_y, (lambda p: p ^ 2, 0, count)),
-            (lower, (lambda p: p ^ 3, 0, half)),
-            (upper, (lambda p: p ^ 3, half, count)),
-        ]
-    found = [(block, (lambda p: p, 0, count))]
-    ahead = {d % chips for d in (-1, 1, chips // 2 - 1, chips // 2, chips // 2 + 1)} - {0}
-    for steps in sorted(ahead):
-        got = permuted(block, "ang", lambda i, steps=steps: (i - 2 * steps) % devices)
-        found.append((got, (lambda p, steps=steps: lax.rem(p + steps, chips), 0, count)))
-    return found
+    half = group[1]
+    if devices == 8:
+        by_y = permuted(own[:half], "ang", lambda i: i ^ 4)
+        by_x = permuted(own[half:], "ang", lambda i: i ^ 2)
+        for_x, for_y = select_views(group, tiles, view_offset, conj_offset, own, by_y, by_x)
+        from_x = permuted(for_x, "ang", lambda i: i ^ 2)
+        from_y = permuted(for_y, "ang", lambda i: i ^ 4)
+        return [own, by_y, by_x, from_x, from_y]
+
+    def ahead(part, chips):
+        return permuted(part, "ang", lambda i: (i - 2 * chips) % devices)
+
+    turned = devices // 4
+    return [
+        own,
+        ahead(own[:, 32:], -1),
+        ahead(own[:, :32], 1),
+        ahead(own[:, 16:], turned - 1),
+        ahead(own, turned),
+        ahead(own[:, :48], turned + 1),
+    ]
 
 
 def on_device(
     sinogram, col_weights, col_start, view_offset, row_offset, conj_offset, ang_weights, row_weights
 ):
     tiles = col_weights.shape[0]
-    chips = lax.axis_size("ang") // 2
+    views = sinogram.shape[0]
+    exchanged = lax.axis_size("ang") == 8
+    core = lax.axis_index("ang") % 2
     groups = ((0, tiles // 4), (tiles // 4, tiles // 4))
     keeps, gots = [], []
+    halos = []
     for group in groups:
         own = resample(group, col_start, sinogram, col_weights)
         prev = permuted(own, "row", lambda i: i + 1)
         after = permuted(own, "row", lambda i: i - 1)
+        halos.append((prev, own, after))
+    blocks = []
+    for number, group in enumerate(groups):
+        prev, own, after = halos[number]
+        if number:
+            prev, after, blocks[-1] = lax.optimization_barrier((prev, after, blocks[-1]))
         keep, send = interpolate_rows(group, tiles, row_offset, prev, own, after, row_weights)
         got = permuted(send, "ang", lambda i: i ^ 1)
-        block = jnp.concatenate([keep, got], axis=1)
-        blocks = chip_blocks(block)
+        blocks.append(lax.dynamic_update_slice(keep, got, (0, (1 - core) * views, 0)))
+    for group, block in zip(groups, blocks):
+        parts = exchanged_blocks(group, tiles, view_offset, conj_offset, block)
         keep, send = interpolate_views(
-            group, tiles, chips, view_offset, conj_offset, ang_weights, blocks
+            group, tiles, exchanged, view_offset, conj_offset, ang_weights, parts
         )
         keeps.append(keep)
         gots.append(permuted(send, "ang", lambda i: i ^ 1))

time: 84.6 us -> 79.9 us (0.944); the launches traced: 84.1 us -> 78.5 us
  waiting for transfers between devices: 40.1 us -> 25.8 us
  starting transfers between devices: 23.9 us -> 31.7 us
  Pallas kernels: 16.2 us -> 17.2 us
    ppermute x16, waiting for transfers between devices: 40.1 us -> 25.8 us  [permuted(): lax.ppermute(value, axis, [(i, j) for i, j in pairs if 0 <= j < count])]
    ppermute x16, starting transfers between devices: 23.9 us -> 31.7 us  [permuted(): lax.ppermute(value, axis, [(i, j) for i, j in pairs if 0 <= j < count])]
    pallas_call x7 -> x9, Pallas kernels: 16.2 us -> 17.2 us  [call(): pl.pallas_call(body, out_shape=outs, in_specs=[SMEM if s else VMEM for s...]
    unnamed x22 -> x20, local copies, waits for them, and re-layouts: 3.54 us -> 3.51 us
  transfers between devices with their start and end apart: 16 -> 16, of which waited for: 11 -> 10; matrix products, arithmetic and copies ran while one was open for 0% -> 0% of each run, Pallas kernels for 9% -> 9%
where the time goes in v2:
time: 79.9 us; the launch traced here: 78.5 us
  starting transfers between devices  31.7 us (40%)
  waiting for transfers between devices  25.8 us (32%)
  Pallas kernels  17.2 us (22%)
  local copies, waits for them, and re-layouts  3.63 us (5%)
    ppermute x16, starting transfers between devices, permuted(): lax.ppermute(value, axis, [(i, j) for i, j in pairs if 0 <= j < count])  31.7 us
    ppermute x16, waiting for transfers between devices, permuted(): lax.ppermute(value, axis, [(i, j) for i, j in pairs if 0 <= j < count])  25.8 us
    pallas_call x9, Pallas kernels, call(): pl.pallas_call(body, out_shape=outs, in_specs=[SMEM if s else VMEM for s...  17.2 us
    unnamed x20, local copies, waits for them, and re-layouts  3.51 us
  transfers between devices with their start and end apart: 16, of which 10 were waited for; matrix products, arithmetic and copies ran while one was open for 0% of the time, Pallas kernels for 9%

profile of v2, /device:TPU:11, one launch (start us, length us, event | category | flops | bytes accessed | tf_op | source)
XLA Modules:
  0.0 78.5 jit_solution(6601811170165117654)
XLA Ops:
  0.0 1.6 %copy-done = bf16[32,256,128]{2,1,0:T(8,128)(2,1)S(1)} copy-done((bf16[32,256,128]{2,1,0:T(8,128)(2,1)S(1)}, bf16[32,256,128]{2,1,0:T(8,128)(2,1)}, u32[]{:S(2)}) %copy-start) | copy-done | bytes 2097176
  3.5 2.7 %shard_map.92.own_ref = f32[16,64,128]{2,1,0:T(8,128)S(1)} custom-call(s32[32]{0:T(128)S(1)} %copy-done.7, f32[32,2,4096]{2,1,0:T(2,128)S(1)} %copy-done.1, bf16[32,256,128]{2,1,0:T(8,128)(2,1)S(1)} %copy-done), custom_call_target="tpu_custom_call" | custom-call | flops 134217728 | bytes 6291456 | tf_op jit(solution)/shard_map/pallas_call | solution.py:22
  6.2 2.1 %collective-permute-start.3 = (f32[16,64,128]{2,1,0:T(8,128)S(1)}, f32[16,64,128]{2,1,0:T(8,128)S(1)}, u32[]{:S(2)}, u32[]{:S(2)}) collective-permute-start(f32[16,64,128]{2,1,0:T(8,128)S(1)} %shard_map.92.own_ref), channel_id=1, source_target_pairs={{1,0},{2,1},{3,2},{5,4},{6,5},{7,6},{9,8},{10,9},{11,10},{13,12},{... | collective-permute-start | bytes 1572872 | tf_op jit(solution)/shard_map/ppermute | solution.py:369
  8.3 3.2 %collective-permute-start.2 = (f32[16,64,128]{2,1,0:T(8,128)S(1)}, f32[16,64,128]{2,1,0:T(8,128)S(1)}, u32[]{:S(2)}, u32[]{:S(2)}) collective-permute-start(f32[16,64,128]{2,1,0:T(8,128)S(1)} %shard_map.92.own_ref), channel_id=1, source_target_pairs={{0,1},{1,2},{2,3},{4,5},{5,6},{6,7},{8,9},{9,10},{10,11},{12,13},{... | collective-permute-start | bytes 1572872 | tf_op jit(solution)/shard_map/ppermute | solution.py:369
  11.5 2.7 %shard_map.91.own_ref = f32[16,64,128]{2,1,0:T(8,128)S(1)} custom-call(s32[32]{0:T(128)S(1)} %copy-done.7, f32[32,2,4096]{2,1,0:T(2,128)S(1)} %copy-done.1, bf16[32,256,128]{2,1,0:T(8,128)(2,1)S(1)} %copy-done), custom_call_target="tpu_custom_call" | custom-call | flops 134217728 | bytes 6291456 | tf_op jit(solution)/shard_map/pallas_call | solution.py:22
  14.2 2.1 %collective-permute-start.1 = (f32[16,64,128]{2,1,0:T(8,128)S(1)}, f32[16,64,128]{2,1,0:T(8,128)S(1)}, u32[]{:S(2)}, u32[]{:S(2)}) collective-permute-start(f32[16,64,128]{2,1,0:T(8,128)S(1)} %shard_map.91.own_ref), channel_id=1, source_target_pairs={{1,0},{2,1},{3,2},{5,4},{6,5},{7,6},{9,8},{10,9},{11,10},{13,12},{... | collective-permute-start | bytes 1572872 | tf_op jit(solution)/shard_map/ppermute | solution.py:369
  16.4 3.2 %collective-permute-start = (f32[16,64,128]{2,1,0:T(8,128)S(1)}, f32[16,64,128]{2,1,0:T(8,128)S(1)}, u32[]{:S(2)}, u32[]{:S(2)}) collective-permute-start(f32[16,64,128]{2,1,0:T(8,128)S(1)} %shard_map.91.own_ref), channel_id=1, source_target_pairs={{0,1},{1,2},{2,3},{4,5},{5,6},{6,7},{8,9},{9,10},{10,11},{12,13},{... | collective-permute-start | bytes 1572872 | tf_op jit(solution)/shard_map/ppermute | solution.py:369
  19.5 1.4 %collective-permute-done.3.next_ref = f32[16,64,128]{2,1,0:T(8,128)S(1)} collective-permute-done((f32[16,64,128]{2,1,0:T(8,128)S(1)}, f32[16,64,128]{2,1,0:T(8,128)S(1)}, u32[]{:S(2)}, u32[]{:S(2)}) %collective-permute-start.3) | collective-permute-done | bytes 524320 | tf_op jit(solution)/shard_map/ppermute | solution.py:369
  20.9 1.8 %collective-permute-done.2.prev_ref = f32[16,64,128]{2,1,0:T(8,128)S(1)} collective-permute-done((f32[16,64,128]{2,1,0:T(8,128)S(1)}, f32[16,64,128]{2,1,0:T(8,128)S(1)}, u32[]{:S(2)}, u32[]{:S(2)}) %collective-permute-start.2) | collective-permute-done | bytes 524320 | tf_op jit(solution)/shard_map/ppermute | solution.py:369
  23.7 3.4 %collective-permute-start.4 = (f32[16,32,128]{2,1,0:T(8,128)S(1)}, f32[16,32,128]{2,1,0:T(8,128)S(1)}, u32[]{:S(2)}, u32[]{:S(2)}) collective-permute-start(f32[16,32,128]{2,1,0:T(8,128)S(1)} %get-tuple-element.21), channel_id=1, source_target_pairs={{0,4},{4,0},{8,12},{12,8},{16,20},{20,16},{24,28},{28,24},{1,5},{5... | collective-permute-start | bytes 786440 | tf_op jit(solution)/shard_map/ppermute | solution.py:369
  28.4 3.8 %collective-permute-done.1.next_ref = f32[16,64,128]{2,1,0:T(8,128)S(1)} collective-permute-done((f32[16,64,128]{2,1,0:T(8,128)S(1)}, f32[16,64,128]{2,1,0:T(8,128)S(1)}, u32[]{:S(2)}, u32[]{:S(2)}) %collective-permute-start.1) | collective-permute-done | bytes 524320 | tf_op jit(solution)/shard_map/ppermute | solution.py:369
  32.1 1.8 %collective-permute-done.prev_ref = f32[16,64,128]{2,1,0:T(8,128)S(1)} collective-permute-done((f32[16,64,128]{2,1,0:T(8,128)S(1)}, f32[16,64,128]{2,1,0:T(8,128)S(1)}, u32[]{:S(2)}, u32[]{:S(2)}) %collective-permute-start) | collective-permute-done | bytes 524320 | tf_op jit(solution)/shard_map/ppermute | solution.py:369
  35.0 1.9 %collective-permute-start.9 = (f32[16,32,128]{2,1,0:T(8,128)S(1)}, f32[16,32,128]{2,1,0:T(8,128)S(1)}, u32[]{:S(2)}, u32[]{:S(2)}) collective-permute-start(f32[16,32,128]{2,1,0:T(8,128)S(1)} %get-tuple-element.29), channel_id=1, source_target_pairs={{0,4},{4,0},{8,12},{12,8},{16,20},{20,16},{24,28},{28,24},{1,5},{5... | collective-permute-start | bytes 786440 | tf_op jit(solution)/shard_map/ppermute | solution.py:369
  37.1 1.4 %collective-permute-start.5 = (f32[8,64,128]{2,1,0:T(8,128)S(1)}, f32[8,64,128]{2,1,0:T(8,128)S(1)}, u32[]{:S(2)}, u32[]{:S(2)}) collective-permute-start(f32[8,64,128]{2,1,0:T(8,128)S(1)} %get-tuple-element.38), channel_id=1, source_target_pairs={{0,16},{4,20},{8,24},{12,28},{16,0},{20,4},{24,8},{28,12},{1,17},{... | collective-permute-start | bytes 786440 | tf_op jit(solution)/shard_map/ppermute | solution.py:369
  38.6 1.3 %collective-permute-start.11 = (f32[8,64,128]{2,1,0:T(8,128)S(1)}, f32[8,64,128]{2,1,0:T(8,128)S(1)}, u32[]{:S(2)}, u32[]{:S(2)}) collective-permute-start(f32[8,64,128]{2,1,0:T(8,128)S(1)} %get-tuple-element.35), channel_id=1, source_target_pairs={{0,8},{4,12},{8,0},{12,4},{16,24},{20,28},{24,16},{28,20},{1,9},{5... | collective-permute-start | bytes 786440 | tf_op jit(solution)/shard_map/ppermute | solution.py:369
  40.1 4.8 %collective-permute-done.6.by_x_ref.refs_2_ = f32[8,64,128]{2,1,0:T(8,128)S(1)} collective-permute-done((f32[8,64,128]{2,1,0:T(8,128)S(1)}, f32[8,64,128]{2,1,0:T(8,128)S(1)}, u32[]{:S(2)}, u32[]{:S(2)}) %collective-permute-start.6) | collective-permute-done | bytes 262176 | tf_op jit(solution)/shard_map/ppermute | solution.py:369
  45.7 1.3 %collective-permute-start.8 = (f32[8,88,128]{2,1,0:T(8,128)S(1)}, f32[8,88,128]{2,1,0:T(8,128)S(1)}, u32[]{:S(2)}, u32[]{:S(2)}) collective-permute-start(f32[8,88,128]{2,1,0:T(8,128)S(1)} %get-tuple-element.24), channel_id=1, source_target_pairs={{0,16},{4,20},{8,24},{12,28},{16,0},{20,4},{24,8},{28,12},{1,17},{... | collective-permute-start | bytes 1081352 | tf_op jit(solution)/shard_map/ppermute | solution.py:369
  47.0 3.5 %collective-permute-done.11.by_x_ref.refs_2_ = f32[8,64,128]{2,1,0:T(8,128)S(1)} collective-permute-done((f32[8,64,128]{2,1,0:T(8,128)S(1)}, f32[8,64,128]{2,1,0:T(8,128)S(1)}, u32[]{:S(2)}, u32[]{:S(2)}) %collective-permute-start.11) | collective-permute-done | bytes 262176 | tf_op jit(solution)/shard_map/ppermute | solution.py:369
  51.3 1.3 %collective-permute-start.13 = (f32[8,88,128]{2,1,0:T(8,128)S(1)}, f32[8,88,128]{2,1,0:T(8,128)S(1)}, u32[]{:S(2)}, u32[]{:S(2)}) collective-permute-start(f32[8,88,128]{2,1,0:T(8,128)S(1)} %get-tuple-element.31), channel_id=1, source_target_pairs={{0,16},{4,20},{8,24},{12,28},{16,0},{20,4},{24,8},{28,12},{1,17},{... | collective-permute-start | bytes 1081352 | tf_op jit(solution)/shard_map/ppermute | solution.py:369
  54.1 5.7 %collective-permute-done.7.refs_3_ = f32[8,80,128]{2,1,0:T(8,128)S(1)} collective-permute-done((f32[8,80,128]{2,1,0:T(8,128)S(1)}, f32[8,80,128]{2,1,0:T(8,128)S(1)}, u32[]{:S(2)}, u32[]{:S(2)}) %collective-permute-start.7) | collective-permute-done | bytes 327712 | tf_op jit(solution)/shard_map/ppermute | solution.py:369
  60.8 5.6 %collective-permute-start.14 = (f32[16,2,32,128]{3,2,1,0:T(8,128)S(1)}, f32[16,2,32,128]{3,2,1,0:T(8,128)S(1)}, u32[]{:S(2)}, u32[]{:S(2)}) collective-permute-start(f32[16,2,32,128]{3,2,1,0:T(8,128)S(1)} %get-tuple-element.33), channel_id=1, source_target_pairs={{0,4},{4,0},{8,12},{12,8},{16,20},{20,16},{24,28},{28,24},{1,5},{5... | collective-permute-start | bytes 1572872 | tf_op jit(solution)/shard_map/ppermute | solution.py:369
  67.8 3.0 %collective-permute-start.15 = (f32[16,2,32,128]{3,2,1,0:T(8,128)S(1)}, f32[16,2,32,128]{3,2,1,0:T(8,128)S(1)}, u32[]{:S(2)}, u32[]{:S(2)}) collective-permute-start(f32[16,2,32,128]{3,2,1,0:T(8,128)S(1)} %get-tuple-element.34), channel_id=1, source_target_pairs={{0,4},{4,0},{8,12},{12,8},{16,20},{20,16},{24,28},{28,24},{1,5},{5... | collective-permute-start | bytes 1572872 | tf_op jit(solution)/shard_map/ppermute | solution.py:369
  70.9 1.5 %collective-permute-done.15.refs_3_ = f32[16,2,32,128]{3,2,1,0:T(8,128)S(1)} collective-permute-done((f32[16,2,32,128]{3,2,1,0:T(8,128)S(1)}, f32[16,2,32,128]{3,2,1,0:T(8,128)S(1)}, u32[]{:S(2)}, u32[]{:S(2)}) %collective-permute-start.15) | collective-permute-done | bytes 524320 | tf_op jit(solution)/shard_map/ppermute | solution.py:369
  72.4 6.1 %shard_map.99 = f32[32,2,8192]{2,1,0:T(2,128)} custom-call(bf16[768,256]{1,0:T(8,128)(2,1)S(1)} %copy-done.9, bf16[768,256]{1,0:T(8,128)(2,1)S(1)} %copy-done.8, f32[16,2,32,128]{3,2,1,0:T(8,128)S(1)} %get-tuple-element.25.refs_0_, f32[16,2,32,128]{3,2,1,0:T(8,128)S(1)} %get-tuple-element.32.refs_1_, f32[16,2,32,128]{3,2,1,0:T(8,128)S(1)} %collective-permute-done.14.refs_2_, ...), custom_call_target="tpu_custom_call" | custom-call | flops 2415919104 | bytes 5242880 | tf_op jit(solution)/shard_map/pallas_call | solution.py:22
  (41 shorter events, 11.1 us)
Async XLA Ops:
  0.0 1.6 %copy-start = (bf16[32,256,128]{2,1,0:T(8,128)(2,1)S(1)}, bf16[32,256,128]{2,1,0:T(8,128)(2,1)}, u32[]{:S(2)}) copy-start(bf16[32,256,128]{2,1,0:T(8,128)(2,1)} %weights_ref.7) | copy-start | bytes 6291460
  6.2 16.5 %copy-start.3 = (f32[2,4096]{1,0:T(2,128)S(1)}, f32[2,4096]{1,0:T(2,128)}, u32[]{:S(2)}) copy-start(f32[2,4096]{1,0:T(2,128)} %weights_ref.10) | copy-start | bytes 98308
  6.2 16.5 %copy-start.6 = (s32[32]{0:T(128)S(1)}, s32[32]{0:T(128)}, u32[]{:S(2)}) copy-start(s32[32]{0:T(128)} %offset_ref.3) | copy-start | bytes 388
  6.2 14.7 %collective-permute-start.3 = (f32[16,64,128]{2,1,0:T(8,128)S(1)}, f32[16,64,128]{2,1,0:T(8,128)S(1)}, u32[]{:S(2)}, u32[]{:S(2)}) collective-permute-start(f32[16,64,128]{2,1,0:T(8,128)S(1)} %shard_map.92.own_ref), channel_id=1, source_target_pairs={{1,0},{2,1},{3,2},{5,4},{6,5},{7,6},{9,8},{10,9},{11,10},{13,12},{... | collective-permute-start | bytes 1572872 | tf_op jit(solution)/shard_map/ppermute | solution.py:369
  8.3 14.4 %collective-permute-start.2 = (f32[16,64,128]{2,1,0:T(8,128)S(1)}, f32[16,64,128]{2,1,0:T(8,128)S(1)}, u32[]{:S(2)}, u32[]{:S(2)}) collective-permute-start(f32[16,64,128]{2,1,0:T(8,128)S(1)} %shard_map.92.own_ref), channel_id=1, source_target_pairs={{0,1},{1,2},{2,3},{4,5},{5,6},{6,7},{8,9},{9,10},{10,11},{12,13},{... | collective-permute-start | bytes 1572872 | tf_op jit(solution)/shard_map/ppermute | solution.py:369
  14.2 17.9 %collective-permute-start.1 = (f32[16,64,128]{2,1,0:T(8,128)S(1)}, f32[16,64,128]{2,1,0:T(8,128)S(1)}, u32[]{:S(2)}, u32[]{:S(2)}) collective-permute-start(f32[16,64,128]{2,1,0:T(8,128)S(1)} %shard_map.91.own_ref), channel_id=1, source_target_pairs={{1,0},{2,1},{3,2},{5,4},{6,5},{7,6},{9,8},{10,9},{11,10},{13,12},{... | collective-permute-start | bytes 1572872 | tf_op jit(solution)/shard_map/ppermute | solution.py:369
  16.4 17.6 %collective-permute-start = (f32[16,64,128]{2,1,0:T(8,128)S(1)}, f32[16,64,128]{2,1,0:T(8,128)S(1)}, u32[]{:S(2)}, u32[]{:S(2)}) collective-permute-start(f32[16,64,128]{2,1,0:T(8,128)S(1)} %shard_map.91.own_ref), channel_id=1, source_target_pairs={{0,1},{1,2},{2,3},{4,5},{5,6},{6,7},{8,9},{9,10},{10,11},{12,13},{... | collective-permute-start | bytes 1572872 | tf_op jit(solution)/shard_map/ppermute | solution.py:369
  23.7 4.6 %collective-permute-start.4 = (f32[16,32,128]{2,1,0:T(8,128)S(1)}, f32[16,32,128]{2,1,0:T(8,128)S(1)}, u32[]{:S(2)}, u32[]{:S(2)}) collective-permute-start(f32[16,32,128]{2,1,0:T(8,128)S(1)} %get-tuple-element.21), channel_id=1, source_target_pairs={{0,4},{4,0},{8,12},{12,8},{16,20},{20,16},{24,28},{28,24},{1,5},{5... | collective-permute-start | bytes 786440 | tf_op jit(solution)/shard_map/ppermute | solution.py:369
  28.3 16.6 %copy-start.4 = (s32[32]{0:T(128)S(1)}, s32[32]{0:T(128)}, u32[]{:S(2)}) copy-start(s32[32]{0:T(128)} %view_ref.7) | copy-start | bytes 388
  28.4 16.6 %copy-start.5 = (s32[32]{0:T(128)S(1)}, s32[32]{0:T(128)}, u32[]{:S(2)}) copy-start(s32[32]{0:T(128)} %conj_ref.7) | copy-start | bytes 388
  35.0 3.6 %collective-permute-start.9 = (f32[16,32,128]{2,1,0:T(8,128)S(1)}, f32[16,32,128]{2,1,0:T(8,128)S(1)}, u32[]{:S(2)}, u32[]{:S(2)}) collective-permute-start(f32[16,32,128]{2,1,0:T(8,128)S(1)} %get-tuple-element.29), channel_id=1, source_target_pairs={{0,4},{4,0},{8,12},{12,8},{16,20},{20,16},{24,28},{28,24},{1,5},{5... | collective-permute-start | bytes 786440 | tf_op jit(solution)/shard_map/ppermute | solution.py:369
  36.9 22.8 %copy-start.2 = (f32[4,4096]{1,0:T(4,128)S(1)}, f32[4,4096]{1,0:T(4,128)}, u32[]{:S(2)}) copy-start(f32[4,4096]{1,0:T(4,128)} %weights_ref.11) | copy-start | bytes 196612
  36.9 8.0 %collective-permute-start.6 = (f32[8,64,128]{2,1,0:T(8,128)S(1)}, f32[8,64,128]{2,1,0:T(8,128)S(1)}, u32[]{:S(2)}, u32[]{:S(2)}) collective-permute-start(f32[8,64,128]{2,1,0:T(8,128)S(1)} %get-tuple-element.37), channel_id=1, source_target_pairs={{0,8},{4,12},{8,0},{12,4},{16,24},{20,28},{24,16},{28,20},{1,9},{5... | collective-permute-start | bytes 786440 | tf_op jit(solution)/shard_map/ppermute | solution.py:369
  37.1 7.8 %collective-permute-start.5 = (f32[8,64,128]{2,1,0:T(8,128)S(1)}, f32[8,64,128]{2,1,0:T(8,128)S(1)}, u32[]{:S(2)}, u32[]{:S(2)}) collective-permute-start(f32[8,64,128]{2,1,0:T(8,128)S(1)} %get-tuple-element.38), channel_id=1, source_target_pairs={{0,16},{4,20},{8,24},{12,28},{16,0},{20,4},{24,8},{28,12},{1,17},{... | collective-permute-start | bytes 786440 | tf_op jit(solution)/shard_map/ppermute | solution.py:369
  38.6 12.0 %collective-permute-start.11 = (f32[8,64,128]{2,1,0:T(8,128)S(1)}, f32[8,64,128]{2,1,0:T(8,128)S(1)}, u32[]{:S(2)}, u32[]{:S(2)}) collective-permute-start(f32[8,64,128]{2,1,0:T(8,128)S(1)} %get-tuple-element.35), channel_id=1, source_target_pairs={{0,8},{4,12},{8,0},{12,4},{16,24},{20,28},{24,16},{28,20},{1,9},{5... | collective-permute-start | bytes 786440 | tf_op jit(solution)/shard_map/ppermute | solution.py:369
  39.9 10.7 %collective-permute-start.10 = (f32[8,64,128]{2,1,0:T(8,128)S(1)}, f32[8,64,128]{2,1,0:T(8,128)S(1)}, u32[]{:S(2)}, u32[]{:S(2)}) collective-permute-start(f32[8,64,128]{2,1,0:T(8,128)S(1)} %get-tuple-element.36), channel_id=1, source_target_pairs={{0,16},{4,20},{8,24},{12,28},{16,0},{20,4},{24,8},{28,12},{1,17},{... | collective-permute-start | bytes 786440 | tf_op jit(solution)/shard_map/ppermute | solution.py:369
  45.7 26.7 %copy-start.8 = (bf16[768,256]{1,0:T(8,128)(2,1)S(1)}, bf16[768,256]{1,0:T(8,128)(2,1)}, u32[]{:S(2)}) copy-start(bf16[768,256]{1,0:T(8,128)(2,1)} %constant.32.low_ref) | copy-start | bytes 1179652
  45.7 26.7 %copy-start.9 = (bf16[768,256]{1,0:T(8,128)(2,1)S(1)}, bf16[768,256]{1,0:T(8,128)(2,1)}, u32[]{:S(2)}) copy-start(bf16[768,256]{1,0:T(8,128)(2,1)} %constant.29.high_ref) | copy-start | bytes 1179652
  45.7 14.0 %collective-permute-start.8 = (f32[8,88,128]{2,1,0:T(8,128)S(1)}, f32[8,88,128]{2,1,0:T(8,128)S(1)}, u32[]{:S(2)}, u32[]{:S(2)}) collective-permute-start(f32[8,88,128]{2,1,0:T(8,128)S(1)} %get-tuple-element.24), channel_id=1, source_target_pairs={{0,16},{4,20},{8,24},{12,28},{16,0},{20,4},{24,8},{28,12},{1,17},{... | collective-permute-start | bytes 1081352 | tf_op jit(solution)/shard_map/ppermute | solution.py:369
  51.3 15.5 %collective-permute-start.13 = (f32[8,88,128]{2,1,0:T(8,128)S(1)}, f32[8,88,128]{2,1,0:T(8,128)S(1)}, u32[]{:S(2)}, u32[]{:S(2)}) collective-permute-start(f32[8,88,128]{2,1,0:T(8,128)S(1)} %get-tuple-element.31), channel_id=1, source_target_pairs={{0,16},{4,20},{8,24},{12,28},{16,0},{20,4},{24,8},{28,12},{1,17},{... | collective-permute-start | bytes 1081352 | tf_op jit(solution)/shard_map/ppermute | solution.py:369
  52.6 7.2 %collective-permute-start.7 = (f32[8,80,128]{2,1,0:T(8,128)S(1)}, f32[8,80,128]{2,1,0:T(8,128)S(1)}, u32[]{:S(2)}, u32[]{:S(2)}) collective-permute-start(f32[8,80,128]{2,1,0:T(8,128)S(1)} %get-tuple-element.23), channel_id=1, source_target_pairs={{0,8},{4,12},{8,0},{12,4},{16,24},{20,28},{24,16},{28,20},{1,9},{5... | collective-permute-start | bytes 983048 | tf_op jit(solution)/shard_map/ppermute | solution.py:369
  53.8 13.0 %collective-permute-start.12 = (f32[8,80,128]{2,1,0:T(8,128)S(1)}, f32[8,80,128]{2,1,0:T(8,128)S(1)}, u32[]{:S(2)}, u32[]{:S(2)}) collective-permute-start(f32[8,80,128]{2,1,0:T(8,128)S(1)} %get-tuple-element.30), channel_id=1, source_target_pairs={{0,8},{4,12},{8,0},{12,4},{16,24},{20,28},{24,16},{28,20},{1,9},{5... | collective-permute-start | bytes 983048 | tf_op jit(solution)/shard_map/ppermute | solution.py:369
  60.8 10.1 %collective-permute-start.14 = (f32[16,2,32,128]{3,2,1,0:T(8,128)S(1)}, f32[16,2,32,128]{3,2,1,0:T(8,128)S(1)}, u32[]{:S(2)}, u32[]{:S(2)}) collective-permute-start(f32[16,2,32,128]{3,2,1,0:T(8,128)S(1)} %get-tuple-element.33), channel_id=1, source_target_pairs={{0,4},{4,0},{8,12},{12,8},{16,20},{20,16},{24,28},{28,24},{1,5},{5... | collective-permute-start | bytes 1572872 | tf_op jit(solution)/shard_map/ppermute | solution.py:369
  67.8 4.6 %collective-permute-start.15 = (f32[16,2,32,128]{3,2,1,0:T(8,128)S(1)}, f32[16,2,32,128]{3,2,1,0:T(8,128)S(1)}, u32[]{:S(2)}, u32[]{:S(2)}) collective-permute-start(f32[16,2,32,128]{3,2,1,0:T(8,128)S(1)} %get-tuple-element.34), channel_id=1, source_target_pairs={{0,4},{4,0},{8,12},{12,8},{16,20},{20,16},{24,28},{28,24},{1,5},{5... | collective-permute-start | bytes 1572872 | tf_op jit(solution)/shard_map/ppermute | solution.py:369
  (2 other events, 1.9 us)

commit v3 on v2

v3 whole, which is shorter than its diff:
```python
import functools
import math

import jax
import jax.numpy as jnp
import numpy as np
from jax import lax
from jax.experimental import pallas as pl
from jax.experimental.pallas import tpu as pltpu
from jax.sharding import PartitionSpec as P

KR = 256
GROUPS = ((0, 8), (8, 8))
LANES = 128
WINDOW = 3 * LANES
VMEM = pl.BlockSpec(memory_space=pltpu.VMEM)
SMEM = pl.BlockSpec(memory_space=pltpu.SMEM)
ANY = pl.BlockSpec(memory_space=pl.ANY)
PARAMS = pltpu.CompilerParams(vmem_limit_bytes=48 * 1024 * 1024)


COST = pl.CostEstimate(flops=1, bytes_accessed=1, transcendentals=0)
ROWS_COST = pl.CostEstimate(flops=1 << 32, bytes_accessed=1 << 26, transcendentals=0)


def call(body, outs, scratch, args, cost=COST):
    smem = [a.dtype == jnp.int32 for a in args]
    return pl.pallas_call(
        body,
        out_shape=outs,
        in_specs=[SMEM if s else VMEM for s in smem],
        out_specs=[VMEM] * len(outs),
        scratch_shapes=scratch,
        compiler_params=PARAMS,
        cost_estimate=cost,
    )(*args)


def f32(*shape):
    return jax.ShapeDtypeStruct(shape, jnp.float32)


def tile_of(index, group, tiles):
    first, half = group
    return jnp.where(index < half, first + index, tiles - first - 2 * half + index)


def split(x):
    high = x.astype(jnp.bfloat16)
    low = (x - high.astype(jnp.float32)).astype(jnp.bfloat16)
    return high, low


def dot(a, b):
    return jnp.dot(a, b, preferred_element_type=jnp.float32)


def resample_body(group, start_any, sino_any, weights_any, out_ref, start_ref, sino_ref, weights_ref, sems):
    tiles, band, _ = weights_any.shape
    views, rows, cols = sino_any.shape
    first, half = group
    quarter = views // 4
    copies = [pltpu.make_async_copy(start_any, start_ref, sems.at[0])]
    for i in range(4):
        part = pl.ds(quarter * i, quarter)
        copies.append(pltpu.make_async_copy(sino_any.at[part], sino_ref.at[part], sems.at[1 + i]))
    for i, begin in enumerate((first, tiles - first - half)):
        source = weights_any.at[pl.ds(begin, half)]
        copies.append(pltpu.make_async_copy(source, weights_ref.at[pl.ds(half * i, half)], sems.at[5 + i]))
    for copy in copies:
        copy.start()
    for copy in copies:
        copy.wait()

    def step(index, carry):
        start = start_ref[tile_of(index, group, tiles)]
        base = jnp.minimum(start // LANES * LANES, cols - WINDOW)
        shift = start - base
        slab = sino_ref[:, :, pl.ds(pl.multiple_of(base, LANES), WINDOW)]
        slab = slab.reshape(views * rows, WINDOW)
        slab = pltpu.roll(slab, WINDOW - shift, 1)[:, :band]
        high, low = split(slab)
        weights = weights_ref[index]
        out_ref[index] = dot(high, weights) + dot(low, weights)
        return carry

    lax.fori_loop(0, 2 * half, step, 0, unroll=2)


def resample(group, start, sino, weights):
    views, rows, cols = sino.shape
    count = 2 * group[1]
    return pl.pallas_call(
        functools.partial(resample_body, group),
        out_shape=f32(count, views * rows, LANES),
        in_specs=[ANY] * 3,
        out_specs=VMEM,
        scratch_shapes=[
            pltpu.SMEM(start.shape, jnp.int32),
            pltpu.VMEM(sino.shape, jnp.float32),
            pltpu.VMEM((count, *weights.shape[1:]), weights.dtype),
            pltpu.SemaphoreType.DMA((7,)),
        ],
        compiler_params=pltpu.CompilerParams(vmem_limit_bytes=(60 if group[0] == 0 else 40) << 20),
        cost_estimate=COST,
    )(start, sino, weights)


def rows_body(group, tiles, offset_ref, prev_ref, own_ref, next_ref, weights_ref, keep_ref, send_ref, stack):
    count, height, _ = own_ref.shape
    views = height // 2
    core = lax.axis_index("ang") % 2

    def step(index, slot):
        tile = tile_of(index, group, tiles)
        offset = offset_ref[tile]
        stack[slot, 0:height] = prev_ref[index]
        stack[slot, height : 2 * height] = own_ref[index]
        stack[slot, 2 * height : 3 * height] = next_ref[index]
        weights = weights_ref[:, pl.ds(pl.multiple_of(tile * LANES, LANES), LANES)]

        def picked(row):
            lifted = row + 2
            first = lifted // 2 * height + lifted % 2
            return stack[slot, pl.ds(first, views, stride=2), :]

        for out_ref, row in ((keep_ref, core), (send_ref, 1 - core)):
            lower = picked(row + offset)
            upper = picked(row + offset + 1)
            mixed = weights[0:1] * lower + weights[1:2] * upper
            out_ref[index] = mixed

    def pair(index, carry):
        step(2 * index, 0)
        step(2 * index + 1, 1)
        return carry

    lax.fori_loop(0, count // 2, pair, 0)


def interpolate_rows(group, tiles, offset, prev, own, after, weights):
    count, height, _ = own.shape
    return call(
        functools.partial(rows_body, group, tiles),
        [f32(count, height // 2, LANES)] * 2,
        [pltpu.VMEM((2, 3 * height, LANES), jnp.float32)],
        (offset, prev, own, after, weights),
        ROWS_COST,
    )


def merge_body(keep_ref, got_ref, *out_refs):
    half, views, _ = keep_ref.shape
    half //= 2
    core = lax.axis_index("ang") % 2
    mine = pl.multiple_of(core * views, 8)
    other = pl.multiple_of((1 - core) * views, 8)
    for part, out_ref in enumerate(out_refs):

        def step(index, slot, part=part, out_ref=out_ref):
            out_ref[index, pl.ds(mine, views)] = keep_ref[part * half + index]
            out_ref[index, pl.ds(other, views)] = got_ref[part * half + index]

        paired(step, half)


def merge(keep, got):
    count, views, _ = keep.shape
    return call(merge_body, [f32(count // 2, 2 * views, LANES)] * 2, [], (keep, got))


def select_body(
    group, tiles, view_ref, conj_ref, low_ref, high_ref, by_y_ref, by_x_ref, for_x_ref, for_y_ref, stack
):
    half = group[1]
    _, chip_views, lanes = low_ref.shape
    side = lax.axis_index("ang") // 2 % 2

    def shifts(index):
        tile = tile_of(index, group, tiles)
        shift = view_ref[tile]
        return shift, shift + conj_ref[tiles - 1 - tile]

    def slots(low, high):
        return low + lax.broadcasted_iota(jnp.int32, (high - low, lanes), 0)

    def across_x(index, slot):
        shift, opposite = shifts(index)
        own_at = pl.multiple_of((1 - side) * chip_views, 8)
        got_at = pl.multiple_of(side * chip_views, 8)
        stack[slot, pl.ds(own_at, chip_views)] = low_ref[index]
        stack[slot, pl.ds(got_at, chip_views)] = by_y_ref[index]
        near, far = stack.at[slot, 0:64], stack.at[slot, 64:128]
        for_x_ref[index, 0:32] = jnp.where(slots(0, 32) >= shift + 32, far[32:64], near[0:32])
        for_x_ref[index, 32:80] = jnp.where(slots(0, 48) >= opposite + 48, near[16:64], far[0:48])

    def across_y_first(index, slot):
        shift, opposite = shifts(half + index)
        stack[slot, 0:64] = high_ref[index]
        stack[slot, 64:128] = by_x_ref[index]
        both = stack.at[slot]
        for_y_ref[index, 0:40] = jnp.where(slots(0, 40) >= opposite, both[0:40], both[72:112])
        for_y_ref[index, 40:56] = both[40:56]
        for_y_ref[index, 56:72] = jnp.where(slots(56, 72) >= 88 + shift, both[96:112], both[56:72])
        for_y_ref[index, 72:88] = both[112:128]

    def across_y_last(index, slot):
        shift, opposite = shifts(half + index)
        stack[slot, 0:64] = by_x_ref[index]
        stack[slot, 64:128] = high_ref[index]
        both = stack.at[slot]
        for_y_ref[index, 0:16] = both[0:16]
        for_y_ref[index, 16:32] = jnp.where(slots(16, 32) < shift + 3, both[16:32], both[56:72])
        for_y_ref[index, 32:48] = both[72:88]
        for_y_ref[index, 48:88] = jnp.where(slots(48, 88) < 91 + opposite, both[88:128], both[16:56])

    paired(across_x, half)
    pl.when(side == 0)(lambda: paired(across_y_first, half))
    pl.when(side == 1)(lambda: paired(across_y_last, half))


def paired(step, count):
    def pair(index, carry):
        step(2 * index, 0)
        step(2 * index + 1, 1)
        return carry

    lax.fori_loop(0, count // 2, pair, 0)


def select_views(group, tiles, view_offset, conj_offset, low, high, by_y, by_x):
    half = group[1]
    return call(
        functools.partial(select_body, group, tiles),
        [f32(half, 80, LANES), f32(half, 88, LANES)],
        [pltpu.VMEM((2, 128, LANES), jnp.float32)],
        (view_offset, conj_offset, low, high, by_y, by_x),
    )


def views_body(group, tiles, exchanged, view_ref, conj_ref, weights_ref, *refs):
    *blocks, keep_ref, send_ref, stack = refs
    half = group[1]
    views = keep_ref.shape[2]
    index_ang = lax.axis_index("ang")
    side, core = index_ang // 2 % 2, index_ang % 2
    taps = weights_ref.shape[0]

    def interpolate(index, slot):
        tile = tile_of(index, group, tiles)
        weights = weights_ref[:, pl.ds(pl.multiple_of(tile * LANES, LANES), LANES)]
        shift = view_ref[tile]
        opposite = shift + conj_ref[tiles - 1 - tile]
        for part, by in ((0, 32 + shift), (1, 176 + opposite)):
            for out_ref, first in ((keep_ref, core), (send_ref, 1 - core)):
                begin = by + first * views
                total = weights[0:1] * stack[slot, pl.ds(begin, views)]
                for tap in range(1, taps):
                    total = total + weights[tap : tap + 1] * stack[slot, pl.ds(begin + tap, views)]
                out_ref[index, part] = total

    def filled(slot, *parts):
        at = 0
        for part in parts:
            stack[slot, at : at + part.shape[0]] = part[...]
            at += part.shape[0]

    if not exchanged:
        for part in range(2):

            def whole(index, slot, part=part):
                filled(slot, *(ref.at[index] for ref in blocks[part::2]))
                interpolate(part * half + index, slot)

            paired(whole, half)
        return
    own_low, own_high, by_y, by_x, from_x, from_y = blocks

    def first_half(index, slot):
        near, far = from_x.at[index, 0:32], from_x.at[index, 32:80]
        filled(slot, near, own_low.at[index], near, far, by_y.at[index], far)
        interpolate(index, slot)

    def last_half_first(index, slot):
        got = from_y.at[index]
        beside = by_x.at[index]
        filled(
            slot, got.at[56:88], own_high.at[index], beside.at[0:32], beside.at[16:64], got.at[0:72], got.at[0:40]
        )
        interpolate(half + index, slot)

    def last_half_last(index, slot):
        got = from_y.at[index]
        beside = by_x.at[index]
        filled(
            slot, beside.at[32:64], own_high.at[index], got.at[0:32], got.at[48:88], got.at[16:88], beside.at[0:48]
        )
        interpolate(half + index, slot)

    paired(first_half, half)
    pl.when(side == 0)(lambda: paired(last_half_first, half))
    pl.when(side == 1)(lambda: paired(last_half_last, half))


def interpolate_views(group, tiles, exchanged, view_offset, conj_offset, weights, blocks):
    count = 2 * group[1]
    views = blocks[0 if exchanged else 2].shape[1] // 2
    return call(
        functools.partial(views_body, group, tiles, exchanged),
        [f32(count, 2, views, LANES)] * 2,
        [pltpu.VMEM((2, 288, LANES), jnp.float32)],
        (view_offset, conj_offset, weights, *blocks),
    )


def ramp(lag):
    lag = lag.astype(np.float64)
    odd = np.abs(lag) % 2 == 1
    values = np.where(lag == 0, 0.25, np.where(odd, -1.0 / (math.pi**2 * np.maximum(lag * lag, 1.0)), 0.0))
    return np.where(np.abs(lag) <= KR, values, 0.0).astype(np.float32)


def filter_matrix():
    column = np.arange(WINDOW)[:, None]
    place = np.arange(2 * LANES)[None, :]
    lag = place - 2 * (column - LANES)
    even = ramp(lag)
    odd = ramp(lag - 1)[::-1]
    whole = np.concatenate([even, odd], axis=0)
    high = whole.astype(jnp.bfloat16)
    low = (whole - high.astype(np.float32)).astype(jnp.bfloat16)
    return jnp.asarray(high), jnp.asarray(low)


def stage_spans(groups, number, tiles):
    first, half = groups[number]
    begin = first - 1 if number else 0
    if number == len(groups) - 1:
        ranges = [(begin, tiles - begin)]
    else:
        ranges = [(begin, first + half - 1), (tiles - first - half + 1, tiles - begin)]
    spans = []
    for low, high in ranges:
        while low < high:
            count = min(4, high - low)
            spans.append((low, count))
            low += count
    return spans


def filter_body(groups, number, tiles, high_ref, low_ref, *refs):
    parts = refs[: 4 if number else 2]
    out_any, mixed, high_all, low_all, result, sems = refs[-6:]
    views = out_any.shape[0]
    core = lax.axis_index("ang") % 2
    if number == 0:
        for ref in (high_all, low_all):
            for part in range(2):
                ref[part, 0] = jnp.zeros(ref.shape[2:], ref.dtype)
                ref[part, tiles + 1] = jnp.zeros(ref.shape[2:], ref.dtype)

    def gather(group, keep, got, index, slot):
        tile = tile_of(index, group, tiles)
        for part in range(2):
            mixed[slot, part, pl.ds(core, views, stride=2), :] = keep[index, part]
            mixed[slot, part, pl.ds(1 - core, views, stride=2), :] = got[index, part]
            high, low = split(mixed[slot, part])
            high_all[part, tile + 1] = high
            low_all[part, tile + 1] = low

    paired(functools.partial(gather, groups[number], *parts[:2]), 2 * groups[number][1])
    if number:
        half = groups[number - 1][1]
        for index in range(half - 2, half + 2):
            gather(groups[number - 1], *parts[2:], index, index % 2)

    copies = []
    for place, (first, count) in enumerate(stage_spans(groups, number, tiles)):

        def window(ref):
            pieces = []
            for section in range(3):
                piece = ref[0, first + section : first + section + count]
                pieces.append(piece.reshape(count * 2 * views, LANES))
            for section in range(3):
                last = tiles - 1 - first + section
                piece = jnp.stack([ref[1, last - i] for i in range(count)])
                pieces.append(piece.reshape(count * 2 * views, LANES))
            return jnp.concatenate(pieces, axis=1)

        high, low = window(high_all), window(low_all)
        total = dot(high, high_ref[...]) + dot(low, high_ref[...]) + dot(high, low_ref[...])
        for i in range(count):
            block = total[2 * views * i : 2 * views * (i + 1)].reshape(views, 2, 2 * LANES)
            result[:, :, (first + i) * 2 * LANES : (first + i + 1) * 2 * LANES] = block
        columns = pl.ds(first * 2 * LANES, count * 2 * LANES)
        copy = pltpu.make_async_copy(
            result.at[:, :, columns], out_any.at[:, :, columns], sems.at[place]
        )
        copy.start()
        copies.append(copy)
    for copy in copies:
        copy.wait()


def ramp_filter(groups, number, tiles, keeps, gots, out):
    views = keeps[0].shape[2]
    args = [*filter_matrix(), keeps[number], gots[number]]
    if number:
        args += [keeps[number - 1], gots[number - 1], out]
    stored = pltpu.VMEM((2, tiles + 2, 2 * views, LANES), jnp.bfloat16)
    shape = f32(views, 2, 2 * tiles * LANES)
    return pl.pallas_call(
        functools.partial(filter_body, groups, number, tiles),
        out_shape=shape,
        in_specs=[VMEM] * 6 + [ANY] if number else [VMEM] * 4,
        out_specs=ANY,
        scratch_shapes=[
            pltpu.VMEM((2, 2, 2 * views, LANES), jnp.float32),
            stored,
            stored,
            pltpu.VMEM(shape.shape, jnp.float32),
            pltpu.SemaphoreType.DMA((len(stage_spans(groups, number, tiles)),)),
        ],
        input_output_aliases={6: 0} if number else {},
        compiler_params=PARAMS,
        cost_estimate=COST,
    )(*args)


def permuted(value, axis, target):
    count = lax.axis_size(axis)
    pairs = [(i, target(i)) for i in range(count)]
    return lax.ppermute(value, axis, [(i, j) for i, j in pairs if 0 <= j < count])


def first_exchange(low, high):
    if lax.axis_size("ang") == 8:
        by_y = permuted(low, "ang", lambda i: i ^ 4)
        by_x = permuted(high, "ang", lambda i: i ^ 2)
        return [by_y, by_x]
    return []


def second_exchange(group, tiles, view_offset, conj_offset, low, high, first):
    devices = lax.axis_size("ang")
    if first:
        for_x, for_y = select_views(group, tiles, view_offset, conj_offset, low, high, *first)
        from_x = permuted(for_x, "ang", lambda i: i ^ 2)
        from_y = permuted(for_y, "ang", lambda i: i ^ 4)
        return [low, high, *first, from_x, from_y]

    def ahead(begin, end, chips):
        def target(i):
            return (i - 2 * chips) % devices

        return [permuted(part[:, begin:end], "ang", target) for part in (low, high)]

    turned = devices // 4
    return [
        *ahead(32, 64, -1),
        low,
        high,
        *ahead(0, 32, 1),
        *ahead(16, 64, turned - 1),
        *ahead(0, 64, turned),
        *ahead(0, 48, turned + 1),
    ]


def on_device(
    sinogram, col_weights, col_start, view_offset, row_offset, conj_offset, ang_weights, row_weights
):
    tiles = col_weights.shape[0]
    exchanged = lax.axis_size("ang") == 8
    groups = GROUPS
    halos, owns = [], []
    for group in groups:
        own = resample(group, col_start, sinogram, col_weights)
        prev = permuted(own, "row", lambda i: i + 1)
        after = permuted(own, "row", lambda i: i - 1)
        halos.append((prev, own, after))
    for group, (prev, own, after) in zip(groups, halos):
        keep, send = interpolate_rows(group, tiles, row_offset, prev, own, after, row_weights)
        got = permuted(send, "ang", lambda i: i ^ 1)
        owns.append(merge(keep, got))
    keeps, gots = [], []
    out = None
    for number, group in enumerate(groups):
        low, high = owns[number]
        first = first_exchange(low, high)
        if keeps:
            first, keeps[-1] = lax.optimization_barrier((first, keeps[-1]))
        blocks = second_exchange(group, tiles, view_offset, conj_offset, low, high, first)
        if keeps:
            out = ramp_filter(groups, number - 1, tiles, keeps, gots, out)
            blocks[-1], out = lax.optimization_barrier((blocks[-1], out))
        keep, send = interpolate_views(
            group, tiles, exchanged, view_offset, conj_offset, ang_weights, blocks
        )
        keeps.append(keep)
        gots.append(permuted(send, "ang", lambda i: i ^ 1))
    return ramp_filter(groups, len(groups) - 1, tiles, keeps, gots, out)


def solution(mesh):
    return jax.shard_map(
        on_device,
        mesh=mesh,
        in_specs=(P("ang", "row", None), P(), P(), P(), P(), P(), P(), P()),
        out_specs=P("ang", "row", None),
        check_vma=False,
    )
```

time: 79.9 us -> 69.8 us (0.87); the launches traced: 78.5 us -> 69.4 us
  starting transfers between devices: 31.7 us -> 27.9 us
  local copies, waits for them, and re-layouts: 3.63 us -> 0.05 us
  waiting for transfers between devices: 25.8 us -> 22.7 us
  Pallas kernels: 17.2 us -> 18.5 us
    pallas_call x0 -> x4, Pallas kernels: none -> 12.7 us  [the longest x2 7.5 us: resample(): pl.pallas_call(functools.partial(resample_body, group), out_shape=f32(cou...]
    pallas_call x9 -> x8, Pallas kernels: 17.2 us -> 5.76 us  [call(): pl.pallas_call(body, out_shape=outs, in_specs=[SMEM if s else VMEM for s...]
    ppermute x16, starting transfers between devices: 31.7 us -> 27.9 us  [permuted(): lax.ppermute(value, axis, [(i, j) for i, j in pairs if 0 <= j < count])]
    unnamed x20 -> x22, local copies, waits for them, and re-layouts: 3.51 us -> 0.05 us
    ppermute x16, waiting for transfers between devices: 25.8 us -> 22.7 us  [permuted(): lax.ppermute(value, axis, [(i, j) for i, j in pairs if 0 <= j < count])]
  transfers between devices with their start and end apart: 16 -> 16, of which waited for: 10 -> 11; matrix products, arithmetic and copies ran while one was open for 0% -> 0% of each run, Pallas kernels for 9% -> 14%
where the time goes in v3:
time: 69.8 us; the launch traced here: 69.4 us
  starting transfers between devices  27.9 us (40%)
  waiting for transfers between devices  22.7 us (33%)
  Pallas kernels  18.5 us (27%)
    ppermute x16, starting transfers between devices, permuted(): lax.ppermute(value, axis, [(i, j) for i, j in pairs if 0 <= j < count])  27.9 us
    ppermute x16, waiting for transfers between devices, permuted(): lax.ppermute(value, axis, [(i, j) for i, j in pairs if 0 <= j < count])  22.7 us
    pallas_call x2, Pallas kernels, resample(): pl.pallas_call(functools.partial(resample_body, group), out_shape=f32(cou...  7.5 us
    pallas_call x8, Pallas kernels, call(): pl.pallas_call(body, out_shape=outs, in_specs=[SMEM if s else VMEM for s...  5.76 us
    pallas_call x2, Pallas kernels, ramp_filter(): pl.pallas_call(functools.partial(filter_body, groups, number, tiles), out...  5.24 us
  transfers between devices with their start and end apart: 16, of which 11 were waited for; matrix products, arithmetic and copies ran while one was open for 0% of the time, Pallas kernels for 14%

profile of v3, /device:TPU:11, one launch (start us, length us, event | category | flops | bytes accessed | tf_op | source)
XLA Modules:
  0.0 69.4 jit_solution(14109082511117382788)
XLA Ops:
  0.0 4.7 %shard_map.121.own_ref = f32[16,64,128]{2,1,0:T(8,128)} custom-call(s32[32]{0:T(128)} %start_any.3, f32[32,2,4096]{2,1,0:T(2,128)} %sino_any.3, bf16[32,256,128]{2,1,0:T(8,128)(2,1)} %weights_any.3), custom_call_target="tpu_custom_call" | custom-call | flops 1 | bytes 1 | tf_op jit(solution)/shard_map/pallas_call | solution.py:93
  4.8 2.2 %collective-permute-start.6 = (f32[16,64,128]{2,1,0:T(8,128)}, f32[16,64,128]{2,1,0:T(8,128)S(1)}, u32[]{:S(2)}, u32[]{:S(2)}) collective-permute-start(f32[16,64,128]{2,1,0:T(8,128)} %shard_map.121.own_ref), channel_id=1, source_target_pairs={{1,0},{2,1},{3,2},{5,4},{6,5},{7,6},{9,8},{10,9},{11,10},{13,12},{... | collective-permute-start | bytes 1572872 | tf_op jit(solution)/shard_map/ppermute | solution.py:434
  7.0 3.2 %collective-permute-start.5 = (f32[16,64,128]{2,1,0:T(8,128)}, f32[16,64,128]{2,1,0:T(8,128)S(1)}, u32[]{:S(2)}, u32[]{:S(2)}) collective-permute-start(f32[16,64,128]{2,1,0:T(8,128)} %shard_map.121.own_ref), channel_id=1, source_target_pairs={{0,1},{1,2},{2,3},{4,5},{5,6},{6,7},{8,9},{9,10},{10,11},{12,13},{... | collective-permute-start | bytes 1572872 | tf_op jit(solution)/shard_map/ppermute | solution.py:434
  10.2 2.8 %shard_map.118.own_ref = f32[16,64,128]{2,1,0:T(8,128)S(1)} custom-call(s32[32]{0:T(128)S(1)} %copy-done.8, f32[32,2,4096]{2,1,0:T(2,128)S(1)} %copy-done.1, bf16[32,256,128]{2,1,0:T(8,128)(2,1)S(1)} %copy-done), custom_call_target="tpu_custom_call" | custom-call | flops 1 | bytes 1 | tf_op jit(solution)/shard_map/pallas_call | solution.py:93
  13.0 2.1 %collective-permute-start.1 = (f32[16,64,128]{2,1,0:T(8,128)S(1)}, f32[16,64,128]{2,1,0:T(8,128)S(1)}, u32[]{:S(2)}, u32[]{:S(2)}) collective-permute-start(f32[16,64,128]{2,1,0:T(8,128)S(1)} %shard_map.118.own_ref), channel_id=1, source_target_pairs={{1,0},{2,1},{3,2},{5,4},{6,5},{7,6},{9,8},{10,9},{11,10},{13,12},{... | collective-permute-start | bytes 1572872 | tf_op jit(solution)/shard_map/ppermute | solution.py:434
  15.1 3.2 %collective-permute-start = (f32[16,64,128]{2,1,0:T(8,128)S(1)}, f32[16,64,128]{2,1,0:T(8,128)S(1)}, u32[]{:S(2)}, u32[]{:S(2)}) collective-permute-start(f32[16,64,128]{2,1,0:T(8,128)S(1)} %shard_map.118.own_ref), channel_id=1, source_target_pairs={{0,1},{1,2},{2,3},{4,5},{5,6},{6,7},{8,9},{9,10},{10,11},{12,13},{... | collective-permute-start | bytes 1572872 | tf_op jit(solution)/shard_map/ppermute | solution.py:434
  18.3 1.5 %collective-permute-done.6.next_ref = f32[16,64,128]{2,1,0:T(8,128)S(1)} collective-permute-done((f32[16,64,128]{2,1,0:T(8,128)}, f32[16,64,128]{2,1,0:T(8,128)S(1)}, u32[]{:S(2)}, u32[]{:S(2)}) %collective-permute-start.6) | collective-permute-done | bytes 524320 | tf_op jit(solution)/shard_map/ppermute | solution.py:434
  19.8 1.8 %collective-permute-done.5.prev_ref = f32[16,64,128]{2,1,0:T(8,128)S(1)} collective-permute-done((f32[16,64,128]{2,1,0:T(8,128)}, f32[16,64,128]{2,1,0:T(8,128)S(1)}, u32[]{:S(2)}, u32[]{:S(2)}) %collective-permute-start.5) | collective-permute-done | bytes 524320 | tf_op jit(solution)/shard_map/ppermute | solution.py:434
  22.6 3.4 %collective-permute-start.7 = (f32[16,32,128]{2,1,0:T(8,128)S(1)}, f32[16,32,128]{2,1,0:T(8,128)S(1)}, u32[]{:S(2)}, u32[]{:S(2)}) collective-permute-start(f32[16,32,128]{2,1,0:T(8,128)S(1)} %get-tuple-element.31), channel_id=1, source_target_pairs={{0,4},{4,0},{8,12},{12,8},{16,20},{20,16},{24,28},{28,24},{1,5},{5... | collective-permute-start | bytes 786440 | tf_op jit(solution)/shard_map/ppermute | solution.py:434
  26.0 1.2 %collective-permute-done.7.got_ref = f32[16,32,128]{2,1,0:T(8,128)S(1)} collective-permute-done((f32[16,32,128]{2,1,0:T(8,128)S(1)}, f32[16,32,128]{2,1,0:T(8,128)S(1)}, u32[]{:S(2)}, u32[]{:S(2)}) %collective-permute-start.7) | collective-permute-done | bytes 262176 | tf_op jit(solution)/shard_map/ppermute | solution.py:434
  27.3 1.3 %collective-permute-start.8 = (f32[8,64,128]{2,1,0:T(8,128)S(1)}, f32[8,64,128]{2,1,0:T(8,128)S(1)}, u32[]{:S(2)}, u32[]{:S(2)}) collective-permute-start(f32[8,64,128]{2,1,0:T(8,128)S(1)} %get-tuple-element.32.low_ref.refs_0_), channel_id=1, source_target_pairs={{0,16},{4,20},{8,24},{12,28},{16,0},{20,4},{24,8},{28,12},{1,17},{... | collective-permute-start | bytes 786440 | tf_op jit(solution)/shard_map/ppermute | solution.py:434
  28.8 2.2 %collective-permute-done.1.next_ref = f32[16,64,128]{2,1,0:T(8,128)S(1)} collective-permute-done((f32[16,64,128]{2,1,0:T(8,128)S(1)}, f32[16,64,128]{2,1,0:T(8,128)S(1)}, u32[]{:S(2)}, u32[]{:S(2)}) %collective-permute-start.1) | collective-permute-done | bytes 524320 | tf_op jit(solution)/shard_map/ppermute | solution.py:434
  31.0 1.8 %collective-permute-done.prev_ref = f32[16,64,128]{2,1,0:T(8,128)S(1)} collective-permute-done((f32[16,64,128]{2,1,0:T(8,128)S(1)}, f32[16,64,128]{2,1,0:T(8,128)S(1)}, u32[]{:S(2)}, u32[]{:S(2)}) %collective-permute-start) | collective-permute-done | bytes 524320 | tf_op jit(solution)/shard_map/ppermute | solution.py:434
  33.9 1.9 %collective-permute-start.2 = (f32[16,32,128]{2,1,0:T(8,128)S(1)}, f32[16,32,128]{2,1,0:T(8,128)S(1)}, u32[]{:S(2)}, u32[]{:S(2)}) collective-permute-start(f32[16,32,128]{2,1,0:T(8,128)S(1)} %get-tuple-element.27), channel_id=1, source_target_pairs={{0,4},{4,0},{8,12},{12,8},{16,20},{20,16},{24,28},{28,24},{1,5},{5... | collective-permute-start | bytes 786440 | tf_op jit(solution)/shard_map/ppermute | solution.py:434
  36.6 1.3 %collective-permute-start.11 = (f32[8,88,128]{2,1,0:T(8,128)S(1)}, f32[8,88,128]{2,1,0:T(8,128)S(1)}, u32[]{:S(2)}, u32[]{:S(2)}) collective-permute-start(f32[8,88,128]{2,1,0:T(8,128)S(1)} %get-tuple-element.35), channel_id=1, source_target_pairs={{0,16},{4,20},{8,24},{12,28},{16,0},{20,4},{24,8},{28,12},{1,17},{... | collective-permute-start | bytes 1081352 | tf_op jit(solution)/shard_map/ppermute | solution.py:434
  38.4 1.3 %collective-permute-start.4 = (f32[8,64,128]{2,1,0:T(8,128)S(1)}, f32[8,64,128]{2,1,0:T(8,128)S(1)}, u32[]{:S(2)}, u32[]{:S(2)}) collective-permute-start(f32[8,64,128]{2,1,0:T(8,128)S(1)} %get-tuple-element.29.high_ref.refs_1_), channel_id=1, source_target_pairs={{0,8},{4,12},{8,0},{12,4},{16,24},{20,28},{24,16},{28,20},{1,9},{5... | collective-permute-start | bytes 786440 | tf_op jit(solution)/shard_map/ppermute | solution.py:434
  39.7 6.7 %collective-permute-done.10.refs_4_ = f32[8,80,128]{2,1,0:T(8,128)S(1)} collective-permute-done((f32[8,80,128]{2,1,0:T(8,128)S(1)}, f32[8,80,128]{2,1,0:T(8,128)S(1)}, u32[]{:S(2)}, u32[]{:S(2)}) %collective-permute-start.10) | collective-permute-done | bytes 327712 | tf_op jit(solution)/shard_map/ppermute | solution.py:434
  47.4 3.1 %collective-permute-start.14 = (f32[16,2,32,128]{3,2,1,0:T(8,128)S(1)}, f32[16,2,32,128]{3,2,1,0:T(8,128)S(1)}, u32[]{:S(2)}, u32[]{:S(2)}) collective-permute-start(f32[16,2,32,128]{3,2,1,0:T(8,128)S(1)} %get-tuple-element.42), channel_id=1, source_target_pairs={{0,4},{4,0},{8,12},{12,8},{16,20},{20,16},{24,28},{28,24},{1,5},{5... | collective-permute-start | bytes 1572872 | tf_op jit(solution)/shard_map/ppermute | solution.py:434
  50.8 1.2 %collective-permute-done.4.by_x_ref.refs_3_ = f32[8,64,128]{2,1,0:T(8,128)S(1)} collective-permute-done((f32[8,64,128]{2,1,0:T(8,128)S(1)}, f32[8,64,128]{2,1,0:T(8,128)S(1)}, u32[]{:S(2)}, u32[]{:S(2)}) %collective-permute-start.4) | collective-permute-done | bytes 262176 | tf_op jit(solution)/shard_map/ppermute | solution.py:434
  54.3 2.5 %shard_map.127.refs_4_ = f32[32,2,8192]{2,1,0:T(2,128)} custom-call(bf16[768,256]{1,0:T(8,128)(2,1)S(1)} %copy-done.3, bf16[768,256]{1,0:T(8,128)(2,1)S(1)} %copy-done.2, f32[16,2,32,128]{3,2,1,0:T(8,128)S(1)} %get-tuple-element.41.refs_0_.refs_2_, f32[16,2,32,128]{3,2,1,0:T(8,128)S(1)} %collective-permute-done.14.refs_1_.refs_3_), custom_call_target="tpu_custom_call" | custom-call | flops 1 | bytes 1 | tf_op jit(solution)/shard_map/pallas_call | solution.py:413
  56.8 4.3 %collective-permute-done.13.refs_5_ = f32[8,88,128]{2,1,0:T(8,128)S(1)} collective-permute-done((f32[8,88,128]{2,1,0:T(8,128)S(1)}, f32[8,88,128]{2,1,0:T(8,128)S(1)}, u32[]{:S(2)}, u32[]{:S(2)}) %collective-permute-start.13) | collective-permute-done | bytes 360480 | tf_op jit(solution)/shard_map/ppermute | solution.py:434
  62.5 2.6 %collective-permute-start.15 = (f32[16,2,32,128]{3,2,1,0:T(8,128)S(1)}, f32[16,2,32,128]{3,2,1,0:T(8,128)S(1)}, u32[]{:S(2)}, u32[]{:S(2)}) collective-permute-start(f32[16,2,32,128]{3,2,1,0:T(8,128)S(1)} %get-tuple-element.45), channel_id=1, source_target_pairs={{0,4},{4,0},{8,12},{12,8},{16,20},{20,16},{24,28},{28,24},{1,5},{5... | collective-permute-start | bytes 1572872 | tf_op jit(solution)/shard_map/ppermute | solution.py:434
  65.1 1.5 %collective-permute-done.15.refs_1_ = f32[16,2,32,128]{3,2,1,0:T(8,128)S(1)} collective-permute-done((f32[16,2,32,128]{3,2,1,0:T(8,128)S(1)}, f32[16,2,32,128]{3,2,1,0:T(8,128)S(1)}, u32[]{:S(2)}, u32[]{:S(2)}) %collective-permute-start.15) | collective-permute-done | bytes 524320 | tf_op jit(solution)/shard_map/ppermute | solution.py:434
  66.6 2.7 %shard_map.129 = f32[32,2,8192]{2,1,0:T(2,128)} custom-call(bf16[768,256]{1,0:T(8,128)(2,1)S(1)} %copy-done.3, bf16[768,256]{1,0:T(8,128)(2,1)S(1)} %copy-done.2, f32[16,2,32,128]{3,2,1,0:T(8,128)S(1)} %get-tuple-element.44.refs_0_, f32[16,2,32,128]{3,2,1,0:T(8,128)S(1)} %collective-permute-done.15.refs_1_, ...), custom_call_target="tpu_custom_call", output_to_operand_aliasing={{}: (6, {})} | custom-call | flops 1 | bytes 1 | tf_op jit(solution)/shard_map/pallas_call | solution.py:413
  (42 shorter events, 8.7 us)
Async XLA Ops:
  0.0 10.2 %copy-start = (bf16[32,256,128]{2,1,0:T(8,128)(2,1)S(1)}, bf16[32,256,128]{2,1,0:T(8,128)(2,1)}, u32[]{:S(2)}) copy-start(bf16[32,256,128]{2,1,0:T(8,128)(2,1)} %weights_any.3) | copy-start | bytes 6291460
  0.0 10.2 %copy-start.1 = (f32[32,2,4096]{2,1,0:T(2,128)S(1)}, f32[32,2,4096]{2,1,0:T(2,128)}, u32[]{:S(2)}) copy-start(f32[32,2,4096]{2,1,0:T(2,128)} %sino_any.3) | copy-start | bytes 3145732
  4.7 16.8 %copy-start.4 = (f32[16,64,128]{2,1,0:T(8,128)S(1)}, f32[16,64,128]{2,1,0:T(8,128)}, u32[]{:S(2)}) copy-start(f32[16,64,128]{2,1,0:T(8,128)} %shard_map.121.own_ref) | copy-start | bytes 1572868
  4.7 16.8 %copy-start.9 = (f32[2,4096]{1,0:T(2,128)S(1)}, f32[2,4096]{1,0:T(2,128)}, u32[]{:S(2)}) copy-start(f32[2,4096]{1,0:T(2,128)} %weights_ref.5) | copy-start | bytes 98308
  4.8 16.8 %copy-start.10 = (s32[32]{0:T(128)S(1)}, s32[32]{0:T(128)}, u32[]{:S(2)}) copy-start(s32[32]{0:T(128)} %offset_ref.3) | copy-start | bytes 388
  4.8 15.0 %collective-permute-start.6 = (f32[16,64,128]{2,1,0:T(8,128)}, f32[16,64,128]{2,1,0:T(8,128)S(1)}, u32[]{:S(2)}, u32[]{:S(2)}) collective-permute-start(f32[16,64,128]{2,1,0:T(8,128)} %shard_map.121.own_ref), channel_id=1, source_target_pairs={{1,0},{2,1},{3,2},{5,4},{6,5},{7,6},{9,8},{10,9},{11,10},{13,12},{... | collective-permute-start | bytes 1572872 | tf_op jit(solution)/shard_map/ppermute | solution.py:434
  7.0 14.6 %collective-permute-start.5 = (f32[16,64,128]{2,1,0:T(8,128)}, f32[16,64,128]{2,1,0:T(8,128)S(1)}, u32[]{:S(2)}, u32[]{:S(2)}) collective-permute-start(f32[16,64,128]{2,1,0:T(8,128)} %shard_map.121.own_ref), channel_id=1, source_target_pairs={{0,1},{1,2},{2,3},{4,5},{5,6},{6,7},{8,9},{9,10},{10,11},{12,13},{... | collective-permute-start | bytes 1572872 | tf_op jit(solution)/shard_map/ppermute | solution.py:434
  13.0 18.0 %collective-permute-start.1 = (f32[16,64,128]{2,1,0:T(8,128)S(1)}, f32[16,64,128]{2,1,0:T(8,128)S(1)}, u32[]{:S(2)}, u32[]{:S(2)}) collective-permute-start(f32[16,64,128]{2,1,0:T(8,128)S(1)} %shard_map.118.own_ref), channel_id=1, source_target_pairs={{1,0},{2,1},{3,2},{5,4},{6,5},{7,6},{9,8},{10,9},{11,10},{13,12},{... | collective-permute-start | bytes 1572872 | tf_op jit(solution)/shard_map/ppermute | solution.py:434
  15.1 17.7 %collective-permute-start = (f32[16,64,128]{2,1,0:T(8,128)S(1)}, f32[16,64,128]{2,1,0:T(8,128)S(1)}, u32[]{:S(2)}, u32[]{:S(2)}) collective-permute-start(f32[16,64,128]{2,1,0:T(8,128)S(1)} %shard_map.118.own_ref), channel_id=1, source_target_pairs={{0,1},{1,2},{2,3},{4,5},{5,6},{6,7},{8,9},{9,10},{10,11},{12,13},{... | collective-permute-start | bytes 1572872 | tf_op jit(solution)/shard_map/ppermute | solution.py:434
  22.6 4.6 %collective-permute-start.7 = (f32[16,32,128]{2,1,0:T(8,128)S(1)}, f32[16,32,128]{2,1,0:T(8,128)S(1)}, u32[]{:S(2)}, u32[]{:S(2)}) collective-permute-start(f32[16,32,128]{2,1,0:T(8,128)S(1)} %get-tuple-element.31), channel_id=1, source_target_pairs={{0,4},{4,0},{8,12},{12,8},{16,20},{20,16},{24,28},{28,24},{1,5},{5... | collective-permute-start | bytes 786440 | tf_op jit(solution)/shard_map/ppermute | solution.py:434
  27.3 8.5 %collective-permute-start.8 = (f32[8,64,128]{2,1,0:T(8,128)S(1)}, f32[8,64,128]{2,1,0:T(8,128)S(1)}, u32[]{:S(2)}, u32[]{:S(2)}) collective-permute-start(f32[8,64,128]{2,1,0:T(8,128)S(1)} %get-tuple-element.32.low_ref.refs_0_), channel_id=1, source_target_pairs={{0,16},{4,20},{8,24},{12,28},{16,0},{20,4},{24,8},{28,12},{1,17},{... | collective-permute-start | bytes 786440 | tf_op jit(solution)/shard_map/ppermute | solution.py:434
  28.6 17.8 %copy-start.5 = (f32[4,4096]{1,0:T(4,128)S(1)}, f32[4,4096]{1,0:T(4,128)}, u32[]{:S(2)}) copy-start(f32[4,4096]{1,0:T(4,128)} %weights_ref.7) | copy-start | bytes 196612
  28.6 7.2 %collective-permute-start.9 = (f32[8,64,128]{2,1,0:T(8,128)S(1)}, f32[8,64,128]{2,1,0:T(8,128)S(1)}, u32[]{:S(2)}, u32[]{:S(2)}) collective-permute-start(f32[8,64,128]{2,1,0:T(8,128)S(1)} %get-tuple-element.33.high_ref.refs_1_), channel_id=1, source_target_pairs={{0,8},{4,12},{8,0},{12,4},{16,24},{20,28},{24,16},{28,20},{1,9},{5... | collective-permute-start | bytes 786440 | tf_op jit(solution)/shard_map/ppermute | solution.py:434
  33.8 20.4 %copy-start.2 = (bf16[768,256]{1,0:T(8,128)(2,1)S(1)}, bf16[768,256]{1,0:T(8,128)(2,1)}, u32[]{:S(2)}) copy-start(bf16[768,256]{1,0:T(8,128)(2,1)} %constant.5.clone.low_ref) | copy-start | bytes 1179652
  33.9 20.4 %copy-start.3 = (bf16[768,256]{1,0:T(8,128)(2,1)S(1)}, bf16[768,256]{1,0:T(8,128)(2,1)}, u32[]{:S(2)}) copy-start(bf16[768,256]{1,0:T(8,128)(2,1)} %constant.4.clone.high_ref) | copy-start | bytes 1179652
  33.9 4.3 %collective-permute-start.2 = (f32[16,32,128]{2,1,0:T(8,128)S(1)}, f32[16,32,128]{2,1,0:T(8,128)S(1)}, u32[]{:S(2)}, u32[]{:S(2)}) collective-permute-start(f32[16,32,128]{2,1,0:T(8,128)S(1)} %get-tuple-element.27), channel_id=1, source_target_pairs={{0,4},{4,0},{8,12},{12,8},{16,20},{20,16},{24,28},{28,24},{1,5},{5... | collective-permute-start | bytes 786440 | tf_op jit(solution)/shard_map/ppermute | solution.py:434
  36.6 9.8 %collective-permute-start.11 = (f32[8,88,128]{2,1,0:T(8,128)S(1)}, f32[8,88,128]{2,1,0:T(8,128)S(1)}, u32[]{:S(2)}, u32[]{:S(2)}) collective-permute-start(f32[8,88,128]{2,1,0:T(8,128)S(1)} %get-tuple-element.35), channel_id=1, source_target_pairs={{0,16},{4,20},{8,24},{12,28},{16,0},{20,4},{24,8},{28,12},{1,17},{... | collective-permute-start | bytes 1081352 | tf_op jit(solution)/shard_map/ppermute | solution.py:434
  37.9 8.5 %collective-permute-start.10 = (f32[8,80,128]{2,1,0:T(8,128)S(1)}, f32[8,80,128]{2,1,0:T(8,128)S(1)}, u32[]{:S(2)}, u32[]{:S(2)}) collective-permute-start(f32[8,80,128]{2,1,0:T(8,128)S(1)} %get-tuple-element.34), channel_id=1, source_target_pairs={{0,8},{4,12},{8,0},{12,4},{16,24},{20,28},{24,16},{28,20},{1,9},{5... | collective-permute-start | bytes 983048 | tf_op jit(solution)/shard_map/ppermute | solution.py:434
  38.2 12.6 %collective-permute-start.3 = (f32[8,64,128]{2,1,0:T(8,128)S(1)}, f32[8,64,128]{2,1,0:T(8,128)S(1)}, u32[]{:S(2)}, u32[]{:S(2)}) collective-permute-start(f32[8,64,128]{2,1,0:T(8,128)S(1)} %get-tuple-element.28.low_ref.refs_0_), channel_id=1, source_target_pairs={{0,16},{4,20},{8,24},{12,28},{16,0},{20,4},{24,8},{28,12},{1,17},{... | collective-permute-start | bytes 786440 | tf_op jit(solution)/shard_map/ppermute | solution.py:434
  38.4 13.6 %collective-permute-start.4 = (f32[8,64,128]{2,1,0:T(8,128)S(1)}, f32[8,64,128]{2,1,0:T(8,128)S(1)}, u32[]{:S(2)}, u32[]{:S(2)}) collective-permute-start(f32[8,64,128]{2,1,0:T(8,128)S(1)} %get-tuple-element.29.high_ref.refs_1_), channel_id=1, source_target_pairs={{0,8},{4,12},{8,0},{12,4},{16,24},{20,28},{24,16},{28,20},{1,9},{5... | collective-permute-start | bytes 786440 | tf_op jit(solution)/shard_map/ppermute | solution.py:434
  47.4 6.8 %collective-permute-start.14 = (f32[16,2,32,128]{3,2,1,0:T(8,128)S(1)}, f32[16,2,32,128]{3,2,1,0:T(8,128)S(1)}, u32[]{:S(2)}, u32[]{:S(2)}) collective-permute-start(f32[16,2,32,128]{3,2,1,0:T(8,128)S(1)} %get-tuple-element.42), channel_id=1, source_target_pairs={{0,4},{4,0},{8,12},{12,8},{16,20},{20,16},{24,28},{28,24},{1,5},{5... | collective-permute-start | bytes 1572872 | tf_op jit(solution)/shard_map/ppermute | solution.py:434
  52.8 8.3 %collective-permute-start.13 = (f32[8,88,128]{2,1,0:T(8,128)S(1)}, f32[8,88,128]{2,1,0:T(8,128)S(1)}, u32[]{:S(2)}, u32[]{:S(2)}) collective-permute-start(f32[8,88,128]{2,1,0:T(8,128)S(1)} %get-tuple-element.40), channel_id=1, source_target_pairs={{0,16},{4,20},{8,24},{12,28},{16,0},{20,4},{24,8},{28,12},{1,17},{... | collective-permute-start | bytes 1081352 | tf_op jit(solution)/shard_map/ppermute | solution.py:434
  53.9 7.6 %collective-permute-start.12 = (f32[8,80,128]{2,1,0:T(8,128)S(1)}, f32[8,80,128]{2,1,0:T(8,128)S(1)}, u32[]{:S(2)}, u32[]{:S(2)}) collective-permute-start(f32[8,80,128]{2,1,0:T(8,128)S(1)} %get-tuple-element.39), channel_id=1, source_target_pairs={{0,8},{4,12},{8,0},{12,4},{16,24},{20,28},{24,16},{28,20},{1,9},{5... | collective-permute-start | bytes 983048 | tf_op jit(solution)/shard_map/ppermute | solution.py:434
  62.5 4.1 %collective-permute-start.15 = (f32[16,2,32,128]{3,2,1,0:T(8,128)S(1)}, f32[16,2,32,128]{3,2,1,0:T(8,128)S(1)}, u32[]{:S(2)}, u32[]{:S(2)}) collective-permute-start(f32[16,2,32,128]{3,2,1,0:T(8,128)S(1)} %get-tuple-element.45), channel_id=1, source_target_pairs={{0,4},{4,0},{8,12},{12,8},{16,20},{20,16},{24,28},{28,24},{1,5},{5... | collective-permute-start | bytes 1572872 | tf_op jit(solution)/shard_map/ppermute | solution.py:434
  (3 other events, 24.7 us)

commit v4 on v3

v4 whole, which is shorter than its diff:
```python
import functools
import math

import jax
import jax.numpy as jnp
import numpy as np
from jax import lax
from jax.experimental import pallas as pl
from jax.experimental.pallas import tpu as pltpu
from jax.sharding import PartitionSpec as P

KR = 256
OUTER, INNER = (0, 6), (6, 10)
LANES = 128
WINDOW = 3 * LANES
SLOTS = 88
VMEM = pl.BlockSpec(memory_space=pltpu.VMEM)
SMEM = pl.BlockSpec(memory_space=pltpu.SMEM)
ANY = pl.BlockSpec(memory_space=pl.ANY)
SHORT = pl.CostEstimate(flops=1, bytes_accessed=1, transcendentals=0)


def cycles(number):
    return pl.CostEstimate(flops=number << 19, bytes_accessed=1, transcendentals=0)


def call(body, outs, scratch, args, cost=SHORT, after=(), specs=None, limit=48, out=VMEM, aliases={}):
    if specs is None:
        specs = [SMEM if a.dtype == jnp.int32 else VMEM for a in args]
    taken = len(args)

    def kernel(*refs):
        body(*refs[:taken], *refs[taken + len(after) :])

    return pl.pallas_call(
        kernel,
        out_shape=outs,
        in_specs=[*specs, *[ANY] * len(after)],
        out_specs=[out] * len(outs),
        scratch_shapes=scratch,
        input_output_aliases=aliases,
        compiler_params=pltpu.CompilerParams(vmem_limit_bytes=limit << 20),
        cost_estimate=cost,
    )(*args, *after)


def f32(*shape):
    return jax.ShapeDtypeStruct(shape, jnp.float32)


def position():
    index = lax.axis_index("ang")
    return index // 2 % 2, index % 2


def tile_of(index, group, tiles, core):
    first, half = group
    return index + jnp.where(core == 0, first, tiles - first - half)


def split(x):
    high = x.astype(jnp.bfloat16)
    low = (x - high.astype(jnp.float32)).astype(jnp.bfloat16)
    return high, low


def dot(a, b):
    return jnp.dot(a, b, preferred_element_type=jnp.float32)


def paired(step, count):
    def pair(index, carry):
        step(2 * index, 0)
        step(2 * index + 1, 1)
        return carry

    lax.fori_loop(0, count // 2, pair, 0)
    if count % 2:
        step(count - 1, 0)


def resample_body(group, whole, apart, start_any, weights_any, *refs):
    number = 2 if whole else 1
    slabs_any, *rest = refs[:number], *refs[number:]
    done_ref = None if whole or len(rest) == 6 else rest.pop(0)
    out_ref, start_ref, weights_ref, sino_ref, sems, stack = rest
    tiles = weights_any.shape[0]
    band = weights_any.shape[1]
    views, rows, cols = slabs_any[0].shape
    height = views * rows
    _, core = position()
    mine = pl.multiple_of(core * height, 8)
    other = pl.multiple_of((1 - core) * height, 8)
    first = tile_of(0, group, tiles, core)
    copies = [
        pltpu.make_async_copy(start_any, start_ref, sems.at[0]),
        pltpu.make_async_copy(weights_any.at[pl.ds(first, group[1])], weights_ref, sems.at[1]),
    ]
    for i, slab_any in enumerate(slabs_any):
        copies.append(pltpu.make_async_copy(slab_any, sino_ref.at[i], sems.at[2 + i]))
    for copy in copies:
        copy.start()
    for copy in copies:
        copy.wait()

    def step(index, slot):
        start = start_ref[first + index]
        base = jnp.minimum(start // LANES * LANES, cols - WINDOW)
        shift = start - base
        columns = pl.ds(pl.multiple_of(base, LANES), WINDOW)
        slab = sino_ref[:, :, :, columns].reshape(number * height, WINDOW)
        slab = pltpu.roll(slab, WINDOW - shift, 1)[:, :band]
        high, low = split(slab)
        weights = weights_ref[index]
        total = dot(high, weights) + dot(low, weights)
        if whole:
            target = stack.at[slot] if apart else out_ref.at[index]
            target[pl.ds(mine, height)] = total[:height]
            target[pl.ds(other, height)] = total[height:]
            if apart:
                for row in range(rows):
                    out_ref[index, row] = stack[slot, pl.ds(row, 2 * views, stride=rows), :]
        elif done_ref is None:
            out_ref[index] = total
        else:
            out_ref[index, pl.ds(mine, height)] = done_ref[index]
            out_ref[index, pl.ds(other, height)] = total

    paired(step, group[1])


def resample(group, start, weights, slabs, done=(), apart=False, after=()):
    views, rows, _ = slabs[0].shape
    whole = len(slabs) == 2
    height = views * rows * (2 if whole or done else 1)
    return call(
        functools.partial(resample_body, group, whole, apart),
        [f32(group[1], rows, 2 * views, LANES) if apart else f32(group[1], height, LANES)],
        [
            pltpu.SMEM(start.shape, jnp.int32),
            pltpu.VMEM((group[1], *weights.shape[1:]), weights.dtype),
            pltpu.VMEM((len(slabs), *slabs[0].shape), jnp.float32),
            pltpu.SemaphoreType.DMA((4,)),
            pltpu.VMEM((2, 2 * views * rows + 8, LANES), jnp.float32),
        ],
        (start, weights, *slabs, *done),
        cost=cycles(4000) if apart else SHORT,
        after=after,
        specs=[ANY] * (2 + len(slabs)) + [VMEM] * len(done),
        limit=48 if whole or done else 60,
    )[0]


def rows_body(group, tiles, offset_ref, even_ref, odd_ref, own_ref, weights_ref, out_ref, stack):
    count, height, _ = own_ref.shape
    views = height // 2
    _, core = position()
    after = lax.axis_index("row") % 2 == 0
    even_at = pl.multiple_of(jnp.where(after, 2 * height, 0), 8)
    odd_at = pl.multiple_of(jnp.where(after, 0, 2 * height), 8)

    def step(index, slot):
        tile = tile_of(index, group, tiles, core)
        offset = offset_ref[tile]
        stack[slot, pl.ds(even_at, height)] = even_ref[index]
        stack[slot, pl.ds(odd_at, height)] = odd_ref[index]
        stack[slot, height : 2 * height] = own_ref[index]
        weights = weights_ref[:, pl.ds(pl.multiple_of(tile * LANES, LANES), LANES)]

        def picked(row):
            lifted = row + 2
            first = lifted // 2 * height + lifted % 2
            return stack[slot, pl.ds(first, views, stride=2), :]

        terms = [picked(row + offset) for row in range(3)]
        for row in range(2):
            out_ref[index, row] = weights[0:1] * terms[row] + weights[1:2] * terms[row + 1]

    paired(step, count)


def interpolate_rows(group, tiles, offset, even, odd, own, weights, after):
    count, height, _ = own.shape
    return call(
        functools.partial(rows_body, group, tiles),
        [f32(count, 2, height // 2, LANES)],
        [pltpu.VMEM((2, 3 * height + 8, LANES), jnp.float32)],
        (offset, even, odd, own, weights),
        after=after,
    )[0]


def last_rows_body(group, tiles, offset_ref, even_ref, odd_ref, own_ref, weights_ref, keep_ref, send_ref, stack):
    count, parts, rows, chip_views, _ = own_ref.shape
    views = chip_views // 2
    _, core = position()
    after = lax.axis_index("row") % 2 == 0
    even_at = jnp.where(after, 2 * rows, 0)
    odd_at = jnp.where(after, 0, 2 * rows)
    mine = pl.multiple_of(core * views, 8)
    other = pl.multiple_of((1 - core) * views, 8)

    def step(index, slot):
        tile = tile_of(index, group, tiles, core)
        first = offset_ref[tile] + rows
        weights = weights_ref[:, pl.ds(pl.multiple_of(tile * LANES, LANES), LANES)]
        for part in range(parts):
            for row in range(rows):
                stack[slot, even_at + row] = even_ref[index, part, row]
                stack[slot, odd_at + row] = odd_ref[index, part, row]
                stack[slot, rows + row] = own_ref[index, part, row]
            for out_ref, begin in ((keep_ref, mine), (send_ref, other)):
                terms = [stack[slot, first + i, pl.ds(begin, views)] for i in range(rows + 1)]
                for row in range(rows):
                    out_ref[index, part, row] = weights[0:1] * terms[row] + weights[1:2] * terms[row + 1]

    paired(step, count)


def interpolate_rows_last(group, tiles, offset, even, odd, own, weights):
    count, parts, rows, chip_views, _ = own.shape
    return call(
        functools.partial(last_rows_body, group, tiles),
        [f32(count, parts, rows, chip_views // 2, LANES)] * 2,
        [pltpu.VMEM((2, 3 * rows, chip_views, LANES), jnp.float32)],
        (offset, even, odd, own, weights),
        cycles(4000),
    )


def select_body(group, tiles, view_ref, conj_ref, own_ref, got_ref, out_ref, stack):
    count, rows, chip_views, lanes = own_ref.shape
    side, core = position()

    def shifts(index):
        tile = tile_of(index, group, tiles, core)
        shift = view_ref[tile]
        return shift, shift + conj_ref[tiles - 1 - tile]

    def slots(low, high):
        return low + lax.broadcasted_iota(jnp.int32, (high - low, lanes), 0)

    def across_x(index, slot):
        shift, opposite = shifts(index)
        own_at = pl.multiple_of((1 - side) * chip_views, 8)
        got_at = pl.multiple_of(side * chip_views, 8)
        for row in range(rows):
            out = out_ref.at[index, row]
            both = stack.at[slot, row]
            both[pl.ds(own_at, chip_views)] = own_ref[index, row]
            both[pl.ds(got_at, chip_views)] = got_ref[index, row]
            out[0:32] = jnp.where(slots(0, 32) >= shift + 32, both[96:128], both[0:32])
            out[32:80] = jnp.where(slots(0, 48) >= opposite + 48, both[16:64], both[64:112])
            out[80:88] = jnp.zeros((8, lanes), jnp.float32)

    def across_y_first(index, slot):
        shift, opposite = shifts(index)
        for row in range(rows):
            out = out_ref.at[index, row]
            both = stack.at[slot, row]
            both[0:64] = own_ref[index, row]
            both[64:128] = got_ref[index, row]
            out[0:40] = jnp.where(slots(0, 40) >= opposite, both[0:40], both[72:112])
            out[40:56] = both[40:56]
            out[56:72] = jnp.where(slots(56, 72) >= 88 + shift, both[96:112], both[56:72])
            out[72:88] = both[112:128]

    def across_y_last(index, slot):
        shift, opposite = shifts(index)
        for row in range(rows):
            out = out_ref.at[index, row]
            both = stack.at[slot, row]
            both[0:64] = got_ref[index, row]
            both[64:128] = own_ref[index, row]
            out[0:16] = both[0:16]
            out[16:32] = jnp.where(slots(16, 32) < shift + 3, both[16:32], both[56:72])
            out[32:48] = both[72:88]
            out[48:88] = jnp.where(slots(48, 88) < 91 + opposite, both[88:128], both[16:56])

    pl.when(core == 0)(lambda: paired(across_x, count))
    pl.when((core == 1) & (side == 0))(lambda: paired(across_y_first, count))
    pl.when((core == 1) & (side == 1))(lambda: paired(across_y_last, count))


def select_views(group, tiles, view_offset, conj_offset, own, got, after=()):
    count, rows, chip_views, _ = own.shape
    return call(
        functools.partial(select_body, group, tiles),
        [f32(count, rows, SLOTS, LANES)],
        [pltpu.VMEM((2, rows, 2 * chip_views, LANES), jnp.float32)],
        (view_offset, conj_offset, own, got),
        after=after,
    )[0]


def views_body(group, tiles, exchanged, view_ref, conj_ref, weights_ref, *refs):
    *blocks, stack = refs
    outs = blocks[3 if exchanged else 6 :]
    blocks = blocks[: 3 if exchanged else 6]
    count, _, rows, views, _ = outs[0].shape
    side, core = position()
    firsts = (core, 1 - core) if len(outs) == 2 else (0,)
    taps = weights_ref.shape[0]

    def interpolate(index, slot, row):
        tile = tile_of(index, group, tiles, core)
        weights = weights_ref[:, pl.ds(pl.multiple_of(tile * LANES, LANES), LANES)]
        shift = view_ref[tile]
        opposite = shift + conj_ref[tiles - 1 - tile]
        for part, by in ((0, 32 + shift), (1, 176 + opposite)):
            for out_ref, first in zip(outs, firsts):
                begin = by + first * views
                total = weights[0:1] * stack[slot, row, pl.ds(begin, views)]
                for tap in range(1, taps):
                    total = total + weights[tap : tap + 1] * stack[slot, row, pl.ds(begin + tap, views)]
                out_ref[index, part, row] = total

    def run(parts):
        def step(index, slot):
            for row in range(rows):
                at = 0
                for part in parts(*(ref.at[index, row] for ref in blocks)):
                    stack[slot, row, at : at + part.shape[0]] = part[...]
                    at += part.shape[0]
                interpolate(index, slot, row)

        paired(step, count)

    def from_neighbours(before, own, after, early, middle, late):
        return before, own, after, early, middle, late

    def from_x(own, beyond, got):
        near, far = got.at[0:32], got.at[32:80]
        return near, own, near, far, beyond, far

    def from_y_first(own, beside, got):
        return got.at[56:88], own, beside.at[0:32], beside.at[16:64], got.at[0:72], got.at[0:40]

    def from_y_last(own, beside, got):
        return beside.at[32:64], own, got.at[0:32], got.at[48:88], got.at[16:88], beside.at[0:48]

    if exchanged:
        pl.when(core == 0)(lambda: run(from_x))
        pl.when((core == 1) & (side == 0))(lambda: run(from_y_first))
        pl.when((core == 1) & (side == 1))(lambda: run(from_y_last))
    else:
        run(from_neighbours)


def interpolate_views(group, tiles, exchanged, view_offset, conj_offset, weights, blocks, pieces, cost=SHORT, after=()):
    count, rows, chip_views, _ = blocks[0 if exchanged else 1].shape
    return call(
        functools.partial(views_body, group, tiles, exchanged),
        [f32(count, 2, rows, chip_views // pieces, LANES)] * pieces,
        [pltpu.VMEM((2, rows, 288, LANES), jnp.float32)],
        (view_offset, conj_offset, weights, *blocks),
        cost,
        after,
    )


def ramp(lag):
    lag = lag.astype(np.float64)
    odd = np.abs(lag) % 2 == 1
    values = np.where(lag == 0, 0.25, np.where(odd, -1.0 / (math.pi**2 * np.maximum(lag * lag, 1.0)), 0.0))
    return np.where(np.abs(lag) <= KR, values, 0.0).astype(np.float32)


def filter_matrix():
    column = np.arange(WINDOW)[:, None]
    place = np.arange(2 * LANES)[None, :]
    lag = place - 2 * (column - LANES)
    whole = np.concatenate([ramp(lag), ramp(lag - 1)[::-1]], axis=0)
    high = whole.astype(jnp.bfloat16)
    low = (whole - high.astype(np.float32)).astype(jnp.bfloat16)
    return jnp.asarray(high), jnp.asarray(low)


def stage_spans(groups, number, tiles):
    first, half = groups[number]
    begin = first - 1 if number else 0
    if number == len(groups) - 1:
        ranges = [(begin, tiles - begin)]
    else:
        ranges = [(begin, first + half - 1), (tiles - first - half + 1, tiles - begin)]
    spans = []
    for low, high in ranges:
        while low < high:
            count = min(4, high - low)
            spans.append((low, count))
            low += count
    return spans


def filter_body(groups, number, tiles, high_ref, low_ref, *refs):
    parts = refs[: 4 if number else 2]
    out_any, mixed, high_all, low_all, result, sems = refs[-6:]
    views = out_any.shape[0]
    _, core = position()
    if number == 0:
        for ref in (high_all, low_all):
            for part in range(2):
                ref[part, 0] = jnp.zeros(ref.shape[2:], ref.dtype)
                ref[part, tiles + 1] = jnp.zeros(ref.shape[2:], ref.dtype)

    def gather(group, ref, owner, index, slot):
        tile = tile_of(index, group, tiles, owner)
        for part in range(2):
            for row in range(2):
                mixed[slot, part, pl.ds(row, views, stride=2), :] = ref[index, part, row]
            high, low = split(mixed[slot, part, 0 : 2 * views])
            high_all[part, tile + 1] = high
            low_all[part, tile + 1] = low

    for ref, owner in zip(parts[:2], (core, 1 - core)):
        paired(functools.partial(gather, groups[number], ref, owner), groups[number][1])
    if number:
        half = groups[number - 1][1]
        for ref, owner in zip(parts[2:], (core, 1 - core)):
            begin = jnp.where(owner == 0, half - 2, 0)
            for i in range(2):
                gather(groups[number - 1], ref, owner, begin + i, i)

    copies = []
    for place, (first, count) in enumerate(stage_spans(groups, number, tiles)):

        def window(ref):
            pieces = []
            for section in range(3):
                piece = ref[0, first + section : first + section + count]
                pieces.append(piece.reshape(count * 2 * views, LANES))
            for section in range(3):
                last = tiles - 1 - first + section
                piece = jnp.stack([ref[1, last - i] for i in range(count)])
                pieces.append(piece.reshape(count * 2 * views, LANES))
            return jnp.concatenate(pieces, axis=1)

        high, low = window(high_all), window(low_all)
        total = dot(high, high_ref[...]) + dot(low, high_ref[...]) + dot(high, low_ref[...])
        for i in range(count):
            block = total[2 * views * i : 2 * views * (i + 1)].reshape(views, 2, 2 * LANES)
            result[:, :, (first + i) * 2 * LANES : (first + i + 1) * 2 * LANES] = block
        columns = pl.ds(first * 2 * LANES, count * 2 * LANES)
        copy = pltpu.make_async_copy(
            result.at[:, :, columns], out_any.at[:, :, columns], sems.at[place]
        )
        copy.start()
        copies.append(copy)
    for copy in copies:
        copy.wait()


def ramp_filter(groups, number, tiles, keeps, gots, out):
    views = keeps[0].shape[3]
    args = [*filter_matrix(), keeps[number], gots[number]]
    if number:
        args += [keeps[number - 1], gots[number - 1], out]
    stored = pltpu.VMEM((2, tiles + 2, 2 * views, LANES), jnp.bfloat16)
    shape = f32(views, 2, 2 * tiles * LANES)
    return call(
        functools.partial(filter_body, groups, number, tiles),
        [shape],
        [
            pltpu.VMEM((2, 2, 2 * views + 8, LANES), jnp.float32),
            stored,
            stored,
            pltpu.VMEM(shape.shape, jnp.float32),
            pltpu.SemaphoreType.DMA((len(stage_spans(groups, number, tiles)),)),
        ],
        args,
        specs=[VMEM] * 6 + [ANY] if number else [VMEM] * 4,
        out=ANY,
        aliases={6: 0} if number else {},
        cost=SHORT if number else cycles(6000),
    )[0]


def permuted(value, axis, target):
    count = lax.axis_size(axis)
    pairs = [(i, target(i)) for i in range(count)]
    return lax.ppermute(value, axis, [(i, j) for i, j in pairs if 0 <= j < count])


def swapped(value):
    return permuted(value, "ang", lambda i: i ^ 1)


def row_pairs(own):
    even = permuted(own, "row", lambda i: i ^ 1)
    odd = permuted(own, "row", lambda i: ((i + 1) ^ 1) - 1)
    return even, odd


def first_exchange(own):
    if lax.axis_size("ang") == 8:
        return [permuted(own, "ang", lambda i: i ^ (2 if i % 2 else 4))]
    return []


def second_exchange(own, first, chosen):
    devices = lax.axis_size("ang")
    if first:
        return [own, *first, permuted(chosen[0], "ang", lambda i: i ^ (4 if i % 2 else 2))]

    def ahead(begin, end, chips):
        return permuted(own[:, :, begin:end], "ang", lambda i: (i - 2 * chips) % devices)

    turned = devices // 4
    return [
        ahead(32, 64, -1),
        own,
        ahead(0, 32, 1),
        ahead(16, 64, turned - 1),
        ahead(0, 64, turned),
        ahead(0, 48, turned + 1),
    ]


def on_device(
    sinogram, col_weights, col_start, view_offset, row_offset, conj_offset, ang_weights, row_weights
):
    tiles = col_weights.shape[0]
    exchanged = lax.axis_size("ang") == 8
    offsets = (view_offset, conj_offset)
    groups = (OUTER, INNER)

    beside = swapped(sinogram)
    inner = resample(INNER, col_start, col_weights, (sinogram,))
    inner = resample(INNER, col_start, col_weights, (beside,), (inner,))
    inner_halo = row_pairs(inner)
    outer = resample(
        OUTER, col_start, col_weights, (sinogram, beside), apart=True, after=(inner,)
    )

    first = first_exchange(outer)
    chosen = [select_views(OUTER, tiles, *offsets, outer, got) for got in first]
    parts = second_exchange(outer, first, chosen)
    (outer,) = interpolate_views(
        OUTER, tiles, exchanged, *offsets, ang_weights, parts, 1, cycles(5000)
    )
    outer_halo = row_pairs(outer)

    inner = interpolate_rows(INNER, tiles, row_offset, *inner_halo, inner, row_weights, chosen)
    first = first_exchange(inner)
    chosen = [select_views(INNER, tiles, *offsets, inner, got, (outer,)) for got in first]
    parts = second_exchange(inner, first, chosen)

    outer_keep, send = interpolate_rows_last(
        OUTER, tiles, row_offset, *outer_halo, outer, row_weights
    )
    outer_got = swapped(send)
    out = ramp_filter(groups, 0, tiles, [outer_keep], [outer_got], None)
    inner_keep, send = interpolate_views(
        INNER, tiles, exchanged, *offsets, ang_weights, parts, 2
    )
    inner_got = swapped(send)
    return ramp_filter(
        groups, 1, tiles, (outer_keep, inner_keep), (outer_got, inner_got), out
    )


def solution(mesh):
    return jax.shard_map(
        on_device,
        mesh=mesh,
        in_specs=(P("ang", "row", None), P(), P(), P(), P(), P(), P(), P()),
        out_specs=P("ang", "row", None),
        check_vma=False,
    )
```

time: 69.8 us -> 60.8 us (0.87)
  starting transfers between devices: 27.9 us -> 14.2 us
  waiting for transfers between devices: 22.7 us -> 27.1 us
  Pallas kernels: 18.5 us -> 17.4 us
  local copies, waits for them, and re-layouts: 0.05 us -> 1.02 us
    ppermute x16 -> x11, starting transfers between devices: 27.9 us -> 14.2 us  [permuted(): lax.ppermute(value, axis, [(i, j) for i, j in pairs if 0 <= j < count])]
    ppermute x16 -> x11, waiting for transfers between devices: 22.7 us -> 27.1 us  [permuted(): lax.ppermute(value, axis, [(i, j) for i, j in pairs if 0 <= j < count])]
    pallas_call x12 -> x11, Pallas kernels: 18.5 us -> 17.4 us  [call(): pl.pallas_call(kernel, out_shape=outs, in_specs=[*specs, *[ANY] * len(aft...]
    unnamed x22, local copies, waits for them, and re-layouts: 0.05 us -> 1.02 us
  transfers between devices with their start and end apart: 16 -> 11, of which waited for: 11 -> 6; matrix products, arithmetic and copies ran while one was open for 0% -> 0% of each run, Pallas kernels for 14% -> 21%
where the time goes in v4:
time: 60.8 us; the launch traced here: 59.9 us
  waiting for transfers between devices  27.1 us (45%)
  Pallas kernels  17.4 us (29%)
  starting transfers between devices  14.2 us (23%)
  local copies, waits for them, and re-layouts  1.02 us (2%)
    ppermute x11, waiting for transfers between devices, permuted(): lax.ppermute(value, axis, [(i, j) for i, j in pairs if 0 <= j < count])  27.1 us
    pallas_call x11, Pallas kernels, call(): pl.pallas_call(kernel, out_shape=outs, in_specs=[*specs, *[ANY] * len(aft...  17.4 us
    ppermute x11, starting transfers between devices, permuted(): lax.ppermute(value, axis, [(i, j) for i, j in pairs if 0 <= j < count])  14.2 us
  transfers between devices with their start and end apart: 11, of which 6 were waited for; matrix products, arithmetic and copies ran while one was open for 0% of the time, Pallas kernels for 21%

profile of v4, /device:TPU:11, one launch (start us, length us, event | category | flops | bytes accessed | tf_op | source)
XLA Modules:
  0.0 59.9 jit_solution(13567506287184700559)
XLA Ops:
  0.0 0.7 %collective-permute-start = (f32[32,2,4096]{2,1,0:T(2,128)}, f32[32,2,4096]{2,1,0:T(2,128)S(1)}, u32[]{:S(2)}, u32[]{:S(2)}) collective-permute-start(f32[32,2,4096]{2,1,0:T(2,128)} %refs_2_.5), channel_id=1, source_target_pairs={{0,4},{4,0},{8,12},{12,8},{16,20},{20,16},{24,28},{28,24},{1,5},{5... | collective-permute-start | bytes 3145736 | tf_op jit(solution)/shard_map/ppermute | solution.py:481
  0.7 3.5 %shard_map.118.refs_3_ = f32[10,64,128]{2,1,0:T(8,128)} custom-call(s32[32]{0:T(128)} %refs_0_.13, bf16[32,256,128]{2,1,0:T(8,128)(2,1)} %refs_1_.11, f32[32,2,4096]{2,1,0:T(2,128)} %refs_2_.5), custom_call_target="tpu_custom_call" | custom-call | flops 1 | bytes 1 | tf_op jit(solution)/shard_map/pallas_call | solution.py:35
  4.3 1.0 %copy-done.1 = f32[10,64,128]{2,1,0:T(8,128)S(1)} copy-done((f32[10,64,128]{2,1,0:T(8,128)S(1)}, f32[10,64,128]{2,1,0:T(8,128)}, u32[]{:S(2)}) %copy-start.1) | copy-done | bytes 327704
  5.2 1.9 %shard_map.119.refs_4_.refs_3_ = f32[10,128,128]{2,1,0:T(8,128)S(1)} custom-call(s32[32]{0:T(128)S(1)} %copy-done.9, bf16[32,256,128]{2,1,0:T(8,128)(2,1)S(1)} %copy-done, f32[32,2,4096]{2,1,0:T(2,128)S(1)} %collective-permute-done.refs_2_.refs_3_, f32[10,64,128]{2,1,0:T(8,128)S(1)} %copy-done.1), custom_call_target="tpu_custom_call" | custom-call | flops 1 | bytes 1 | tf_op jit(solution)/shard_map/pallas_call | solution.py:35
  7.2 3.3 %collective-permute-start.2 = (f32[10,128,128]{2,1,0:T(8,128)S(1)}, f32[10,128,128]{2,1,0:T(8,128)S(1)}, u32[]{:S(2)}, u32[]{:S(2)}) collective-permute-start(f32[10,128,128]{2,1,0:T(8,128)S(1)} %shard_map.119.refs_4_.refs_3_), channel_id=1, source_target_pairs={{1,2},{2,1},{5,6},{6,5},{9,10},{10,9},{13,14},{14,13},{17,18},{18,... | collective-permute-start | bytes 1966088 | tf_op jit(solution)/shard_map/ppermute | solution.py:481
  10.7 1.6 %shard_map.120.refs_2_.refs_3_ = f32[6,2,64,128]{3,2,1,0:T(8,128)S(1)} custom-call(s32[32]{0:T(128)S(1)} %copy-done.9, bf16[32,256,128]{2,1,0:T(8,128)(2,1)S(1)} %copy-done, f32[32,2,4096]{2,1,0:T(2,128)S(1)} %copy-done.2, f32[32,2,4096]{2,1,0:T(2,128)S(1)} %collective-permute-done.refs_2_.refs_3_, f32[10,128,128]{2,1,0:T(8,128)S(1)} %shard_map.119.refs_4_.refs_3_), custom_call_target="tpu_custom_call" | custom-call | flops 2097152000 | bytes 1 | tf_op jit(solution)/shard_map/pallas_call | solution.py:35
  12.6 6.7 %collective-permute-done.3.refs_3_.refs_4_ = f32[6,2,64,128]{3,2,1,0:T(8,128)S(1)} collective-permute-done((f32[6,2,64,128]{3,2,1,0:T(8,128)S(1)}, f32[6,2,64,128]{3,2,1,0:T(8,128)S(1)}, u32[]{:S(2)}, u32[]{:S(2)}) %collective-permute-start.3) | collective-permute-done | bytes 393248 | tf_op jit(solution)/shard_map/ppermute | solution.py:481
  19.9 1.3 %collective-permute-start.5 = (f32[6,2,88,128]{3,2,1,0:T(8,128)S(1)}, f32[6,2,88,128]{3,2,1,0:T(8,128)S(1)}, u32[]{:S(2)}, u32[]{:S(2)}) collective-permute-start(f32[6,2,88,128]{3,2,1,0:T(8,128)S(1)} %shard_map.121.refs_5_), channel_id=1, source_target_pairs={{0,8},{4,20},{8,0},{12,28},{16,24},{20,4},{24,16},{28,12},{1,9},{5... | collective-permute-start | bytes 1622024 | tf_op jit(solution)/shard_map/ppermute | solution.py:481
  21.3 4.2 %collective-permute-done.2.refs_2_ = f32[10,128,128]{2,1,0:T(8,128)S(1)} collective-permute-done((f32[10,128,128]{2,1,0:T(8,128)S(1)}, f32[10,128,128]{2,1,0:T(8,128)S(1)}, u32[]{:S(2)}, u32[]{:S(2)}) %collective-permute-start.2) | collective-permute-done | bytes 655392 | tf_op jit(solution)/shard_map/ppermute | solution.py:481
  25.5 1.1 %collective-permute-done.1.refs_1_ = f32[10,128,128]{2,1,0:T(8,128)S(1)} collective-permute-done((f32[10,128,128]{2,1,0:T(8,128)S(1)}, f32[10,128,128]{2,1,0:T(8,128)S(1)}, u32[]{:S(2)}, u32[]{:S(2)}) %collective-permute-start.1) | collective-permute-done | bytes 655392 | tf_op jit(solution)/shard_map/ppermute | solution.py:481
  26.5 0.9 %shard_map.122.refs_2_.refs_3_ = f32[10,2,64,128]{3,2,1,0:T(8,128)S(1)} custom-call(s32[32]{0:T(128)S(1)} %copy-done.10, f32[10,128,128]{2,1,0:T(8,128)S(1)} %collective-permute-done.1.refs_1_, f32[10,128,128]{2,1,0:T(8,128)S(1)} %collective-permute-done.2.refs_2_, f32[10,128,128]{2,1,0:T(8,128)S(1)} %shard_map.119.refs_4_.refs_3_, f32[2,4096]{1,0:T(2,128)S(1)} %copy-done.6, ...), custom_call_target="tpu_custom_call" | custom-call | flops 1 | bytes 1 | tf_op jit(solution)/shard_map/pallas_call | solution.py:35
  27.7 0.8 %collective-permute-done.5.refs_5_ = f32[6,2,88,128]{3,2,1,0:T(8,128)S(1)} collective-permute-done((f32[6,2,88,128]{3,2,1,0:T(8,128)S(1)}, f32[6,2,88,128]{3,2,1,0:T(8,128)S(1)}, u32[]{:S(2)}, u32[]{:S(2)}) %collective-permute-start.5) | collective-permute-done | bytes 540704 | tf_op jit(solution)/shard_map/ppermute | solution.py:481
  28.5 0.9 %shard_map.123.refs_4_.refs_3_ = f32[6,2,2,64,128]{4,3,2,1,0:T(8,128)S(1)} custom-call(s32[32]{0:T(128)S(1)} %copy-done.7, s32[32]{0:T(128)S(1)} %copy-done.8, f32[4,4096]{1,0:T(4,128)S(1)} %copy-done.5, f32[6,2,64,128]{3,2,1,0:T(8,128)S(1)} %shard_map.120.refs_2_.refs_3_, f32[6,2,64,128]{3,2,1,0:T(8,128)S(1)} %collective-permute-done.3.refs_3_.refs_4_, ...), custom_call_target="tpu_custom_call" | custom-call | flops 2621440000 | bytes 1 | tf_op jit(solution)/shard_map/pallas_call | solution.py:35
  29.4 2.1 %collective-permute-start.9 = (f32[6,2,2,64,128]{4,3,2,1,0:T(8,128)S(1)}, f32[6,2,2,64,128]{4,3,2,1,0:T(8,128)S(1)}, u32[]{:S(2)}, u32[]{:S(2)}) collective-permute-start(f32[6,2,2,64,128]{4,3,2,1,0:T(8,128)S(1)} %shard_map.123.refs_4_.refs_3_), channel_id=1, source_target_pairs={{1,2},{2,1},{5,6},{6,5},{9,10},{10,9},{13,14},{14,13},{17,18},{18,... | collective-permute-start | bytes 2359304 | tf_op jit(solution)/shard_map/ppermute | solution.py:481
  31.7 5.7 %collective-permute-done.4.refs_3_.refs_4_ = f32[10,2,64,128]{3,2,1,0:T(8,128)S(1)} collective-permute-done((f32[10,2,64,128]{3,2,1,0:T(8,128)S(1)}, f32[10,2,64,128]{3,2,1,0:T(8,128)S(1)}, u32[]{:S(2)}, u32[]{:S(2)}) %collective-permute-start.4) | collective-permute-done | bytes 655392 | tf_op jit(solution)/shard_map/ppermute | solution.py:481
  37.4 0.7 %shard_map.124 = f32[10,2,88,128]{3,2,1,0:T(8,128)S(1)} custom-call(s32[32]{0:T(128)S(1)} %copy-done.7, s32[32]{0:T(128)S(1)} %copy-done.8, f32[10,2,64,128]{3,2,1,0:T(8,128)S(1)} %shard_map.122.refs_2_.refs_3_, f32[10,2,64,128]{3,2,1,0:T(8,128)S(1)} %collective-permute-done.4.refs_3_.refs_4_, f32[6,2,2,64,128]{4,3,2,1,0:T(8,128)S(1)} %shard_map.123.refs_4_.refs_3_), custom_call_target="tpu_custom_call" | custom-call | flops 1 | bytes 1 | tf_op jit(solution)/shard_map/pallas_call | solution.py:35
  38.1 1.3 %collective-permute-start.6 = (f32[10,2,88,128]{3,2,1,0:T(8,128)S(1)}, f32[10,2,88,128]{3,2,1,0:T(8,128)S(1)}, u32[]{:S(2)}, u32[]{:S(2)}) collective-permute-start(f32[10,2,88,128]{3,2,1,0:T(8,128)S(1)} %shard_map.124), channel_id=1, source_target_pairs={{0,8},{4,20},{8,0},{12,28},{16,24},{20,4},{24,16},{28,12},{1,9},{5... | collective-permute-start | bytes 2703368 | tf_op jit(solution)/shard_map/ppermute | solution.py:481
  39.4 8.6 %collective-permute-done.9.refs_2_ = f32[6,2,2,64,128]{4,3,2,1,0:T(8,128)S(1)} collective-permute-done((f32[6,2,2,64,128]{4,3,2,1,0:T(8,128)S(1)}, f32[6,2,2,64,128]{4,3,2,1,0:T(8,128)S(1)}, u32[]{:S(2)}, u32[]{:S(2)}) %collective-permute-start.9) | collective-permute-done | bytes 786464 | tf_op jit(solution)/shard_map/ppermute | solution.py:481
  48.0 0.9 %shard_map.126 = (f32[6,2,2,32,128]{4,3,2,1,0:T(8,128)S(1)}, f32[6,2,2,32,128]{4,3,2,1,0:T(8,128)S(1)}) custom-call(s32[32]{0:T(128)S(1)} %copy-done.10, f32[6,2,2,64,128]{4,3,2,1,0:T(8,128)S(1)} %collective-permute-done.8.refs_1_, f32[6,2,2,64,128]{4,3,2,1,0:T(8,128)S(1)} %collective-permute-done.9.refs_2_, ...), custom_call_target="tpu_custom_call" | custom-call | flops 2097152000 | bytes 1 | tf_op jit(solution)/shard_map/pallas_call | solution.py:35
  48.9 3.6 %collective-permute-start.10 = (f32[6,2,2,32,128]{4,3,2,1,0:T(8,128)S(1)}, f32[6,2,2,32,128]{4,3,2,1,0:T(8,128)S(1)}, u32[]{:S(2)}, u32[]{:S(2)}) collective-permute-start(f32[6,2,2,32,128]{4,3,2,1,0:T(8,128)S(1)} %get-tuple-element.12), channel_id=1, source_target_pairs={{0,4},{4,0},{8,12},{12,8},{16,20},{20,16},{24,28},{28,24},{1,5},{5... | collective-permute-start | bytes 1179656 | tf_op jit(solution)/shard_map/ppermute | solution.py:481
  52.5 1.1 %shard_map.125 = (f32[10,2,2,32,128]{4,3,2,1,0:T(8,128)S(1)}, f32[10,2,2,32,128]{4,3,2,1,0:T(8,128)S(1)}) custom-call(s32[32]{0:T(128)S(1)} %copy-done.7, s32[32]{0:T(128)S(1)} %copy-done.8, f32[4,4096]{1,0:T(4,128)S(1)} %copy-done.5, f32[10,2,64,128]{3,2,1,0:T(8,128)S(1)} %shard_map.122.refs_2_.refs_3_, ...), custom_call_target="tpu_custom_call" | custom-call | flops 1 | bytes 1 | tf_op jit(solution)/shard_map/pallas_call | solution.py:35
  53.7 1.0 %collective-permute-start.7 = (f32[10,2,2,32,128]{4,3,2,1,0:T(8,128)S(1)}, f32[10,2,2,32,128]{4,3,2,1,0:T(8,128)S(1)}, u32[]{:S(2)}, u32[]{:S(2)}) collective-permute-start(f32[10,2,2,32,128]{4,3,2,1,0:T(8,128)S(1)} %get-tuple-element.10), channel_id=1, source_target_pairs={{0,4},{4,0},{8,12},{12,8},{16,20},{20,16},{24,28},{28,24},{1,5},{5... | collective-permute-start | bytes 1966088 | tf_op jit(solution)/shard_map/ppermute | solution.py:481
  54.7 2.1 %shard_map.127.refs_6_ = f32[32,2,8192]{2,1,0:T(2,128)} custom-call(bf16[768,256]{1,0:T(8,128)(2,1)S(1)} %copy-done.4, bf16[768,256]{1,0:T(8,128)(2,1)S(1)} %copy-done.3, f32[6,2,2,32,128]{4,3,2,1,0:T(8,128)S(1)} %get-tuple-element.11.refs_2_.refs_4_, f32[6,2,2,32,128]{4,3,2,1,0:T(8,128)S(1)} %collective-permute-done.10.refs_3_.refs_5_), custom_call_target="tpu_custom_call" | custom-call | flops 3145728000 | bytes 1 | tf_op jit(solution)/shard_map/pallas_call | solution.py:35
  56.8 3.1 %shard_map.128 = f32[32,2,8192]{2,1,0:T(2,128)} custom-call(bf16[768,256]{1,0:T(8,128)(2,1)S(1)} %copy-done.4, bf16[768,256]{1,0:T(8,128)(2,1)S(1)} %copy-done.3, f32[10,2,2,32,128]{4,3,2,1,0:T(8,128)S(1)} %get-tuple-element.9.refs_2_, f32[10,2,2,32,128]{4,3,2,1,0:T(8,128)S(1)} %collective-permute-done.7.refs_3_, ...), custom_call_target="tpu_custom_call", output_to_operand_aliasing={{}: (6, {})} | custom-call | flops 1 | bytes 1 | tf_op jit(solution)/shard_map/pallas_call | solution.py:35
  (31 shorter events, 1.6 us)
Async XLA Ops:
  0.0 4.3 %copy-start.9 = (s32[32]{0:T(128)S(1)}, s32[32]{0:T(128)}, u32[]{:S(2)}) copy-start(s32[32]{0:T(128)} %refs_0_.13) | copy-start | bytes 388
  0.0 4.3 %copy-start = (bf16[32,256,128]{2,1,0:T(8,128)(2,1)S(1)}, bf16[32,256,128]{2,1,0:T(8,128)(2,1)}, u32[]{:S(2)}) copy-start(bf16[32,256,128]{2,1,0:T(8,128)(2,1)} %refs_1_.11) | copy-start | bytes 6291460
  0.0 4.2 %collective-permute-start = (f32[32,2,4096]{2,1,0:T(2,128)}, f32[32,2,4096]{2,1,0:T(2,128)S(1)}, u32[]{:S(2)}, u32[]{:S(2)}) collective-permute-start(f32[32,2,4096]{2,1,0:T(2,128)} %refs_2_.5), channel_id=1, source_target_pairs={{0,4},{4,0},{8,12},{12,8},{16,20},{20,16},{24,28},{28,24},{1,5},{5... | collective-permute-start | bytes 3145736 | tf_op jit(solution)/shard_map/ppermute | solution.py:481
  4.3 1.0 %copy-start.1 = (f32[10,64,128]{2,1,0:T(8,128)S(1)}, f32[10,64,128]{2,1,0:T(8,128)}, u32[]{:S(2)}) copy-start(f32[10,64,128]{2,1,0:T(8,128)} %shard_map.118.refs_3_) | copy-start | bytes 983044
  5.2 5.4 %copy-start.2 = (f32[32,2,4096]{2,1,0:T(2,128)S(1)}, f32[32,2,4096]{2,1,0:T(2,128)}, u32[]{:S(2)}) copy-start(f32[32,2,4096]{2,1,0:T(2,128)} %refs_2_.5) | copy-start | bytes 3145732
  7.2 12.1 %copy-start.7 = (s32[32]{0:T(128)S(1)}, s32[32]{0:T(128)}, u32[]{:S(2)}) copy-start(s32[32]{0:T(128)} %refs_0_.18) | copy-start | bytes 388
  7.2 12.1 %copy-start.8 = (s32[32]{0:T(128)S(1)}, s32[32]{0:T(128)}, u32[]{:S(2)}) copy-start(s32[32]{0:T(128)} %refs_1_.15) | copy-start | bytes 388
  7.2 19.3 %copy-start.6 = (f32[2,4096]{1,0:T(2,128)S(1)}, f32[2,4096]{1,0:T(2,128)}, u32[]{:S(2)}) copy-start(f32[2,4096]{1,0:T(2,128)} %refs_4_.3) | copy-start | bytes 98308
  7.2 19.3 %copy-start.10 = (s32[32]{0:T(128)S(1)}, s32[32]{0:T(128)}, u32[]{:S(2)}) copy-start(s32[32]{0:T(128)} %refs_0_.19) | copy-start | bytes 388
  7.2 18.2 %collective-permute-start.2 = (f32[10,128,128]{2,1,0:T(8,128)S(1)}, f32[10,128,128]{2,1,0:T(8,128)S(1)}, u32[]{:S(2)}, u32[]{:S(2)}) collective-permute-start(f32[10,128,128]{2,1,0:T(8,128)S(1)} %shard_map.119.refs_4_.refs_3_), channel_id=1, source_target_pairs={{1,2},{2,1},{5,6},{6,5},{9,10},{10,9},{13,14},{14,13},{17,18},{18,... | collective-permute-start | bytes 1966088 | tf_op jit(solution)/shard_map/ppermute | solution.py:481
  10.6 15.9 %collective-permute-start.1 = (f32[10,128,128]{2,1,0:T(8,128)S(1)}, f32[10,128,128]{2,1,0:T(8,128)S(1)}, u32[]{:S(2)}, u32[]{:S(2)}) collective-permute-start(f32[10,128,128]{2,1,0:T(8,128)S(1)} %shard_map.119.refs_4_.refs_3_), channel_id=1, source_target_pairs={{0,1},{1,0},{2,3},{3,2},{4,5},{5,4},{6,7},{7,6},{8,9},{9,8},{10,11... | collective-permute-start | bytes 1966088 | tf_op jit(solution)/shard_map/ppermute | solution.py:481
  12.3 16.2 %copy-start.5 = (f32[4,4096]{1,0:T(4,128)S(1)}, f32[4,4096]{1,0:T(4,128)}, u32[]{:S(2)}) copy-start(f32[4,4096]{1,0:T(4,128)} %refs_2_.7) | copy-start | bytes 196612
  12.3 7.0 %collective-permute-start.3 = (f32[6,2,64,128]{3,2,1,0:T(8,128)S(1)}, f32[6,2,64,128]{3,2,1,0:T(8,128)S(1)}, u32[]{:S(2)}, u32[]{:S(2)}) collective-permute-start(f32[6,2,64,128]{3,2,1,0:T(8,128)S(1)} %shard_map.120.refs_2_.refs_3_), channel_id=1, source_target_pairs={{0,16},{4,12},{8,24},{12,4},{16,0},{20,28},{24,8},{28,20},{1,17},{... | collective-permute-start | bytes 1179656 | tf_op jit(solution)/shard_map/ppermute | solution.py:481
  19.9 8.6 %collective-permute-start.5 = (f32[6,2,88,128]{3,2,1,0:T(8,128)S(1)}, f32[6,2,88,128]{3,2,1,0:T(8,128)S(1)}, u32[]{:S(2)}, u32[]{:S(2)}) collective-permute-start(f32[6,2,88,128]{3,2,1,0:T(8,128)S(1)} %shard_map.121.refs_5_), channel_id=1, source_target_pairs={{0,8},{4,20},{8,0},{12,28},{16,24},{20,4},{24,16},{28,12},{1,9},{5... | collective-permute-start | bytes 1622024 | tf_op jit(solution)/shard_map/ppermute | solution.py:481
  27.4 10.0 %collective-permute-start.4 = (f32[10,2,64,128]{3,2,1,0:T(8,128)S(1)}, f32[10,2,64,128]{3,2,1,0:T(8,128)S(1)}, u32[]{:S(2)}, u32[]{:S(2)}) collective-permute-start(f32[10,2,64,128]{3,2,1,0:T(8,128)S(1)} %shard_map.122.refs_2_.refs_3_), channel_id=1, source_target_pairs={{0,16},{4,12},{8,24},{12,4},{16,0},{20,28},{24,8},{28,20},{1,17},{... | collective-permute-start | bytes 1966088 | tf_op jit(solution)/shard_map/ppermute | solution.py:481
  29.4 18.5 %collective-permute-start.9 = (f32[6,2,2,64,128]{4,3,2,1,0:T(8,128)S(1)}, f32[6,2,2,64,128]{4,3,2,1,0:T(8,128)S(1)}, u32[]{:S(2)}, u32[]{:S(2)}) collective-permute-start(f32[6,2,2,64,128]{4,3,2,1,0:T(8,128)S(1)} %shard_map.123.refs_4_.refs_3_), channel_id=1, source_target_pairs={{1,2},{2,1},{5,6},{6,5},{9,10},{10,9},{13,14},{14,13},{17,18},{18,... | collective-permute-start | bytes 2359304 | tf_op jit(solution)/shard_map/ppermute | solution.py:481
  31.5 16.5 %collective-permute-start.8 = (f32[6,2,2,64,128]{4,3,2,1,0:T(8,128)S(1)}, f32[6,2,2,64,128]{4,3,2,1,0:T(8,128)S(1)}, u32[]{:S(2)}, u32[]{:S(2)}) collective-permute-start(f32[6,2,2,64,128]{4,3,2,1,0:T(8,128)S(1)} %shard_map.123.refs_4_.refs_3_), channel_id=1, source_target_pairs={{0,1},{1,0},{2,3},{3,2},{4,5},{5,4},{6,7},{7,6},{8,9},{9,8},{10,11... | collective-permute-start | bytes 2359304 | tf_op jit(solution)/shard_map/ppermute | solution.py:481
  38.1 14.4 %collective-permute-start.6 = (f32[10,2,88,128]{3,2,1,0:T(8,128)S(1)}, f32[10,2,88,128]{3,2,1,0:T(8,128)S(1)}, u32[]{:S(2)}, u32[]{:S(2)}) collective-permute-start(f32[10,2,88,128]{3,2,1,0:T(8,128)S(1)} %shard_map.124), channel_id=1, source_target_pairs={{0,8},{4,20},{8,0},{12,28},{16,24},{20,4},{24,16},{28,12},{1,9},{5... | collective-permute-start | bytes 2703368 | tf_op jit(solution)/shard_map/ppermute | solution.py:481
  48.9 5.8 %copy-start.3 = (bf16[768,256]{1,0:T(8,128)(2,1)S(1)}, bf16[768,256]{1,0:T(8,128)(2,1)}, u32[]{:S(2)}) copy-start(bf16[768,256]{1,0:T(8,128)(2,1)} %constant.5.clone.refs_1_) | copy-start | bytes 1179652
  48.9 5.8 %copy-start.4 = (bf16[768,256]{1,0:T(8,128)(2,1)S(1)}, bf16[768,256]{1,0:T(8,128)(2,1)}, u32[]{:S(2)}) copy-start(bf16[768,256]{1,0:T(8,128)(2,1)} %constant.4.clone.refs_0_) | copy-start | bytes 1179652
  48.9 5.8 %collective-permute-start.10 = (f32[6,2,2,32,128]{4,3,2,1,0:T(8,128)S(1)}, f32[6,2,2,32,128]{4,3,2,1,0:T(8,128)S(1)}, u32[]{:S(2)}, u32[]{:S(2)}) collective-permute-start(f32[6,2,2,32,128]{4,3,2,1,0:T(8,128)S(1)} %get-tuple-element.12), channel_id=1, source_target_pairs={{0,4},{4,0},{8,12},{12,8},{16,20},{20,16},{24,28},{28,24},{1,5},{5... | collective-permute-start | bytes 1179656 | tf_op jit(solution)/shard_map/ppermute | solution.py:481
  53.7 3.2 %collective-permute-start.7 = (f32[10,2,2,32,128]{4,3,2,1,0:T(8,128)S(1)}, f32[10,2,2,32,128]{4,3,2,1,0:T(8,128)S(1)}, u32[]{:S(2)}, u32[]{:S(2)}) collective-permute-start(f32[10,2,2,32,128]{4,3,2,1,0:T(8,128)S(1)} %get-tuple-element.10), channel_id=1, source_target_pairs={{0,4},{4,0},{8,12},{12,8},{16,20},{20,16},{24,28},{28,24},{1,5},{5... | collective-permute-start | bytes 1966088 | tf_op jit(solution)/shard_map/ppermute | solution.py:481

commit v5 on v4

--- a/solution.py
+++ b/solution.py
@@ -44,6 +44,10 @@
     )(*args, *after)
 
 
+def hbm(x):
+    return pltpu.with_memory_space_constraint(x, pltpu.HBM)
+
+
 def f32(*shape):
     return jax.ShapeDtypeStruct(shape, jnp.float32)
 
@@ -66,6 +70,16 @@
 
 def dot(a, b):
     return jnp.dot(a, b, preferred_element_type=jnp.float32)
+
+
+def dot_terms(high, low, b):
+    both = dot(jnp.concatenate([high, low], axis=0), b)
+    return both[: high.shape[0]] + both[high.shape[0] :]
+
+
+def unrolled(step, count):
+    for index in range(count):
+        step(index, index % 2)
 
 
 def paired(step, count):
@@ -79,75 +93,124 @@
         step(count - 1, 0)
 
 
-def resample_body(group, whole, apart, start_any, weights_any, *refs):
-    number = 2 if whole else 1
-    slabs_any, *rest = refs[:number], *refs[number:]
-    done_ref = None if whole or len(rest) == 6 else rest.pop(0)
-    out_ref, start_ref, weights_ref, sino_ref, sems, stack = rest
+def resampled_tile(slab_refs, start, weights):
+    cols = slab_refs[0].shape[2]
+    base = jnp.minimum(start // LANES * LANES, cols - WINDOW)
+    columns = pl.ds(pl.multiple_of(base, LANES), WINDOW)
+    slabs = [ref[:, :, columns].reshape(-1, WINDOW) for ref in slab_refs]
+    slab = jnp.concatenate(slabs, axis=0)
+    slab = pltpu.roll(slab, WINDOW - (start - base), 1)[:, : weights.shape[0]]
+    return dot_terms(*split(slab), weights)
+
+
+def resample_own_body(group, start_any, weights_any, sino_any, out_ref, weights_ref, sino_ref, start_ref, sems):
     tiles = weights_any.shape[0]
-    band = weights_any.shape[1]
-    views, rows, cols = slabs_any[0].shape
+    held = weights_ref.shape[0]
+    first, half = group
+    _, core = position()
+    place = jnp.where(core == 0, first, held - first - half)
+    origin = core * (tiles - held)
+    later = jnp.where(core == 0, 0, half)
+    needed = [
+        pltpu.make_async_copy(start_any, start_ref, sems.at[0]),
+        pltpu.make_async_copy(sino_any, sino_ref, sems.at[1]),
+        pltpu.make_async_copy(
+            weights_any.at[pl.ds(origin + place, half)], weights_ref.at[pl.ds(place, half)], sems.at[2]
+        ),
+    ]
+    rest = pltpu.make_async_copy(
+        weights_any.at[pl.ds(origin + later, held - half)],
+        weights_ref.at[pl.ds(later, held - half)],
+        sems.at[3],
+    )
+    for copy in (*needed, rest):
+        copy.start()
+    for copy in needed:
+        copy.wait()
+
+    def step(index, slot):
+        start = start_ref[origin + place + index]
+        out_ref[index] = resampled_tile([sino_ref], start, weights_ref[place + index])
+
+    unrolled(step, half)
+    rest.wait()
+
+
+def resample_own(group, start, weights, sino):
+    views, rows, _ = sino.shape
+    held = weights.shape[0] // 2
+    return call(
+        functools.partial(resample_own_body, group),
+        [
+            f32(group[1], views * rows, LANES),
+            jax.ShapeDtypeStruct((held, *weights.shape[1:]), weights.dtype),
+            f32(*sino.shape),
+        ],
+        [pltpu.SMEM(start.shape, jnp.int32), pltpu.SemaphoreType.DMA((4,))],
+        [hbm(x) for x in (start, weights, sino)],
+        specs=[ANY] * 3,
+    )
+
+
+def resample_rest_body(group, tiles, start_ref, weights_ref, got_ref, done_ref, out_ref):
+    held, (first, half) = weights_ref.shape[0], group
+    height = done_ref.shape[1]
+    _, core = position()
+    place = jnp.where(core == 0, first, held - first - half)
+    origin = core * (tiles - held)
+    mine = pl.multiple_of(core * height, 8)
+    other = pl.multiple_of((1 - core) * height, 8)
+
+    def step(index, slot):
+        start = start_ref[origin + place + index]
+        out_ref[index, pl.ds(mine, height)] = done_ref[index]
+        out_ref[index, pl.ds(other, height)] = resampled_tile(
+            [got_ref], start, weights_ref[place + index]
+        )
+
+    unrolled(step, half)
+
+
+def resample_rest(group, tiles, start, weights, got, done):
+    count, height, _ = done.shape
+    return call(
+        functools.partial(resample_rest_body, group, tiles),
+        [f32(count, 2 * height, LANES)],
+        [],
+        (start, weights, got, done),
+    )[0]
+
+
+def resample_apart_body(group, tiles, start_ref, weights_ref, sino_ref, got_ref, out_ref, stack):
+    held, (first, half) = weights_ref.shape[0], group
+    views, rows, _ = sino_ref.shape
     height = views * rows
     _, core = position()
+    place = jnp.where(core == 0, first, held - first - half)
+    origin = core * (tiles - held)
     mine = pl.multiple_of(core * height, 8)
     other = pl.multiple_of((1 - core) * height, 8)
-    first = tile_of(0, group, tiles, core)
-    copies = [
-        pltpu.make_async_copy(start_any, start_ref, sems.at[0]),
-        pltpu.make_async_copy(weights_any.at[pl.ds(first, group[1])], weights_ref, sems.at[1]),
-    ]
-    for i, slab_any in enumerate(slabs_any):
-        copies.append(pltpu.make_async_copy(slab_any, sino_ref.at[i], sems.at[2 + i]))
-    for copy in copies:
-        copy.start()
-    for copy in copies:
-        copy.wait()
 
     def step(index, slot):
-        start = start_ref[first + index]
-        base = jnp.minimum(start // LANES * LANES, cols - WINDOW)
-        shift = start - base
-        columns = pl.ds(pl.multiple_of(base, LANES), WINDOW)
-        slab = sino_ref[:, :, :, columns].reshape(number * height, WINDOW)
-        slab = pltpu.roll(slab, WINDOW - shift, 1)[:, :band]
-        high, low = split(slab)
-        weights = weights_ref[index]
-        total = dot(high, weights) + dot(low, weights)
-        if whole:
-            target = stack.at[slot] if apart else out_ref.at[index]
-            target[pl.ds(mine, height)] = total[:height]
-            target[pl.ds(other, height)] = total[height:]
-            if apart:
-                for row in range(rows):
-                    out_ref[index, row] = stack[slot, pl.ds(row, 2 * views, stride=rows), :]
-        elif done_ref is None:
-            out_ref[index] = total
-        else:
-            out_ref[index, pl.ds(mine, height)] = done_ref[index]
-            out_ref[index, pl.ds(other, height)] = total
-
-    paired(step, group[1])
-
-
-def resample(group, start, weights, slabs, done=(), apart=False, after=()):
-    views, rows, _ = slabs[0].shape
-    whole = len(slabs) == 2
-    height = views * rows * (2 if whole or done else 1)
-    return call(
-        functools.partial(resample_body, group, whole, apart),
-        [f32(group[1], rows, 2 * views, LANES) if apart else f32(group[1], height, LANES)],
-        [
-            pltpu.SMEM(start.shape, jnp.int32),
-            pltpu.VMEM((group[1], *weights.shape[1:]), weights.dtype),
-            pltpu.VMEM((len(slabs), *slabs[0].shape), jnp.float32),
-            pltpu.SemaphoreType.DMA((4,)),
-            pltpu.VMEM((2, 2 * views * rows + 8, LANES), jnp.float32),
-        ],
-        (start, weights, *slabs, *done),
-        cost=cycles(4000) if apart else SHORT,
-        after=after,
-        specs=[ANY] * (2 + len(slabs)) + [VMEM] * len(done),
-        limit=48 if whole or done else 60,
+        start = start_ref[origin + place + index]
+        total = resampled_tile([sino_ref, got_ref], start, weights_ref[place + index])
+        stack[slot, pl.ds(mine, height)] = total[:height]
+        stack[slot, pl.ds(other, height)] = total[height:]
+        for row in range(rows):
+            out_ref[index, row] = stack[slot, pl.ds(row, 2 * views, stride=rows), :]
+
+    unrolled(step, half)
+
+
+def resample_apart(group, tiles, start, weights, sino, got, after):
+    views, rows, _ = sino.shape
+    return call(
+        functools.partial(resample_apart_body, group, tiles),
+        [f32(group[1], rows, 2 * views, LANES)],
+        [pltpu.VMEM((2, 2 * views * rows + 8, LANES), jnp.float32)],
+        (start, weights, sino, got),
+        cycles(4000),
+        after,
     )[0]
 
 
@@ -176,7 +239,7 @@
         for row in range(2):
             out_ref[index, row] = weights[0:1] * terms[row] + weights[1:2] * terms[row + 1]
 
-    paired(step, count)
+    unrolled(step, count)
 
 
 def interpolate_rows(group, tiles, offset, even, odd, own, weights, after):
@@ -214,7 +277,7 @@
                 for row in range(rows):
                     out_ref[index, part, row] = weights[0:1] * terms[row] + weights[1:2] * terms[row + 1]
 
-    paired(step, count)
+    unrolled(step, count)
 
 
 def interpolate_rows_last(group, tiles, offset, even, odd, own, weights):
@@ -277,9 +340,9 @@
             out[32:48] = both[72:88]
             out[48:88] = jnp.where(slots(48, 88) < 91 + opposite, both[88:128], both[16:56])
 
-    pl.when(core == 0)(lambda: paired(across_x, count))
-    pl.when((core == 1) & (side == 0))(lambda: paired(across_y_first, count))
-    pl.when((core == 1) & (side == 1))(lambda: paired(across_y_last, count))
+    pl.when(core == 0)(lambda: unrolled(across_x, count))
+    pl.when((core == 1) & (side == 0))(lambda: unrolled(across_y_first, count))
+    pl.when((core == 1) & (side == 1))(lambda: unrolled(across_y_last, count))
 
 
 def select_views(group, tiles, view_offset, conj_offset, own, got, after=()):
@@ -324,7 +387,7 @@
                     at += part.shape[0]
                 interpolate(index, slot, row)
 
-        paired(step, count)
+        unrolled(step, count)
 
     def from_neighbours(before, own, after, early, middle, late):
         return before, own, after, early, middle, late
@@ -413,7 +476,7 @@
             low_all[part, tile + 1] = low
 
     for ref, owner in zip(parts[:2], (core, 1 - core)):
-        paired(functools.partial(gather, groups[number], ref, owner), groups[number][1])
+        unrolled(functools.partial(gather, groups[number], ref, owner), groups[number][1])
     if number:
         half = groups[number - 1][1]
         for ref, owner in zip(parts[2:], (core, 1 - core)):
@@ -436,7 +499,7 @@
             return jnp.concatenate(pieces, axis=1)
 
         high, low = window(high_all), window(low_all)
-        total = dot(high, high_ref[...]) + dot(low, high_ref[...]) + dot(high, low_ref[...])
+        total = dot_terms(high, low, high_ref[...]) + dot(high, low_ref[...])
         for i in range(count):
             block = total[2 * views * i : 2 * views * (i + 1)].reshape(views, 2, 2 * LANES)
             result[:, :, (first + i) * 2 * LANES : (first + i + 1) * 2 * LANES] = block
@@ -525,12 +588,10 @@
     groups = (OUTER, INNER)
 
     beside = swapped(sinogram)
-    inner = resample(INNER, col_start, col_weights, (sinogram,))
-    inner = resample(INNER, col_start, col_weights, (beside,), (inner,))
+    inner, weights, sino = resample_own(INNER, col_start, col_weights, sinogram)
+    inner = resample_rest(INNER, tiles, col_start, weights, beside, inner)
     inner_halo = row_pairs(inner)
-    outer = resample(
-        OUTER, col_start, col_weights, (sinogram, beside), apart=True, after=(inner,)
-    )
+    outer = resample_apart(OUTER, tiles, col_start, weights, sino, beside, (inner,))
 
     first = first_exchange(outer)
     chosen = [select_views(OUTER, tiles, *offsets, outer, got) for got in first]

time: 60.8 us -> 57.4 us (0.944)
  Pallas kernels: 17.4 us -> 14.4 us
  local copies, waits for them, and re-layouts: 1.02 us -> 0.05 us
    pallas_call x11, Pallas kernels: 17.4 us -> 14.4 us  [call(): pl.pallas_call(kernel, out_shape=outs, in_specs=[*specs, *[ANY] * len(aft...]
    unnamed x22 -> x16, local copies, waits for them, and re-layouts: 1.02 us -> 0.05 us
  transfers between devices with their start and end apart: 11 -> 11, of which waited for: 6 -> 7; matrix products, arithmetic and copies ran while one was open for 0% -> 0% of each run, Pallas kernels for 21% -> 18%
where the time goes in v5:
time: 57.4 us; the launch traced here: 56.5 us
  waiting for transfers between devices  27.4 us (48%)
  starting transfers between devices  14.6 us (25%)
  Pallas kernels  14.4 us (25%)
    ppermute x11, waiting for transfers between devices, permuted(): lax.ppermute(value, axis, [(i, j) for i, j in pairs if 0 <= j < count])  27.4 us
    ppermute x11, starting transfers between devices, permuted(): lax.ppermute(value, axis, [(i, j) for i, j in pairs if 0 <= j < count])  14.6 us
    pallas_call x11, Pallas kernels, call(): pl.pallas_call(kernel, out_shape=outs, in_specs=[*specs, *[ANY] * len(aft...  14.4 us
  transfers between devices with their start and end apart: 11, of which 7 were waited for; matrix products, arithmetic and copies ran while one was open for 0% of the time, Pallas kernels for 18%

profile of v5, /device:TPU:11, one launch (start us, length us, event | category | flops | bytes accessed | tf_op | source)
XLA Modules:
  0.0 56.5 jit_solution(13285446785907417599)
XLA Ops:
  0.0 0.7 %collective-permute-start = (f32[32,2,4096]{2,1,0:T(2,128)}, f32[32,2,4096]{2,1,0:T(2,128)S(1)}, u32[]{:S(2)}, u32[]{:S(2)}) collective-permute-start(f32[32,2,4096]{2,1,0:T(2,128)} %refs_2_.3), channel_id=1, source_target_pairs={{0,4},{4,0},{8,12},{12,8},{16,20},{20,16},{24,28},{28,24},{1,5},{5... | collective-permute-start | bytes 3145736 | tf_op jit(solution)/shard_map/ppermute | solution.py:544
  0.7 2.0 %shard_map.118 = (f32[10,64,128]{2,1,0:T(8,128)S(1)}, bf16[16,256,128]{2,1,0:T(8,128)(2,1)S(1)}, f32[32,2,4096]{2,1,0:T(2,128)S(1)}) custom-call(s32[32]{0:T(128)} %refs_0_.13, bf16[32,256,128]{2,1,0:T(8,128)(2,1)} %refs_1_.7, f32[32,2,4096]{2,1,0:T(2,128)} %refs_2_.3), custom_call_target="tpu_custom_call" | custom-call | flops 1 | bytes 1 | tf_op jit(solution)/shard_map/pallas_call | solution.py:35
  3.2 1.1 %shard_map.119.refs_4_.refs_3_ = f32[10,128,128]{2,1,0:T(8,128)S(1)} custom-call(s32[32]{0:T(128)S(1)} %copy-done.6, bf16[16,256,128]{2,1,0:T(8,128)(2,1)S(1)} %get-tuple-element.12.refs_1_, f32[32,2,4096]{2,1,0:T(2,128)S(1)} %collective-permute-done.refs_2_.refs_3_, f32[10,64,128]{2,1,0:T(8,128)S(1)} %get-tuple-element.13.refs_3_), custom_call_target="tpu_custom_call" | custom-call | flops 1 | bytes 1 | tf_op jit(solution)/shard_map/pallas_call | solution.py:35
  4.3 3.2 %collective-permute-start.2 = (f32[10,128,128]{2,1,0:T(8,128)S(1)}, f32[10,128,128]{2,1,0:T(8,128)S(1)}, u32[]{:S(2)}, u32[]{:S(2)}) collective-permute-start(f32[10,128,128]{2,1,0:T(8,128)S(1)} %shard_map.119.refs_4_.refs_3_), channel_id=1, source_target_pairs={{1,2},{2,1},{5,6},{6,5},{9,10},{10,9},{13,14},{14,13},{17,18},{18,... | collective-permute-start | bytes 1966088 | tf_op jit(solution)/shard_map/ppermute | solution.py:544
  7.6 1.2 %shard_map.120.refs_2_.refs_3_ = f32[6,2,64,128]{3,2,1,0:T(8,128)S(1)} custom-call(s32[32]{0:T(128)S(1)} %copy-done.6, bf16[16,256,128]{2,1,0:T(8,128)(2,1)S(1)} %get-tuple-element.12.refs_1_, f32[32,2,4096]{2,1,0:T(2,128)S(1)} %get-tuple-element.14.refs_2_, f32[32,2,4096]{2,1,0:T(2,128)S(1)} %collective-permute-done.refs_2_.refs_3_, ...), custom_call_target="tpu_custom_call" | custom-call | flops 2097152000 | bytes 1 | tf_op jit(solution)/shard_map/pallas_call | solution.py:35
  9.2 6.7 %collective-permute-done.3.refs_3_.refs_4_ = f32[6,2,64,128]{3,2,1,0:T(8,128)S(1)} collective-permute-done((f32[6,2,64,128]{3,2,1,0:T(8,128)S(1)}, f32[6,2,64,128]{3,2,1,0:T(8,128)S(1)}, u32[]{:S(2)}, u32[]{:S(2)}) %collective-permute-start.3) | collective-permute-done | bytes 393248 | tf_op jit(solution)/shard_map/ppermute | solution.py:544
  15.8 0.6 %shard_map.121.refs_5_ = f32[6,2,88,128]{3,2,1,0:T(8,128)S(1)} custom-call(s32[32]{0:T(128)S(1)} %copy-done.4, s32[32]{0:T(128)S(1)} %copy-done.5, f32[6,2,64,128]{3,2,1,0:T(8,128)S(1)} %shard_map.120.refs_2_.refs_3_, f32[6,2,64,128]{3,2,1,0:T(8,128)S(1)} %collective-permute-done.3.refs_3_.refs_4_), custom_call_target="tpu_custom_call" | custom-call | flops 1 | bytes 1 | tf_op jit(solution)/shard_map/pallas_call | solution.py:35
  16.5 1.3 %collective-permute-start.5 = (f32[6,2,88,128]{3,2,1,0:T(8,128)S(1)}, f32[6,2,88,128]{3,2,1,0:T(8,128)S(1)}, u32[]{:S(2)}, u32[]{:S(2)}) collective-permute-start(f32[6,2,88,128]{3,2,1,0:T(8,128)S(1)} %shard_map.121.refs_5_), channel_id=1, source_target_pairs={{0,8},{4,20},{8,0},{12,28},{16,24},{20,4},{24,16},{28,12},{1,9},{5... | collective-permute-start | bytes 1622024 | tf_op jit(solution)/shard_map/ppermute | solution.py:544
  17.8 4.3 %collective-permute-done.2.refs_2_ = f32[10,128,128]{2,1,0:T(8,128)S(1)} collective-permute-done((f32[10,128,128]{2,1,0:T(8,128)S(1)}, f32[10,128,128]{2,1,0:T(8,128)S(1)}, u32[]{:S(2)}, u32[]{:S(2)}) %collective-permute-start.2) | collective-permute-done | bytes 655392 | tf_op jit(solution)/shard_map/ppermute | solution.py:544
  22.1 1.1 %collective-permute-done.1.refs_1_ = f32[10,128,128]{2,1,0:T(8,128)S(1)} collective-permute-done((f32[10,128,128]{2,1,0:T(8,128)S(1)}, f32[10,128,128]{2,1,0:T(8,128)S(1)}, u32[]{:S(2)}, u32[]{:S(2)}) %collective-permute-start.1) | collective-permute-done | bytes 655392 | tf_op jit(solution)/shard_map/ppermute | solution.py:544
  23.2 0.8 %shard_map.122.refs_2_.refs_3_ = f32[10,2,64,128]{3,2,1,0:T(8,128)S(1)} custom-call(s32[32]{0:T(128)S(1)} %copy-done.7, f32[10,128,128]{2,1,0:T(8,128)S(1)} %collective-permute-done.1.refs_1_, f32[10,128,128]{2,1,0:T(8,128)S(1)} %collective-permute-done.2.refs_2_, f32[10,128,128]{2,1,0:T(8,128)S(1)} %shard_map.119.refs_4_.refs_3_, f32[2,4096]{1,0:T(2,128)S(1)} %copy-done.3, ...), custom_call_target="tpu_custom_call" | custom-call | flops 1 | bytes 1 | tf_op jit(solution)/shard_map/pallas_call | solution.py:35
  24.4 0.7 %collective-permute-done.5.refs_5_ = f32[6,2,88,128]{3,2,1,0:T(8,128)S(1)} collective-permute-done((f32[6,2,88,128]{3,2,1,0:T(8,128)S(1)}, f32[6,2,88,128]{3,2,1,0:T(8,128)S(1)}, u32[]{:S(2)}, u32[]{:S(2)}) %collective-permute-start.5) | collective-permute-done | bytes 540704 | tf_op jit(solution)/shard_map/ppermute | solution.py:544
  25.1 0.9 %shard_map.123.refs_4_.refs_3_ = f32[6,2,2,64,128]{4,3,2,1,0:T(8,128)S(1)} custom-call(s32[32]{0:T(128)S(1)} %copy-done.4, s32[32]{0:T(128)S(1)} %copy-done.5, f32[4,4096]{1,0:T(4,128)S(1)} %copy-done.2, f32[6,2,64,128]{3,2,1,0:T(8,128)S(1)} %shard_map.120.refs_2_.refs_3_, f32[6,2,64,128]{3,2,1,0:T(8,128)S(1)} %collective-permute-done.3.refs_3_.refs_4_, ...), custom_call_target="tpu_custom_call" | custom-call | flops 2621440000 | bytes 1 | tf_op jit(solution)/shard_map/pallas_call | solution.py:35
  26.0 2.1 %collective-permute-start.9 = (f32[6,2,2,64,128]{4,3,2,1,0:T(8,128)S(1)}, f32[6,2,2,64,128]{4,3,2,1,0:T(8,128)S(1)}, u32[]{:S(2)}, u32[]{:S(2)}) collective-permute-start(f32[6,2,2,64,128]{4,3,2,1,0:T(8,128)S(1)} %shard_map.123.refs_4_.refs_3_), channel_id=1, source_target_pairs={{1,2},{2,1},{5,6},{6,5},{9,10},{10,9},{13,14},{14,13},{17,18},{18,... | collective-permute-start | bytes 2359304 | tf_op jit(solution)/shard_map/ppermute | solution.py:544
  28.2 5.9 %collective-permute-done.4.refs_3_.refs_4_ = f32[10,2,64,128]{3,2,1,0:T(8,128)S(1)} collective-permute-done((f32[10,2,64,128]{3,2,1,0:T(8,128)S(1)}, f32[10,2,64,128]{3,2,1,0:T(8,128)S(1)}, u32[]{:S(2)}, u32[]{:S(2)}) %collective-permute-start.4) | collective-permute-done | bytes 655392 | tf_op jit(solution)/shard_map/ppermute | solution.py:544
  34.1 0.7 %shard_map.124 = f32[10,2,88,128]{3,2,1,0:T(8,128)S(1)} custom-call(s32[32]{0:T(128)S(1)} %copy-done.4, s32[32]{0:T(128)S(1)} %copy-done.5, f32[10,2,64,128]{3,2,1,0:T(8,128)S(1)} %shard_map.122.refs_2_.refs_3_, f32[10,2,64,128]{3,2,1,0:T(8,128)S(1)} %collective-permute-done.4.refs_3_.refs_4_, f32[6,2,2,64,128]{4,3,2,1,0:T(8,128)S(1)} %shard_map.123.refs_4_.refs_3_), custom_call_target="tpu_custom_call" | custom-call | flops 1 | bytes 1 | tf_op jit(solution)/shard_map/pallas_call | solution.py:35
  34.8 1.3 %collective-permute-start.6 = (f32[10,2,88,128]{3,2,1,0:T(8,128)S(1)}, f32[10,2,88,128]{3,2,1,0:T(8,128)S(1)}, u32[]{:S(2)}, u32[]{:S(2)}) collective-permute-start(f32[10,2,88,128]{3,2,1,0:T(8,128)S(1)} %shard_map.124), channel_id=1, source_target_pairs={{0,8},{4,20},{8,0},{12,28},{16,24},{20,4},{24,16},{28,12},{1,9},{5... | collective-permute-start | bytes 2703368 | tf_op jit(solution)/shard_map/ppermute | solution.py:544
  36.1 8.1 %collective-permute-done.9.refs_2_ = f32[6,2,2,64,128]{4,3,2,1,0:T(8,128)S(1)} collective-permute-done((f32[6,2,2,64,128]{4,3,2,1,0:T(8,128)S(1)}, f32[6,2,2,64,128]{4,3,2,1,0:T(8,128)S(1)}, u32[]{:S(2)}, u32[]{:S(2)}) %collective-permute-start.9) | collective-permute-done | bytes 786464 | tf_op jit(solution)/shard_map/ppermute | solution.py:544
  44.3 0.8 %shard_map.126 = (f32[6,2,2,32,128]{4,3,2,1,0:T(8,128)S(1)}, f32[6,2,2,32,128]{4,3,2,1,0:T(8,128)S(1)}) custom-call(s32[32]{0:T(128)S(1)} %copy-done.7, f32[6,2,2,64,128]{4,3,2,1,0:T(8,128)S(1)} %collective-permute-done.8.refs_1_, f32[6,2,2,64,128]{4,3,2,1,0:T(8,128)S(1)} %collective-permute-done.9.refs_2_, ...), custom_call_target="tpu_custom_call" | custom-call | flops 2097152000 | bytes 1 | tf_op jit(solution)/shard_map/pallas_call | solution.py:35
  45.2 3.9 %collective-permute-start.10 = (f32[6,2,2,32,128]{4,3,2,1,0:T(8,128)S(1)}, f32[6,2,2,32,128]{4,3,2,1,0:T(8,128)S(1)}, u32[]{:S(2)}, u32[]{:S(2)}) collective-permute-start(f32[6,2,2,32,128]{4,3,2,1,0:T(8,128)S(1)} %get-tuple-element.18), channel_id=1, source_target_pairs={{0,4},{4,0},{8,12},{12,8},{16,20},{20,16},{24,28},{28,24},{1,5},{5... | collective-permute-start | bytes 1179656 | tf_op jit(solution)/shard_map/ppermute | solution.py:544
  49.0 1.1 %shard_map.125 = (f32[10,2,2,32,128]{4,3,2,1,0:T(8,128)S(1)}, f32[10,2,2,32,128]{4,3,2,1,0:T(8,128)S(1)}) custom-call(s32[32]{0:T(128)S(1)} %copy-done.4, s32[32]{0:T(128)S(1)} %copy-done.5, f32[4,4096]{1,0:T(4,128)S(1)} %copy-done.2, f32[10,2,64,128]{3,2,1,0:T(8,128)S(1)} %shard_map.122.refs_2_.refs_3_, ...), custom_call_target="tpu_custom_call" | custom-call | flops 1 | bytes 1 | tf_op jit(solution)/shard_map/pallas_call | solution.py:35
  50.2 1.3 %collective-permute-start.7 = (f32[10,2,2,32,128]{4,3,2,1,0:T(8,128)S(1)}, f32[10,2,2,32,128]{4,3,2,1,0:T(8,128)S(1)}, u32[]{:S(2)}, u32[]{:S(2)}) collective-permute-start(f32[10,2,2,32,128]{4,3,2,1,0:T(8,128)S(1)} %get-tuple-element.16), channel_id=1, source_target_pairs={{0,4},{4,0},{8,12},{12,8},{16,20},{20,16},{24,28},{28,24},{1,5},{5... | collective-permute-start | bytes 1966088 | tf_op jit(solution)/shard_map/ppermute | solution.py:544
  51.5 1.9 %shard_map.127.refs_6_ = f32[32,2,8192]{2,1,0:T(2,128)} custom-call(bf16[768,256]{1,0:T(8,128)(2,1)S(1)} %copy-done.1, bf16[768,256]{1,0:T(8,128)(2,1)S(1)} %copy-done, f32[6,2,2,32,128]{4,3,2,1,0:T(8,128)S(1)} %get-tuple-element.17.refs_2_.refs_4_, f32[6,2,2,32,128]{4,3,2,1,0:T(8,128)S(1)} %collective-permute-done.10.refs_3_.refs_5_), custom_call_target="tpu_custom_call" | custom-call | flops 3145728000 | bytes 1 | tf_op jit(solution)/shard_map/pallas_call | solution.py:35
  53.5 3.1 %shard_map.128 = f32[32,2,8192]{2,1,0:T(2,128)} custom-call(bf16[768,256]{1,0:T(8,128)(2,1)S(1)} %copy-done.1, bf16[768,256]{1,0:T(8,128)(2,1)S(1)} %copy-done, f32[10,2,2,32,128]{4,3,2,1,0:T(8,128)S(1)} %get-tuple-element.15.refs_2_, f32[10,2,2,32,128]{4,3,2,1,0:T(8,128)S(1)} %collective-permute-done.7.refs_3_, ...), custom_call_target="tpu_custom_call", output_to_operand_aliasing={{}: (6, {})} | custom-call | flops 1 | bytes 1 | tf_op jit(solution)/shard_map/pallas_call | solution.py:35
  (25 shorter events, 1.4 us)
Async XLA Ops:
  0.0 3.2 %copy-start.6 = (s32[32]{0:T(128)S(1)}, s32[32]{0:T(128)}, u32[]{:S(2)}) copy-start(s32[32]{0:T(128)} %refs_0_.13) | copy-start | bytes 388
  0.0 3.2 %collective-permute-start = (f32[32,2,4096]{2,1,0:T(2,128)}, f32[32,2,4096]{2,1,0:T(2,128)S(1)}, u32[]{:S(2)}, u32[]{:S(2)}) collective-permute-start(f32[32,2,4096]{2,1,0:T(2,128)} %refs_2_.3), channel_id=1, source_target_pairs={{0,4},{4,0},{8,12},{12,8},{16,20},{20,16},{24,28},{28,24},{1,5},{5... | collective-permute-start | bytes 3145736 | tf_op jit(solution)/shard_map/ppermute | solution.py:544
  4.3 17.8 %collective-permute-start.2 = (f32[10,128,128]{2,1,0:T(8,128)S(1)}, f32[10,128,128]{2,1,0:T(8,128)S(1)}, u32[]{:S(2)}, u32[]{:S(2)}) collective-permute-start(f32[10,128,128]{2,1,0:T(8,128)S(1)} %shard_map.119.refs_4_.refs_3_), channel_id=1, source_target_pairs={{1,2},{2,1},{5,6},{6,5},{9,10},{10,9},{13,14},{14,13},{17,18},{18,... | collective-permute-start | bytes 1966088 | tf_op jit(solution)/shard_map/ppermute | solution.py:544
  7.5 15.7 %collective-permute-start.1 = (f32[10,128,128]{2,1,0:T(8,128)S(1)}, f32[10,128,128]{2,1,0:T(8,128)S(1)}, u32[]{:S(2)}, u32[]{:S(2)}) collective-permute-start(f32[10,128,128]{2,1,0:T(8,128)S(1)} %shard_map.119.refs_4_.refs_3_), channel_id=1, source_target_pairs={{0,1},{1,0},{2,3},{3,2},{4,5},{5,4},{6,7},{7,6},{8,9},{9,8},{10,11... | collective-permute-start | bytes 1966088 | tf_op jit(solution)/shard_map/ppermute | solution.py:544
  7.6 8.3 %copy-start.4 = (s32[32]{0:T(128)S(1)}, s32[32]{0:T(128)}, u32[]{:S(2)}) copy-start(s32[32]{0:T(128)} %refs_0_.18) | copy-start | bytes 388
  7.6 8.3 %copy-start.5 = (s32[32]{0:T(128)S(1)}, s32[32]{0:T(128)}, u32[]{:S(2)}) copy-start(s32[32]{0:T(128)} %refs_1_.11) | copy-start | bytes 388
  7.6 15.6 %copy-start.3 = (f32[2,4096]{1,0:T(2,128)S(1)}, f32[2,4096]{1,0:T(2,128)}, u32[]{:S(2)}) copy-start(f32[2,4096]{1,0:T(2,128)} %refs_4_.3) | copy-start | bytes 98308
  7.6 15.6 %copy-start.7 = (s32[32]{0:T(128)S(1)}, s32[32]{0:T(128)}, u32[]{:S(2)}) copy-start(s32[32]{0:T(128)} %refs_0_.19) | copy-start | bytes 388
  8.8 16.2 %copy-start.2 = (f32[4,4096]{1,0:T(4,128)S(1)}, f32[4,4096]{1,0:T(4,128)}, u32[]{:S(2)}) copy-start(f32[4,4096]{1,0:T(4,128)} %refs_2_.5) | copy-start | bytes 196612
  8.9 7.0 %collective-permute-start.3 = (f32[6,2,64,128]{3,2,1,0:T(8,128)S(1)}, f32[6,2,64,128]{3,2,1,0:T(8,128)S(1)}, u32[]{:S(2)}, u32[]{:S(2)}) collective-permute-start(f32[6,2,64,128]{3,2,1,0:T(8,128)S(1)} %shard_map.120.refs_2_.refs_3_), channel_id=1, source_target_pairs={{0,16},{4,12},{8,24},{12,4},{16,0},{20,28},{24,8},{28,20},{1,17},{... | collective-permute-start | bytes 1179656 | tf_op jit(solution)/shard_map/ppermute | solution.py:544
  16.5 8.6 %collective-permute-start.5 = (f32[6,2,88,128]{3,2,1,0:T(8,128)S(1)}, f32[6,2,88,128]{3,2,1,0:T(8,128)S(1)}, u32[]{:S(2)}, u32[]{:S(2)}) collective-permute-start(f32[6,2,88,128]{3,2,1,0:T(8,128)S(1)} %shard_map.121.refs_5_), channel_id=1, source_target_pairs={{0,8},{4,20},{8,0},{12,28},{16,24},{20,4},{24,16},{28,12},{1,9},{5... | collective-permute-start | bytes 1622024 | tf_op jit(solution)/shard_map/ppermute | solution.py:544
  24.0 10.1 %collective-permute-start.4 = (f32[10,2,64,128]{3,2,1,0:T(8,128)S(1)}, f32[10,2,64,128]{3,2,1,0:T(8,128)S(1)}, u32[]{:S(2)}, u32[]{:S(2)}) collective-permute-start(f32[10,2,64,128]{3,2,1,0:T(8,128)S(1)} %shard_map.122.refs_2_.refs_3_), channel_id=1, source_target_pairs={{0,16},{4,12},{8,24},{12,4},{16,0},{20,28},{24,8},{28,20},{1,17},{... | collective-permute-start | bytes 1966088 | tf_op jit(solution)/shard_map/ppermute | solution.py:544
  26.0 18.3 %collective-permute-start.9 = (f32[6,2,2,64,128]{4,3,2,1,0:T(8,128)S(1)}, f32[6,2,2,64,128]{4,3,2,1,0:T(8,128)S(1)}, u32[]{:S(2)}, u32[]{:S(2)}) collective-permute-start(f32[6,2,2,64,128]{4,3,2,1,0:T(8,128)S(1)} %shard_map.123.refs_4_.refs_3_), channel_id=1, source_target_pairs={{1,2},{2,1},{5,6},{6,5},{9,10},{10,9},{13,14},{14,13},{17,18},{18,... | collective-permute-start | bytes 2359304 | tf_op jit(solution)/shard_map/ppermute | solution.py:544
  28.1 16.2 %collective-permute-start.8 = (f32[6,2,2,64,128]{4,3,2,1,0:T(8,128)S(1)}, f32[6,2,2,64,128]{4,3,2,1,0:T(8,128)S(1)}, u32[]{:S(2)}, u32[]{:S(2)}) collective-permute-start(f32[6,2,2,64,128]{4,3,2,1,0:T(8,128)S(1)} %shard_map.123.refs_4_.refs_3_), channel_id=1, source_target_pairs={{0,1},{1,0},{2,3},{3,2},{4,5},{5,4},{6,7},{7,6},{8,9},{9,8},{10,11... | collective-permute-start | bytes 2359304 | tf_op jit(solution)/shard_map/ppermute | solution.py:544
  34.8 14.2 %collective-permute-start.6 = (f32[10,2,88,128]{3,2,1,0:T(8,128)S(1)}, f32[10,2,88,128]{3,2,1,0:T(8,128)S(1)}, u32[]{:S(2)}, u32[]{:S(2)}) collective-permute-start(f32[10,2,88,128]{3,2,1,0:T(8,128)S(1)} %shard_map.124), channel_id=1, source_target_pairs={{0,8},{4,20},{8,0},{12,28},{16,24},{20,4},{24,16},{28,12},{1,9},{5... | collective-permute-start | bytes 2703368 | tf_op jit(solution)/shard_map/ppermute | solution.py:544
  45.1 6.4 %copy-start = (bf16[768,256]{1,0:T(8,128)(2,1)S(1)}, bf16[768,256]{1,0:T(8,128)(2,1)}, u32[]{:S(2)}) copy-start(bf16[768,256]{1,0:T(8,128)(2,1)} %constant.5.clone.refs_1_) | copy-start | bytes 1179652
  45.2 6.3 %copy-start.1 = (bf16[768,256]{1,0:T(8,128)(2,1)S(1)}, bf16[768,256]{1,0:T(8,128)(2,1)}, u32[]{:S(2)}) copy-start(bf16[768,256]{1,0:T(8,128)(2,1)} %constant.4.clone.refs_0_) | copy-start | bytes 1179652
  45.2 6.3 %collective-permute-start.10 = (f32[6,2,2,32,128]{4,3,2,1,0:T(8,128)S(1)}, f32[6,2,2,32,128]{4,3,2,1,0:T(8,128)S(1)}, u32[]{:S(2)}, u32[]{:S(2)}) collective-permute-start(f32[6,2,2,32,128]{4,3,2,1,0:T(8,128)S(1)} %get-tuple-element.18), channel_id=1, source_target_pairs={{0,4},{4,0},{8,12},{12,8},{16,20},{20,16},{24,28},{28,24},{1,5},{5... | collective-permute-start | bytes 1179656 | tf_op jit(solution)/shard_map/ppermute | solution.py:544
  50.2 3.3 %collective-permute-start.7 = (f32[10,2,2,32,128]{4,3,2,1,0:T(8,128)S(1)}, f32[10,2,2,32,128]{4,3,2,1,0:T(8,128)S(1)}, u32[]{:S(2)}, u32[]{:S(2)}) collective-permute-start(f32[10,2,2,32,128]{4,3,2,1,0:T(8,128)S(1)} %get-tuple-element.16), channel_id=1, source_target_pairs={{0,4},{4,0},{8,12},{12,8},{16,20},{20,16},{24,28},{28,24},{1,5},{5... | collective-permute-start | bytes 1966088 | tf_op jit(solution)/shard_map/ppermute | solution.py:544

commit v6 on v5

--- a/solution.py
+++ b/solution.py
@@ -214,32 +214,34 @@
     )[0]
 
 
-def rows_body(group, tiles, offset_ref, even_ref, odd_ref, own_ref, weights_ref, out_ref, stack):
+def rows_body(group, tiles, offset_ref, odd_ref, even_ref, own_ref, weights_ref, out_ref):
     count, height, _ = own_ref.shape
     views = height // 2
     _, core = position()
-    after = lax.axis_index("row") % 2 == 0
-    even_at = pl.multiple_of(jnp.where(after, 2 * height, 0), 8)
-    odd_at = pl.multiple_of(jnp.where(after, 0, 2 * height), 8)
-
-    def step(index, slot):
-        tile = tile_of(index, group, tiles, core)
-        offset = offset_ref[tile]
-        stack[slot, pl.ds(even_at, height)] = even_ref[index]
-        stack[slot, pl.ds(odd_at, height)] = odd_ref[index]
-        stack[slot, height : 2 * height] = own_ref[index]
-        weights = weights_ref[:, pl.ds(pl.multiple_of(tile * LANES, LANES), LANES)]
-
-        def picked(row):
-            lifted = row + 2
-            first = lifted // 2 * height + lifted % 2
-            return stack[slot, pl.ds(first, views, stride=2), :]
-
-        terms = [picked(row + offset) for row in range(3)]
-        for row in range(2):
-            out_ref[index, row] = weights[0:1] * terms[row] + weights[1:2] * terms[row + 1]
-
-    unrolled(step, count)
+
+    def run(before, after):
+        def step(index, slot):
+            tile = tile_of(index, group, tiles, core)
+            offset = offset_ref[tile]
+            weights = weights_ref[:, pl.ds(pl.multiple_of(tile * LANES, LANES), LANES)]
+            lines = [
+                ref[index, pl.ds(row, views, stride=2), :]
+                for ref in (before, own_ref, after)
+                for row in range(2)
+            ]
+            terms = []
+            for row in range(3):
+                low = jnp.where(offset == -2, lines[row], lines[row + 1])
+                high = jnp.where(offset == 0, lines[row + 2], lines[row + 3])
+                terms.append(jnp.where(offset < 0, low, high))
+            for row in range(2):
+                out_ref[index, row] = weights[0:1] * terms[row] + weights[1:2] * terms[row + 1]
+
+        unrolled(step, count)
+
+    beside = lax.axis_index("row") % 2
+    pl.when(beside == 0)(lambda: run(odd_ref, even_ref))
+    pl.when(beside == 1)(lambda: run(even_ref, odd_ref))
 
 
 def interpolate_rows(group, tiles, offset, even, odd, own, weights, after):
@@ -247,13 +249,13 @@
     return call(
         functools.partial(rows_body, group, tiles),
         [f32(count, 2, height // 2, LANES)],
-        [pltpu.VMEM((2, 3 * height + 8, LANES), jnp.float32)],
-        (offset, even, odd, own, weights),
+        [],
+        (offset, odd, even, own, weights),
         after=after,
     )[0]
 
 
-def last_rows_body(group, tiles, offset_ref, even_ref, odd_ref, own_ref, weights_ref, keep_ref, send_ref, stack):
+def last_rows_body(group, tiles, offset_ref, odd_ref, even_ref, own_ref, weights_ref, keep_ref, send_ref, stack):
     count, parts, rows, chip_views, _ = own_ref.shape
     views = chip_views // 2
     _, core = position()
@@ -286,12 +288,12 @@
         functools.partial(last_rows_body, group, tiles),
         [f32(count, parts, rows, chip_views // 2, LANES)] * 2,
         [pltpu.VMEM((2, 3 * rows, chip_views, LANES), jnp.float32)],
-        (offset, even, odd, own, weights),
+        (offset, odd, even, own, weights),
         cycles(4000),
     )
 
 
-def select_body(group, tiles, view_ref, conj_ref, own_ref, got_ref, out_ref, stack):
+def select_body(group, tiles, view_ref, conj_ref, own_ref, got_ref, out_ref):
     count, rows, chip_views, lanes = own_ref.shape
     side, core = position()
 
@@ -303,46 +305,48 @@
     def slots(low, high):
         return low + lax.broadcasted_iota(jnp.int32, (high - low, lanes), 0)
 
-    def across_x(index, slot):
+    def joined(low, high, first, last):
+        if last <= 64:
+            return low[first:last]
+        if first >= 64:
+            return high[first - 64 : last - 64]
+        return jnp.concatenate([low[first:64], high[0 : last - 64]], axis=0)
+
+    def across_x(index, row, low, high):
         shift, opposite = shifts(index)
-        own_at = pl.multiple_of((1 - side) * chip_views, 8)
-        got_at = pl.multiple_of(side * chip_views, 8)
-        for row in range(rows):
-            out = out_ref.at[index, row]
-            both = stack.at[slot, row]
-            both[pl.ds(own_at, chip_views)] = own_ref[index, row]
-            both[pl.ds(got_at, chip_views)] = got_ref[index, row]
-            out[0:32] = jnp.where(slots(0, 32) >= shift + 32, both[96:128], both[0:32])
-            out[32:80] = jnp.where(slots(0, 48) >= opposite + 48, both[16:64], both[64:112])
-            out[80:88] = jnp.zeros((8, lanes), jnp.float32)
-
-    def across_y_first(index, slot):
+        out = out_ref.at[index, row]
+        both = functools.partial(joined, low.at[index, row], high.at[index, row])
+        out[0:32] = jnp.where(slots(0, 32) >= shift + 32, both(96, 128), both(0, 32))
+        out[32:80] = jnp.where(slots(0, 48) >= opposite + 48, both(16, 64), both(64, 112))
+        out[80:88] = jnp.zeros((8, lanes), jnp.float32)
+
+    def across_y_first(index, row, low, high):
         shift, opposite = shifts(index)
-        for row in range(rows):
-            out = out_ref.at[index, row]
-            both = stack.at[slot, row]
-            both[0:64] = own_ref[index, row]
-            both[64:128] = got_ref[index, row]
-            out[0:40] = jnp.where(slots(0, 40) >= opposite, both[0:40], both[72:112])
-            out[40:56] = both[40:56]
-            out[56:72] = jnp.where(slots(56, 72) >= 88 + shift, both[96:112], both[56:72])
-            out[72:88] = both[112:128]
-
-    def across_y_last(index, slot):
+        out = out_ref.at[index, row]
+        both = functools.partial(joined, low.at[index, row], high.at[index, row])
+        out[0:40] = jnp.where(slots(0, 40) >= opposite, both(0, 40), both(72, 112))
+        out[40:56] = both(40, 56)
+        out[56:72] = jnp.where(slots(56, 72) >= 88 + shift, both(96, 112), both(56, 72))
+        out[72:88] = both(112, 128)
+
+    def across_y_last(index, row, low, high):
         shift, opposite = shifts(index)
-        for row in range(rows):
-            out = out_ref.at[index, row]
-            both = stack.at[slot, row]
-            both[0:64] = got_ref[index, row]
-            both[64:128] = own_ref[index, row]
-            out[0:16] = both[0:16]
-            out[16:32] = jnp.where(slots(16, 32) < shift + 3, both[16:32], both[56:72])
-            out[32:48] = both[72:88]
-            out[48:88] = jnp.where(slots(48, 88) < 91 + opposite, both[88:128], both[16:56])
-
-    pl.when(core == 0)(lambda: unrolled(across_x, count))
-    pl.when((core == 1) & (side == 0))(lambda: unrolled(across_y_first, count))
-    pl.when((core == 1) & (side == 1))(lambda: unrolled(across_y_last, count))
+        out = out_ref.at[index, row]
+        both = functools.partial(joined, low.at[index, row], high.at[index, row])
+        out[0:16] = both(0, 16)
+        out[16:32] = jnp.where(slots(16, 32) < shift + 3, both(16, 32), both(56, 72))
+        out[32:48] = both(72, 88)
+        out[48:88] = jnp.where(slots(48, 88) < 91 + opposite, both(88, 128), both(16, 56))
+
+    def run(part, low, high):
+        for index in range(count):
+            for row in range(rows):
+                part(index, row, low, high)
+
+    pl.when((core == 0) & (side == 0))(lambda: run(across_x, got_ref, own_ref))
+    pl.when((core == 0) & (side == 1))(lambda: run(across_x, own_ref, got_ref))
+    pl.when((core == 1) & (side == 0))(lambda: run(across_y_first, own_ref, got_ref))
+    pl.when((core == 1) & (side == 1))(lambda: run(across_y_last, got_ref, own_ref))
 
 
 def select_views(group, tiles, view_offset, conj_offset, own, got, after=()):
@@ -350,7 +354,7 @@
     return call(
         functools.partial(select_body, group, tiles),
         [f32(count, rows, SLOTS, LANES)],
-        [pltpu.VMEM((2, rows, 2 * chip_views, LANES), jnp.float32)],
+        [],
         (view_offset, conj_offset, own, got),
         after=after,
     )[0]
@@ -457,8 +461,11 @@
 
 def filter_body(groups, number, tiles, high_ref, low_ref, *refs):
     parts = refs[: 4 if number else 2]
-    out_any, mixed, high_all, low_all, result, sems = refs[-6:]
-    views = out_any.shape[0]
+    if number:
+        earlier, out_any, mixed, high_all, low_all, result, sems = refs[4:]
+    else:
+        result, mixed, high_all, low_all = refs[2:]
+    views = result.shape[0]
     _, core = position()
     if number == 0:
         for ref in (high_all, low_all):
@@ -485,7 +492,18 @@
                 gather(groups[number - 1], ref, owner, begin + i, i)
 
     copies = []
-    for place, (first, count) in enumerate(stage_spans(groups, number, tiles)):
+
+    def leave(source, first, count):
+        columns = pl.ds(first * 2 * LANES, count * 2 * LANES)
+        copies.append(
+            pltpu.make_async_copy(source.at[:, :, columns], out_any.at[:, :, columns], sems.at[len(copies)])
+        )
+        copies[-1].start()
+
+    if number:
+        for first, count in stage_spans(groups, 0, tiles):
+            leave(earlier, first, count)
+    for first, count in stage_spans(groups, number, tiles):
 
         def window(ref):
             pieces = []
@@ -503,12 +521,8 @@
         for i in range(count):
             block = total[2 * views * i : 2 * views * (i + 1)].reshape(views, 2, 2 * LANES)
             result[:, :, (first + i) * 2 * LANES : (first + i + 1) * 2 * LANES] = block
-        columns = pl.ds(first * 2 * LANES, count * 2 * LANES)
-        copy = pltpu.make_async_copy(
-            result.at[:, :, columns], out_any.at[:, :, columns], sems.at[place]
-        )
-        copy.start()
-        copies.append(copy)
+        if number:
+            leave(result, first, count)
     for copy in copies:
         copy.wait()
 
@@ -516,24 +530,19 @@
 def ramp_filter(groups, number, tiles, keeps, gots, out):
     views = keeps[0].shape[3]
     args = [*filter_matrix(), keeps[number], gots[number]]
+    stored = pltpu.VMEM((2, tiles + 2, 2 * views, LANES), jnp.bfloat16)
+    scratch = [pltpu.VMEM((2, 2, 2 * views + 8, LANES), jnp.float32), stored, stored]
+    shape = f32(views, 2, 2 * tiles * LANES)
     if number:
         args += [keeps[number - 1], gots[number - 1], out]
-    stored = pltpu.VMEM((2, tiles + 2, 2 * views, LANES), jnp.bfloat16)
-    shape = f32(views, 2, 2 * tiles * LANES)
+        spans = sum(len(stage_spans(groups, i, tiles)) for i in range(2))
+        scratch += [pltpu.VMEM(shape.shape, jnp.float32), pltpu.SemaphoreType.DMA((spans,))]
     return call(
         functools.partial(filter_body, groups, number, tiles),
         [shape],
-        [
-            pltpu.VMEM((2, 2, 2 * views + 8, LANES), jnp.float32),
-            stored,
-            stored,
-            pltpu.VMEM(shape.shape, jnp.float32),
-            pltpu.SemaphoreType.DMA((len(stage_spans(groups, number, tiles)),)),
-        ],
+        scratch,
         args,
-        specs=[VMEM] * 6 + [ANY] if number else [VMEM] * 4,
-        out=ANY,
-        aliases={6: 0} if number else {},
+        out=ANY if number else VMEM,
         cost=SHORT if number else cycles(6000),
     )[0]
 

time: 57.4 us -> 56.7 us (0.988); the launches traced: 56.5 us -> 56.6 us
  starting transfers between devices: 14.6 us -> 15.8 us
  Pallas kernels: 14.4 us -> 13.6 us
    ppermute x11, starting transfers between devices: 14.6 us -> 15.8 us  [permuted(): lax.ppermute(value, axis, [(i, j) for i, j in pairs if 0 <= j < count])]
    pallas_call x11, Pallas kernels: 14.4 us -> 13.6 us  [call(): pl.pallas_call(kernel, out_shape=outs, in_specs=[*specs, *[ANY] * len(aft...]
  transfers between devices with their start and end apart: 11 -> 11, of which waited for: 7 -> 10; matrix products, arithmetic and copies ran while one was open for 0% -> 0% of each run, Pallas kernels for 18% -> 17%
where the time goes in v6:
time: 56.7 us; the launch traced here: 56.6 us
  waiting for transfers between devices  27 us (48%)
  starting transfers between devices  15.8 us (28%)
  Pallas kernels  13.6 us (24%)
    ppermute x11, waiting for transfers between devices, permuted(): lax.ppermute(value, axis, [(i, j) for i, j in pairs if 0 <= j < count])  27 us
    ppermute x11, starting transfers between devices, permuted(): lax.ppermute(value, axis, [(i, j) for i, j in pairs if 0 <= j < count])  15.8 us
    pallas_call x11, Pallas kernels, call(): pl.pallas_call(kernel, out_shape=outs, in_specs=[*specs, *[ANY] * len(aft...  13.6 us
  transfers between devices with their start and end apart: 11, of which 10 were waited for; matrix products, arithmetic and copies ran while one was open for 0% of the time, Pallas kernels for 17%

profile of v6, /device:TPU:11, one launch (start us, length us, event | category | flops | bytes accessed | tf_op | source)
XLA Modules:
  0.0 56.6 jit_solution(17555939698782873229)
XLA Ops:
  0.0 0.7 %collective-permute-start = (f32[32,2,4096]{2,1,0:T(2,128)}, f32[32,2,4096]{2,1,0:T(2,128)S(1)}, u32[]{:S(2)}, u32[]{:S(2)}) collective-permute-start(f32[32,2,4096]{2,1,0:T(2,128)} %refs_2_.3), channel_id=1, source_target_pairs={{0,4},{4,0},{8,12},{12,8},{16,20},{20,16},{24,28},{28,24},{1,5},{5... | collective-permute-start | bytes 3145736 | tf_op jit(solution)/shard_map/ppermute | solution.py:553
  0.7 2.0 %shard_map.118 = (f32[10,64,128]{2,1,0:T(8,128)S(1)}, bf16[16,256,128]{2,1,0:T(8,128)(2,1)S(1)}, f32[32,2,4096]{2,1,0:T(2,128)S(1)}) custom-call(s32[32]{0:T(128)} %refs_0_.13, bf16[32,256,128]{2,1,0:T(8,128)(2,1)} %refs_1_.7, f32[32,2,4096]{2,1,0:T(2,128)} %refs_2_.3), custom_call_target="tpu_custom_call" | custom-call | flops 1 | bytes 1 | tf_op jit(solution)/shard_map/pallas_call | solution.py:35
  3.2 1.1 %shard_map.119.refs_4_.refs_3_ = f32[10,128,128]{2,1,0:T(8,128)S(1)} custom-call(s32[32]{0:T(128)S(1)} %copy-done.6, bf16[16,256,128]{2,1,0:T(8,128)(2,1)S(1)} %get-tuple-element.12.refs_1_, f32[32,2,4096]{2,1,0:T(2,128)S(1)} %collective-permute-done.refs_2_.refs_3_, f32[10,64,128]{2,1,0:T(8,128)S(1)} %get-tuple-element.13.refs_3_), custom_call_target="tpu_custom_call" | custom-call | flops 1 | bytes 1 | tf_op jit(solution)/shard_map/pallas_call | solution.py:35
  4.5 4.3 %collective-permute-start.1 = (f32[10,128,128]{2,1,0:T(8,128)S(1)}, f32[10,128,128]{2,1,0:T(8,128)S(1)}, u32[]{:S(2)}, u32[]{:S(2)}) collective-permute-start(f32[10,128,128]{2,1,0:T(8,128)S(1)} %shard_map.119.refs_4_.refs_3_), channel_id=1, source_target_pairs={{1,2},{2,1},{5,6},{6,5},{9,10},{10,9},{13,14},{14,13},{17,18},{18,... | collective-permute-start | bytes 1966088 | tf_op jit(solution)/shard_map/ppermute | solution.py:553
  8.9 1.2 %shard_map.120.refs_2_.refs_3_ = f32[6,2,64,128]{3,2,1,0:T(8,128)S(1)} custom-call(s32[32]{0:T(128)S(1)} %copy-done.6, bf16[16,256,128]{2,1,0:T(8,128)(2,1)S(1)} %get-tuple-element.12.refs_1_, f32[32,2,4096]{2,1,0:T(2,128)S(1)} %get-tuple-element.14.refs_2_, f32[32,2,4096]{2,1,0:T(2,128)S(1)} %collective-permute-done.refs_2_.refs_3_, ...), custom_call_target="tpu_custom_call" | custom-call | flops 2097152000 | bytes 1 | tf_op jit(solution)/shard_map/pallas_call | solution.py:35
  10.4 6.7 %collective-permute-done.3.refs_3_.refs_4_ = f32[6,2,64,128]{3,2,1,0:T(8,128)S(1)} collective-permute-done((f32[6,2,64,128]{3,2,1,0:T(8,128)S(1)}, f32[6,2,64,128]{3,2,1,0:T(8,128)S(1)}, u32[]{:S(2)}, u32[]{:S(2)}) %collective-permute-start.3) | collective-permute-done | bytes 393248 | tf_op jit(solution)/shard_map/ppermute | solution.py:553
  17.8 1.3 %collective-permute-start.5 = (f32[6,2,88,128]{3,2,1,0:T(8,128)S(1)}, f32[6,2,88,128]{3,2,1,0:T(8,128)S(1)}, u32[]{:S(2)}, u32[]{:S(2)}) collective-permute-start(f32[6,2,88,128]{3,2,1,0:T(8,128)S(1)} %shard_map.121.refs_5_), channel_id=1, source_target_pairs={{0,8},{4,20},{8,0},{12,28},{16,24},{20,4},{24,16},{28,12},{1,9},{5... | collective-permute-start | bytes 1622024 | tf_op jit(solution)/shard_map/ppermute | solution.py:553
  19.1 1.2 %collective-permute-done.2.refs_2_ = f32[10,128,128]{2,1,0:T(8,128)S(1)} collective-permute-done((f32[10,128,128]{2,1,0:T(8,128)S(1)}, f32[10,128,128]{2,1,0:T(8,128)S(1)}, u32[]{:S(2)}, u32[]{:S(2)}) %collective-permute-start.2) | collective-permute-done | bytes 655392 | tf_op jit(solution)/shard_map/ppermute | solution.py:553
  20.3 3.0 %collective-permute-done.1.refs_1_ = f32[10,128,128]{2,1,0:T(8,128)S(1)} collective-permute-done((f32[10,128,128]{2,1,0:T(8,128)S(1)}, f32[10,128,128]{2,1,0:T(8,128)S(1)}, u32[]{:S(2)}, u32[]{:S(2)}) %collective-permute-start.1) | collective-permute-done | bytes 655392 | tf_op jit(solution)/shard_map/ppermute | solution.py:553
  23.3 0.7 %shard_map.122.refs_2_.refs_3_ = f32[10,2,64,128]{3,2,1,0:T(8,128)S(1)} custom-call(s32[32]{0:T(128)S(1)} %copy-done.7, f32[10,128,128]{2,1,0:T(8,128)S(1)} %collective-permute-done.1.refs_1_, f32[10,128,128]{2,1,0:T(8,128)S(1)} %collective-permute-done.2.refs_2_, f32[10,128,128]{2,1,0:T(8,128)S(1)} %shard_map.119.refs_4_.refs_3_, f32[2,4096]{1,0:T(2,128)S(1)} %copy-done.3, ...), custom_call_target="tpu_custom_call" | custom-call | flops 1 | bytes 1 | tf_op jit(solution)/shard_map/pallas_call | solution.py:35
  24.4 2.0 %collective-permute-done.5.refs_5_ = f32[6,2,88,128]{3,2,1,0:T(8,128)S(1)} collective-permute-done((f32[6,2,88,128]{3,2,1,0:T(8,128)S(1)}, f32[6,2,88,128]{3,2,1,0:T(8,128)S(1)}, u32[]{:S(2)}, u32[]{:S(2)}) %collective-permute-start.5) | collective-permute-done | bytes 540704 | tf_op jit(solution)/shard_map/ppermute | solution.py:553
  26.3 0.9 %shard_map.123.refs_4_.refs_3_ = f32[6,2,2,64,128]{4,3,2,1,0:T(8,128)S(1)} custom-call(s32[32]{0:T(128)S(1)} %copy-done.4, s32[32]{0:T(128)S(1)} %copy-done.5, f32[4,4096]{1,0:T(4,128)S(1)} %copy-done.2, f32[6,2,64,128]{3,2,1,0:T(8,128)S(1)} %shard_map.120.refs_2_.refs_3_, f32[6,2,64,128]{3,2,1,0:T(8,128)S(1)} %collective-permute-done.3.refs_3_.refs_4_, ...), custom_call_target="tpu_custom_call" | custom-call | flops 2621440000 | bytes 1 | tf_op jit(solution)/shard_map/pallas_call | solution.py:35
  27.3 1.9 %collective-permute-start.8 = (f32[6,2,2,64,128]{4,3,2,1,0:T(8,128)S(1)}, f32[6,2,2,64,128]{4,3,2,1,0:T(8,128)S(1)}, u32[]{:S(2)}, u32[]{:S(2)}) collective-permute-start(f32[6,2,2,64,128]{4,3,2,1,0:T(8,128)S(1)} %shard_map.123.refs_4_.refs_3_), channel_id=1, source_target_pairs={{1,2},{2,1},{5,6},{6,5},{9,10},{10,9},{13,14},{14,13},{17,18},{18,... | collective-permute-start | bytes 2359304 | tf_op jit(solution)/shard_map/ppermute | solution.py:553
  29.3 6.3 %collective-permute-done.4.refs_3_.refs_4_ = f32[10,2,64,128]{3,2,1,0:T(8,128)S(1)} collective-permute-done((f32[10,2,64,128]{3,2,1,0:T(8,128)S(1)}, f32[10,2,64,128]{3,2,1,0:T(8,128)S(1)}, u32[]{:S(2)}, u32[]{:S(2)}) %collective-permute-start.4) | collective-permute-done | bytes 655392 | tf_op jit(solution)/shard_map/ppermute | solution.py:553
  35.6 0.7 %shard_map.124 = f32[10,2,88,128]{3,2,1,0:T(8,128)S(1)} custom-call(s32[32]{0:T(128)S(1)} %copy-done.4, s32[32]{0:T(128)S(1)} %copy-done.5, f32[10,2,64,128]{3,2,1,0:T(8,128)S(1)} %shard_map.122.refs_2_.refs_3_, f32[10,2,64,128]{3,2,1,0:T(8,128)S(1)} %collective-permute-done.4.refs_3_.refs_4_, f32[6,2,2,64,128]{4,3,2,1,0:T(8,128)S(1)} %shard_map.123.refs_4_.refs_3_), custom_call_target="tpu_custom_call" | custom-call | flops 1 | bytes 1 | tf_op jit(solution)/shard_map/pallas_call | solution.py:35
  36.3 1.3 %collective-permute-start.6 = (f32[10,2,88,128]{3,2,1,0:T(8,128)S(1)}, f32[10,2,88,128]{3,2,1,0:T(8,128)S(1)}, u32[]{:S(2)}, u32[]{:S(2)}) collective-permute-start(f32[10,2,88,128]{3,2,1,0:T(8,128)S(1)} %shard_map.124), channel_id=1, source_target_pairs={{0,8},{4,20},{8,0},{12,28},{16,24},{20,4},{24,16},{28,12},{1,9},{5... | collective-permute-start | bytes 2703368 | tf_op jit(solution)/shard_map/ppermute | solution.py:553
  37.6 4.5 %collective-permute-done.9.refs_2_ = f32[6,2,2,64,128]{4,3,2,1,0:T(8,128)S(1)} collective-permute-done((f32[6,2,2,64,128]{4,3,2,1,0:T(8,128)S(1)}, f32[6,2,2,64,128]{4,3,2,1,0:T(8,128)S(1)}, u32[]{:S(2)}, u32[]{:S(2)}) %collective-permute-start.9) | collective-permute-done | bytes 786464 | tf_op jit(solution)/shard_map/ppermute | solution.py:553
  42.0 1.9 %collective-permute-done.8.refs_1_ = f32[6,2,2,64,128]{4,3,2,1,0:T(8,128)S(1)} collective-permute-done((f32[6,2,2,64,128]{4,3,2,1,0:T(8,128)S(1)}, f32[6,2,2,64,128]{4,3,2,1,0:T(8,128)S(1)}, u32[]{:S(2)}, u32[]{:S(2)}) %collective-permute-start.8) | collective-permute-done | bytes 786464 | tf_op jit(solution)/shard_map/ppermute | solution.py:553
  44.0 0.9 %shard_map.126 = (f32[6,2,2,32,128]{4,3,2,1,0:T(8,128)S(1)}, f32[6,2,2,32,128]{4,3,2,1,0:T(8,128)S(1)}) custom-call(s32[32]{0:T(128)S(1)} %copy-done.7, f32[6,2,2,64,128]{4,3,2,1,0:T(8,128)S(1)} %collective-permute-done.8.refs_1_, f32[6,2,2,64,128]{4,3,2,1,0:T(8,128)S(1)} %collective-permute-done.9.refs_2_, ...), custom_call_target="tpu_custom_call" | custom-call | flops 2097152000 | bytes 1 | tf_op jit(solution)/shard_map/pallas_call | solution.py:35
  44.8 5.3 %collective-permute-start.10 = (f32[6,2,2,32,128]{4,3,2,1,0:T(8,128)S(1)}, f32[6,2,2,32,128]{4,3,2,1,0:T(8,128)S(1)}, u32[]{:S(2)}, u32[]{:S(2)}) collective-permute-start(f32[6,2,2,32,128]{4,3,2,1,0:T(8,128)S(1)} %get-tuple-element.18), channel_id=1, source_target_pairs={{0,4},{4,0},{8,12},{12,8},{16,20},{20,16},{24,28},{28,24},{1,5},{5... | collective-permute-start | bytes 1179656 | tf_op jit(solution)/shard_map/ppermute | solution.py:553
  50.1 1.1 %shard_map.125 = (f32[10,2,2,32,128]{4,3,2,1,0:T(8,128)S(1)}, f32[10,2,2,32,128]{4,3,2,1,0:T(8,128)S(1)}) custom-call(s32[32]{0:T(128)S(1)} %copy-done.4, s32[32]{0:T(128)S(1)} %copy-done.5, f32[4,4096]{1,0:T(4,128)S(1)} %copy-done.2, f32[10,2,64,128]{3,2,1,0:T(8,128)S(1)} %shard_map.122.refs_2_.refs_3_, ...), custom_call_target="tpu_custom_call" | custom-call | flops 1 | bytes 1 | tf_op jit(solution)/shard_map/pallas_call | solution.py:35
  51.5 1.2 %shard_map.127.refs_6_ = f32[32,2,8192]{2,1,0:T(2,128)S(1)} custom-call(bf16[768,256]{1,0:T(8,128)(2,1)S(1)} %copy-done.1, bf16[768,256]{1,0:T(8,128)(2,1)S(1)} %copy-done, f32[6,2,2,32,128]{4,3,2,1,0:T(8,128)S(1)} %get-tuple-element.17.refs_2_.refs_4_, f32[6,2,2,32,128]{4,3,2,1,0:T(8,128)S(1)} %collective-permute-done.10.refs_3_.refs_5_), custom_call_target="tpu_custom_call" | custom-call | flops 3145728000 | bytes 1 | tf_op jit(solution)/shard_map/pallas_call | solution.py:35
  52.7 0.7 %collective-permute-done.7.refs_3_ = f32[10,2,2,32,128]{4,3,2,1,0:T(8,128)S(1)} collective-permute-done((f32[10,2,2,32,128]{4,3,2,1,0:T(8,128)S(1)}, f32[10,2,2,32,128]{4,3,2,1,0:T(8,128)S(1)}, u32[]{:S(2)}, u32[]{:S(2)}) %collective-permute-start.7) | collective-permute-done | bytes 655392 | tf_op jit(solution)/shard_map/ppermute | solution.py:553
  53.4 3.1 %shard_map.128 = f32[32,2,8192]{2,1,0:T(2,128)} custom-call(bf16[768,256]{1,0:T(8,128)(2,1)S(1)} %copy-done.1, bf16[768,256]{1,0:T(8,128)(2,1)S(1)} %copy-done, f32[10,2,2,32,128]{4,3,2,1,0:T(8,128)S(1)} %get-tuple-element.15.refs_2_, f32[10,2,2,32,128]{4,3,2,1,0:T(8,128)S(1)} %collective-permute-done.7.refs_3_, ...), custom_call_target="tpu_custom_call" | custom-call | flops 1 | bytes 1 | tf_op jit(solution)/shard_map/pallas_call | solution.py:35
  (25 shorter events, 2.3 us)
Async XLA Ops:
  0.0 3.2 %copy-start.6 = (s32[32]{0:T(128)S(1)}, s32[32]{0:T(128)}, u32[]{:S(2)}) copy-start(s32[32]{0:T(128)} %refs_0_.13) | copy-start | bytes 388
  0.0 3.2 %collective-permute-start = (f32[32,2,4096]{2,1,0:T(2,128)}, f32[32,2,4096]{2,1,0:T(2,128)S(1)}, u32[]{:S(2)}, u32[]{:S(2)}) collective-permute-start(f32[32,2,4096]{2,1,0:T(2,128)} %refs_2_.3), channel_id=1, source_target_pairs={{0,4},{4,0},{8,12},{12,8},{16,20},{20,16},{24,28},{28,24},{1,5},{5... | collective-permute-start | bytes 3145736 | tf_op jit(solution)/shard_map/ppermute | solution.py:553
  4.3 16.0 %collective-permute-start.2 = (f32[10,128,128]{2,1,0:T(8,128)S(1)}, f32[10,128,128]{2,1,0:T(8,128)S(1)}, u32[]{:S(2)}, u32[]{:S(2)}) collective-permute-start(f32[10,128,128]{2,1,0:T(8,128)S(1)} %shard_map.119.refs_4_.refs_3_), channel_id=1, source_target_pairs={{0,1},{1,0},{2,3},{3,2},{4,5},{5,4},{6,7},{7,6},{8,9},{9,8},{10,11... | collective-permute-start | bytes 1966088 | tf_op jit(solution)/shard_map/ppermute | solution.py:553
  4.5 18.8 %collective-permute-start.1 = (f32[10,128,128]{2,1,0:T(8,128)S(1)}, f32[10,128,128]{2,1,0:T(8,128)S(1)}, u32[]{:S(2)}, u32[]{:S(2)}) collective-permute-start(f32[10,128,128]{2,1,0:T(8,128)S(1)} %shard_map.119.refs_4_.refs_3_), channel_id=1, source_target_pairs={{1,2},{2,1},{5,6},{6,5},{9,10},{10,9},{13,14},{14,13},{17,18},{18,... | collective-permute-start | bytes 1966088 | tf_op jit(solution)/shard_map/ppermute | solution.py:553
  8.8 8.3 %copy-start.4 = (s32[32]{0:T(128)S(1)}, s32[32]{0:T(128)}, u32[]{:S(2)}) copy-start(s32[32]{0:T(128)} %refs_0_.18) | copy-start | bytes 388
  8.9 8.3 %copy-start.5 = (s32[32]{0:T(128)S(1)}, s32[32]{0:T(128)}, u32[]{:S(2)}) copy-start(s32[32]{0:T(128)} %refs_1_.11) | copy-start | bytes 388
  8.9 14.4 %copy-start.3 = (f32[2,4096]{1,0:T(2,128)S(1)}, f32[2,4096]{1,0:T(2,128)}, u32[]{:S(2)}) copy-start(f32[2,4096]{1,0:T(2,128)} %refs_4_.3) | copy-start | bytes 98308
  8.9 14.4 %copy-start.7 = (s32[32]{0:T(128)S(1)}, s32[32]{0:T(128)}, u32[]{:S(2)}) copy-start(s32[32]{0:T(128)} %refs_0_.19) | copy-start | bytes 388
  10.1 16.2 %copy-start.2 = (f32[4,4096]{1,0:T(4,128)S(1)}, f32[4,4096]{1,0:T(4,128)}, u32[]{:S(2)}) copy-start(f32[4,4096]{1,0:T(4,128)} %refs_2_.5) | copy-start | bytes 196612
  10.1 7.0 %collective-permute-start.3 = (f32[6,2,64,128]{3,2,1,0:T(8,128)S(1)}, f32[6,2,64,128]{3,2,1,0:T(8,128)S(1)}, u32[]{:S(2)}, u32[]{:S(2)}) collective-permute-start(f32[6,2,64,128]{3,2,1,0:T(8,128)S(1)} %shard_map.120.refs_2_.refs_3_), channel_id=1, source_target_pairs={{0,16},{4,12},{8,24},{12,4},{16,0},{20,28},{24,8},{28,20},{1,17},{... | collective-permute-start | bytes 1179656 | tf_op jit(solution)/shard_map/ppermute | solution.py:553
  17.8 8.6 %collective-permute-start.5 = (f32[6,2,88,128]{3,2,1,0:T(8,128)S(1)}, f32[6,2,88,128]{3,2,1,0:T(8,128)S(1)}, u32[]{:S(2)}, u32[]{:S(2)}) collective-permute-start(f32[6,2,88,128]{3,2,1,0:T(8,128)S(1)} %shard_map.121.refs_5_), channel_id=1, source_target_pairs={{0,8},{4,20},{8,0},{12,28},{16,24},{20,4},{24,16},{28,12},{1,9},{5... | collective-permute-start | bytes 1622024 | tf_op jit(solution)/shard_map/ppermute | solution.py:553
  24.1 11.5 %collective-permute-start.4 = (f32[10,2,64,128]{3,2,1,0:T(8,128)S(1)}, f32[10,2,64,128]{3,2,1,0:T(8,128)S(1)}, u32[]{:S(2)}, u32[]{:S(2)}) collective-permute-start(f32[10,2,64,128]{3,2,1,0:T(8,128)S(1)} %shard_map.122.refs_2_.refs_3_), channel_id=1, source_target_pairs={{0,16},{4,12},{8,24},{12,4},{16,0},{20,28},{24,8},{28,20},{1,17},{... | collective-permute-start | bytes 1966088 | tf_op jit(solution)/shard_map/ppermute | solution.py:553
  27.3 14.8 %collective-permute-start.9 = (f32[6,2,2,64,128]{4,3,2,1,0:T(8,128)S(1)}, f32[6,2,2,64,128]{4,3,2,1,0:T(8,128)S(1)}, u32[]{:S(2)}, u32[]{:S(2)}) collective-permute-start(f32[6,2,2,64,128]{4,3,2,1,0:T(8,128)S(1)} %shard_map.123.refs_4_.refs_3_), channel_id=1, source_target_pairs={{0,1},{1,0},{2,3},{3,2},{4,5},{5,4},{6,7},{7,6},{8,9},{9,8},{10,11... | collective-permute-start | bytes 2359304 | tf_op jit(solution)/shard_map/ppermute | solution.py:553
  27.3 16.6 %collective-permute-start.8 = (f32[6,2,2,64,128]{4,3,2,1,0:T(8,128)S(1)}, f32[6,2,2,64,128]{4,3,2,1,0:T(8,128)S(1)}, u32[]{:S(2)}, u32[]{:S(2)}) collective-permute-start(f32[6,2,2,64,128]{4,3,2,1,0:T(8,128)S(1)} %shard_map.123.refs_4_.refs_3_), channel_id=1, source_target_pairs={{1,2},{2,1},{5,6},{6,5},{9,10},{10,9},{13,14},{14,13},{17,18},{18,... | collective-permute-start | bytes 2359304 | tf_op jit(solution)/shard_map/ppermute | solution.py:553
  36.3 13.9 %collective-permute-start.6 = (f32[10,2,88,128]{3,2,1,0:T(8,128)S(1)}, f32[10,2,88,128]{3,2,1,0:T(8,128)S(1)}, u32[]{:S(2)}, u32[]{:S(2)}) collective-permute-start(f32[10,2,88,128]{3,2,1,0:T(8,128)S(1)} %shard_map.124), channel_id=1, source_target_pairs={{0,8},{4,20},{8,0},{12,28},{16,24},{20,4},{24,16},{28,12},{1,9},{5... | collective-permute-start | bytes 2703368 | tf_op jit(solution)/shard_map/ppermute | solution.py:553
  44.8 6.7 %copy-start = (bf16[768,256]{1,0:T(8,128)(2,1)S(1)}, bf16[768,256]{1,0:T(8,128)(2,1)}, u32[]{:S(2)}) copy-start(bf16[768,256]{1,0:T(8,128)(2,1)} %constant.5.clone.refs_1_) | copy-start | bytes 1179652
  44.8 6.7 %copy-start.1 = (bf16[768,256]{1,0:T(8,128)(2,1)S(1)}, bf16[768,256]{1,0:T(8,128)(2,1)}, u32[]{:S(2)}) copy-start(bf16[768,256]{1,0:T(8,128)(2,1)} %constant.4.clone.refs_0_) | copy-start | bytes 1179652
  44.8 6.6 %collective-permute-start.10 = (f32[6,2,2,32,128]{4,3,2,1,0:T(8,128)S(1)}, f32[6,2,2,32,128]{4,3,2,1,0:T(8,128)S(1)}, u32[]{:S(2)}, u32[]{:S(2)}) collective-permute-start(f32[6,2,2,32,128]{4,3,2,1,0:T(8,128)S(1)} %get-tuple-element.18), channel_id=1, source_target_pairs={{0,4},{4,0},{8,12},{12,8},{16,20},{20,16},{24,28},{28,24},{1,5},{5... | collective-permute-start | bytes 1179656 | tf_op jit(solution)/shard_map/ppermute | solution.py:553
  51.3 2.2 %collective-permute-start.7 = (f32[10,2,2,32,128]{4,3,2,1,0:T(8,128)S(1)}, f32[10,2,2,32,128]{4,3,2,1,0:T(8,128)S(1)}, u32[]{:S(2)}, u32[]{:S(2)}) collective-permute-start(f32[10,2,2,32,128]{4,3,2,1,0:T(8,128)S(1)} %get-tuple-element.16), channel_id=1, source_target_pairs={{0,4},{4,0},{8,12},{12,8},{16,20},{20,16},{24,28},{28,24},{1,5},{5... | collective-permute-start | bytes 1966088 | tf_op jit(solution)/shard_map/ppermute | solution.py:553

commit v7 on v6

--- a/solution.py
+++ b/solution.py
@@ -10,7 +10,8 @@
 from jax.sharding import PartitionSpec as P
 
 KR = 256
-OUTER, INNER = (0, 6), (6, 10)
+LAST_COST = 1
+GROUPS = ((0, 5), (5, 6), (11, 5))
 LANES = 128
 WINDOW = 3 * LANES
 SLOTS = 88
@@ -214,44 +215,44 @@
     )[0]
 
 
-def rows_body(group, tiles, offset_ref, odd_ref, even_ref, own_ref, weights_ref, out_ref):
-    count, height, _ = own_ref.shape
+def rows_body(group, held, tiles, offset_ref, odd_ref, even_ref, own_ref, weights_ref, out_ref, stack):
+    count, height = out_ref.shape[0], own_ref.shape[1]
     views = height // 2
     _, core = position()
-
-    def run(before, after):
-        def step(index, slot):
-            tile = tile_of(index, group, tiles, core)
-            offset = offset_ref[tile]
-            weights = weights_ref[:, pl.ds(pl.multiple_of(tile * LANES, LANES), LANES)]
-            lines = [
-                ref[index, pl.ds(row, views, stride=2), :]
-                for ref in (before, own_ref, after)
-                for row in range(2)
-            ]
-            terms = []
-            for row in range(3):
-                low = jnp.where(offset == -2, lines[row], lines[row + 1])
-                high = jnp.where(offset == 0, lines[row + 2], lines[row + 3])
-                terms.append(jnp.where(offset < 0, low, high))
-            for row in range(2):
-                out_ref[index, row] = weights[0:1] * terms[row] + weights[1:2] * terms[row + 1]
-
-        unrolled(step, count)
-
-    beside = lax.axis_index("row") % 2
-    pl.when(beside == 0)(lambda: run(odd_ref, even_ref))
-    pl.when(beside == 1)(lambda: run(even_ref, odd_ref))
-
-
-def interpolate_rows(group, tiles, offset, even, odd, own, weights, after):
-    count, height, _ = own.shape
-    return call(
-        functools.partial(rows_body, group, tiles),
-        [f32(count, 2, height // 2, LANES)],
-        [],
+    begin = tile_of(0, group, tiles, core) - tile_of(0, held, tiles, core)
+    after = lax.axis_index("row") % 2 == 0
+    even_at = pl.multiple_of(jnp.where(after, 2 * height, 0), 8)
+    odd_at = pl.multiple_of(jnp.where(after, 0, 2 * height), 8)
+
+    def step(index, slot):
+        tile = tile_of(index, group, tiles, core)
+        offset = offset_ref[tile]
+        stack[slot, pl.ds(even_at, height)] = even_ref[begin + index]
+        stack[slot, pl.ds(odd_at, height)] = odd_ref[begin + index]
+        stack[slot, height : 2 * height] = own_ref[begin + index]
+        weights = weights_ref[:, pl.ds(pl.multiple_of(tile * LANES, LANES), LANES)]
+
+        def picked(row):
+            lifted = row + 2
+            first = lifted // 2 * height + lifted % 2
+            return stack[slot, pl.ds(first, views, stride=2), :]
+
+        terms = [picked(row + offset) for row in range(3)]
+        for row in range(2):
+            out_ref[index, row] = weights[0:1] * terms[row] + weights[1:2] * terms[row + 1]
+
+    unrolled(step, count)
+
+
+def interpolate_rows(group, held, tiles, offset, even, odd, own, weights, after, cost):
+    height = own.shape[1]
+    return call(
+        functools.partial(rows_body, group, held, tiles),
+        [f32(group[1], 2, height // 2, LANES)],
+        [pltpu.VMEM((2, 3 * height + 8, LANES), jnp.float32)],
         (offset, odd, even, own, weights),
-        after=after,
+        cost,
+        after,
     )[0]
 
 
@@ -289,7 +290,7 @@
         [f32(count, parts, rows, chip_views // 2, LANES)] * 2,
         [pltpu.VMEM((2, 3 * rows, chip_views, LANES), jnp.float32)],
         (offset, odd, even, own, weights),
-        cycles(4000),
+        cycles(LAST_COST),
     )
 
 
@@ -349,14 +350,15 @@
     pl.when((core == 1) & (side == 1))(lambda: run(across_y_last, got_ref, own_ref))
 
 
-def select_views(group, tiles, view_offset, conj_offset, own, got, after=()):
+def select_views(group, tiles, view_offset, conj_offset, own, got, after=(), cost=SHORT):
     count, rows, chip_views, _ = own.shape
     return call(
         functools.partial(select_body, group, tiles),
         [f32(count, rows, SLOTS, LANES)],
         [],
         (view_offset, conj_offset, own, got),
-        after=after,
+        cost,
+        after,
     )[0]
 
 
@@ -459,10 +461,10 @@
     return spans
 
 
-def filter_body(groups, number, tiles, high_ref, low_ref, *refs):
-    parts = refs[: 4 if number else 2]
+def filter_body(groups, held, number, tiles, high_ref, low_ref, *refs):
+    parts = refs[: 2 * len(held)]
     if number:
-        earlier, out_any, mixed, high_all, low_all, result, sems = refs[4:]
+        earlier, out_any, mixed, high_all, low_all, result, sems = refs[2 * len(held) :]
     else:
         result, mixed, high_all, low_all = refs[2:]
     views = result.shape[0]
@@ -482,14 +484,15 @@
             high_all[part, tile + 1] = high
             low_all[part, tile + 1] = low
 
-    for ref, owner in zip(parts[:2], (core, 1 - core)):
-        unrolled(functools.partial(gather, groups[number], ref, owner), groups[number][1])
-    if number:
-        half = groups[number - 1][1]
-        for ref, owner in zip(parts[2:], (core, 1 - core)):
-            begin = jnp.where(owner == 0, half - 2, 0)
+    for place, group in enumerate(held):
+        pair = parts[2 * place : 2 * place + 2]
+        for ref, owner in zip(pair, (core, 1 - core)):
+            if group[0] >= groups[number][0]:
+                unrolled(functools.partial(gather, group, ref, owner), group[1])
+                continue
+            begin = jnp.where(owner == 0, group[1] - 2, 0)
             for i in range(2):
-                gather(groups[number - 1], ref, owner, begin + i, i)
+                gather(group, ref, owner, begin + i, i)
 
     copies = []
 
@@ -527,18 +530,20 @@
         copy.wait()
 
 
-def ramp_filter(groups, number, tiles, keeps, gots, out):
+def ramp_filter(groups, held, number, tiles, keeps, gots, out):
     views = keeps[0].shape[3]
-    args = [*filter_matrix(), keeps[number], gots[number]]
+    args = [*filter_matrix()]
+    for keep, got in zip(keeps, gots):
+        args += [keep, got]
     stored = pltpu.VMEM((2, tiles + 2, 2 * views, LANES), jnp.bfloat16)
     scratch = [pltpu.VMEM((2, 2, 2 * views + 8, LANES), jnp.float32), stored, stored]
     shape = f32(views, 2, 2 * tiles * LANES)
     if number:
-        args += [keeps[number - 1], gots[number - 1], out]
+        args.append(out)
         spans = sum(len(stage_spans(groups, i, tiles)) for i in range(2))
         scratch += [pltpu.VMEM(shape.shape, jnp.float32), pltpu.SemaphoreType.DMA((spans,))]
     return call(
-        functools.partial(filter_body, groups, number, tiles),
+        functools.partial(filter_body, groups, held, number, tiles),
         [shape],
         scratch,
         args,
@@ -594,39 +599,39 @@
     tiles = col_weights.shape[0]
     exchanged = lax.axis_size("ang") == 8
     offsets = (view_offset, conj_offset)
-    groups = (OUTER, INNER)
+    outer, *others = GROUPS
+    inner = (others[0][0], sum(half for _, half in others))
 
     beside = swapped(sinogram)
-    inner, weights, sino = resample_own(INNER, col_start, col_weights, sinogram)
-    inner = resample_rest(INNER, tiles, col_start, weights, beside, inner)
-    inner_halo = row_pairs(inner)
-    outer = resample_apart(OUTER, tiles, col_start, weights, sino, beside, (inner,))
-
-    first = first_exchange(outer)
-    chosen = [select_views(OUTER, tiles, *offsets, outer, got) for got in first]
-    parts = second_exchange(outer, first, chosen)
-    (outer,) = interpolate_views(
-        OUTER, tiles, exchanged, *offsets, ang_weights, parts, 1, cycles(5000)
+    own, weights, sino = resample_own(inner, col_start, col_weights, sinogram)
+    resampled = resample_rest(inner, tiles, col_start, weights, beside, own)
+    halo = row_pairs(resampled)
+    block = resample_apart(outer, tiles, col_start, weights, sino, beside, (resampled,))
+
+    first = first_exchange(block)
+    chosen = [select_views(outer, tiles, *offsets, block, got) for got in first]
+    parts = second_exchange(block, first, chosen)
+    blocks = [
+        interpolate_rows(group, inner, tiles, row_offset, *halo, resampled, row_weights, chosen, cost)
+        for group, cost in zip(others, (cycles(10000), cycles(1)))
+    ]
+    (whole,) = interpolate_views(
+        outer, tiles, exchanged, *offsets, ang_weights, parts, 1, cycles(1), tuple(blocks)
     )
-    outer_halo = row_pairs(outer)
-
-    inner = interpolate_rows(INNER, tiles, row_offset, *inner_halo, inner, row_weights, chosen)
-    first = first_exchange(inner)
-    chosen = [select_views(INNER, tiles, *offsets, inner, got, (outer,)) for got in first]
-    parts = second_exchange(inner, first, chosen)
-
-    outer_keep, send = interpolate_rows_last(
-        OUTER, tiles, row_offset, *outer_halo, outer, row_weights
-    )
-    outer_got = swapped(send)
-    out = ramp_filter(groups, 0, tiles, [outer_keep], [outer_got], None)
-    inner_keep, send = interpolate_views(
-        INNER, tiles, exchanged, *offsets, ang_weights, parts, 2
-    )
-    inner_got = swapped(send)
-    return ramp_filter(
-        groups, 1, tiles, (outer_keep, inner_keep), (outer_got, inner_got), out
-    )
+    outer_halo = row_pairs(whole)
+    keep, send = interpolate_rows_last(outer, tiles, row_offset, *outer_halo, whole, row_weights)
+    keeps, gots = [keep], [swapped(send)]
+
+    for group, block, cost in zip(others, blocks, (SHORT, cycles(8000))):
+        first = first_exchange(block)
+        selected = [select_views(group, tiles, *offsets, block, got, (whole,), cost) for got in first]
+        parts = second_exchange(block, first, selected)
+        keep, send = interpolate_views(group, tiles, exchanged, *offsets, ang_weights, parts, 2)
+        keeps.append(keep)
+        gots.append(swapped(send))
+    stages = (outer, inner)
+    out = ramp_filter(stages, GROUPS[:1], 0, tiles, keeps[:1], gots[:1], None)
+    return ramp_filter(stages, GROUPS, 1, tiles, keeps, gots, out)
 
 
 def solution(mesh):

time: 56.7 us -> 55.8 us (0.984)
  waiting for transfers between devices: 27 us -> 22.6 us
  starting transfers between devices: 15.8 us -> 17.6 us
  Pallas kernels: 13.6 us -> 15.3 us
    ppermute x11 -> x14, waiting for transfers between devices: 27 us -> 22.6 us  [permuted(): lax.ppermute(value, axis, [(i, j) for i, j in pairs if 0 <= j < count])]
    ppermute x11 -> x14, starting transfers between devices: 15.8 us -> 17.6 us  [permuted(): lax.ppermute(value, axis, [(i, j) for i, j in pairs if 0 <= j < count])]
    pallas_call x11 -> x14, Pallas kernels: 13.6 us -> 15.3 us  [call(): pl.pallas_call(kernel, out_shape=outs, in_specs=[*specs, *[ANY] * len(aft...]
  transfers between devices with their start and end apart: 11 -> 14, of which waited for: 10 -> 9; matrix products, arithmetic and copies ran while one was open for 0% -> 0% of each run, Pallas kernels for 17% -> 19%
where the time goes in v7:
time: 55.8 us; the launch traced here: 55.6 us
  waiting for transfers between devices  22.6 us (41%)
  starting transfers between devices  17.6 us (32%)
  Pallas kernels  15.3 us (27%)
    ppermute x14, waiting for transfers between devices, permuted(): lax.ppermute(value, axis, [(i, j) for i, j in pairs if 0 <= j < count])  22.6 us
    ppermute x14, starting transfers between devices, permuted(): lax.ppermute(value, axis, [(i, j) for i, j in pairs if 0 <= j < count])  17.6 us
    pallas_call x14, Pallas kernels, call(): pl.pallas_call(kernel, out_shape=outs, in_specs=[*specs, *[ANY] * len(aft...  15.3 us
  transfers between devices with their start and end apart: 14, of which 9 were waited for; matrix products, arithmetic and copies ran while one was open for 0% of the time, Pallas kernels for 19%

profile of v7, /device:TPU:11, one launch (start us, length us, event | category | flops | bytes accessed | tf_op | source)
XLA Modules:
  0.0 55.6 jit_solution(3261965342589756638)
XLA Ops:
  0.7 2.0 %shard_map.118 = (f32[11,64,128]{2,1,0:T(8,128)S(1)}, bf16[16,256,128]{2,1,0:T(8,128)(2,1)S(1)}, f32[32,2,4096]{2,1,0:T(2,128)S(1)}) custom-call(s32[32]{0:T(128)} %refs_0_.16, bf16[32,256,128]{2,1,0:T(8,128)(2,1)} %refs_1_.9, f32[32,2,4096]{2,1,0:T(2,128)} %refs_2_.4), custom_call_target="tpu_custom_call" | custom-call | flops 1 | bytes 1 | tf_op jit(solution)/shard_map/pallas_call | solution.py:36
  3.2 1.1 %shard_map.119.refs_4_.refs_3_ = f32[11,128,128]{2,1,0:T(8,128)S(1)} custom-call(s32[32]{0:T(128)S(1)} %copy-done.7, bf16[16,256,128]{2,1,0:T(8,128)(2,1)S(1)} %get-tuple-element.14.refs_1_, f32[32,2,4096]{2,1,0:T(2,128)S(1)} %collective-permute-done.refs_2_.refs_3_, f32[11,64,128]{2,1,0:T(8,128)S(1)} %get-tuple-element.16.refs_3_), custom_call_target="tpu_custom_call" | custom-call | flops 1 | bytes 1 | tf_op jit(solution)/shard_map/pallas_call | solution.py:36
  4.6 4.3 %collective-permute-start.3 = (f32[11,128,128]{2,1,0:T(8,128)S(1)}, f32[11,128,128]{2,1,0:T(8,128)S(1)}, u32[]{:S(2)}, u32[]{:S(2)}) collective-permute-start(f32[11,128,128]{2,1,0:T(8,128)S(1)} %shard_map.119.refs_4_.refs_3_), channel_id=1, source_target_pairs={{1,2},{2,1},{5,6},{6,5},{9,10},{10,9},{13,14},{14,13},{17,18},{18,... | collective-permute-start | bytes 2162696 | tf_op jit(solution)/shard_map/ppermute | solution.py:558
  8.9 1.1 %shard_map.120.refs_2_.refs_3_ = f32[5,2,64,128]{3,2,1,0:T(8,128)S(1)} custom-call(s32[32]{0:T(128)S(1)} %copy-done.7, bf16[16,256,128]{2,1,0:T(8,128)(2,1)S(1)} %get-tuple-element.14.refs_1_, f32[32,2,4096]{2,1,0:T(2,128)S(1)} %get-tuple-element.15.refs_2_, f32[32,2,4096]{2,1,0:T(2,128)S(1)} %collective-permute-done.refs_2_.refs_3_, ...), custom_call_target="tpu_custom_call" | custom-call | flops 2097152000 | bytes 1 | tf_op jit(solution)/shard_map/pallas_call | solution.py:36
  10.4 6.0 %collective-permute-done.1.refs_3_.refs_4_ = f32[5,2,64,128]{3,2,1,0:T(8,128)S(1)} collective-permute-done((f32[5,2,64,128]{3,2,1,0:T(8,128)S(1)}, f32[5,2,64,128]{3,2,1,0:T(8,128)S(1)}, u32[]{:S(2)}, u32[]{:S(2)}) %collective-permute-start.1) | collective-permute-done | bytes 327712 | tf_op jit(solution)/shard_map/ppermute | solution.py:558
  17.0 1.3 %collective-permute-start.2 = (f32[5,2,88,128]{3,2,1,0:T(8,128)S(1)}, f32[5,2,88,128]{3,2,1,0:T(8,128)S(1)}, u32[]{:S(2)}, u32[]{:S(2)}) collective-permute-start(f32[5,2,88,128]{3,2,1,0:T(8,128)S(1)} %shard_map.121.refs_5_), channel_id=1, source_target_pairs={{0,8},{4,20},{8,0},{12,28},{16,24},{20,4},{24,16},{28,12},{1,9},{5... | collective-permute-start | bytes 1351688 | tf_op jit(solution)/shard_map/ppermute | solution.py:558
  18.3 3.4 %collective-permute-done.4.refs_2_ = f32[11,128,128]{2,1,0:T(8,128)S(1)} collective-permute-done((f32[11,128,128]{2,1,0:T(8,128)S(1)}, f32[11,128,128]{2,1,0:T(8,128)S(1)}, u32[]{:S(2)}, u32[]{:S(2)}) %collective-permute-start.4) | collective-permute-done | bytes 720928 | tf_op jit(solution)/shard_map/ppermute | solution.py:558
  21.7 3.0 %collective-permute-done.3.refs_1_ = f32[11,128,128]{2,1,0:T(8,128)S(1)} collective-permute-done((f32[11,128,128]{2,1,0:T(8,128)S(1)}, f32[11,128,128]{2,1,0:T(8,128)S(1)}, u32[]{:S(2)}, u32[]{:S(2)}) %collective-permute-start.3) | collective-permute-done | bytes 720928 | tf_op jit(solution)/shard_map/ppermute | solution.py:558
  24.8 0.7 %shard_map.122.refs_6_.refs_2_.refs_3_ = f32[6,2,64,128]{3,2,1,0:T(8,128)S(1)} custom-call(s32[32]{0:T(128)S(1)} %copy-done.6, f32[11,128,128]{2,1,0:T(8,128)S(1)} %collective-permute-done.3.refs_1_, f32[11,128,128]{2,1,0:T(8,128)S(1)} %collective-permute-done.4.refs_2_, f32[11,128,128]{2,1,0:T(8,128)S(1)} %shard_map.119.refs_4_.refs_3_, ...), custom_call_target="tpu_custom_call" | custom-call | flops 5242880000 | bytes 1 | tf_op jit(solution)/shard_map/pallas_call | solution.py:36
  25.8 0.7 %shard_map.123.refs_7_.refs_2_.refs_3_ = f32[5,2,64,128]{3,2,1,0:T(8,128)S(1)} custom-call(s32[32]{0:T(128)S(1)} %copy-done.6, f32[11,128,128]{2,1,0:T(8,128)S(1)} %collective-permute-done.3.refs_1_, f32[11,128,128]{2,1,0:T(8,128)S(1)} %collective-permute-done.4.refs_2_, f32[11,128,128]{2,1,0:T(8,128)S(1)} %shard_map.119.refs_4_.refs_3_, ...), custom_call_target="tpu_custom_call" | custom-call | flops 524288 | bytes 1 | tf_op jit(solution)/shard_map/pallas_call | solution.py:36
  26.5 1.3 %collective-permute-start.11 = (f32[5,2,64,128]{3,2,1,0:T(8,128)S(1)}, f32[5,2,64,128]{3,2,1,0:T(8,128)S(1)}, u32[]{:S(2)}, u32[]{:S(2)}) collective-permute-start(f32[5,2,64,128]{3,2,1,0:T(8,128)S(1)} %shard_map.123.refs_7_.refs_2_.refs_3_), channel_id=1, source_target_pairs={{0,16},{4,12},{8,24},{12,4},{16,0},{20,28},{24,8},{28,20},{1,17},{... | collective-permute-start | bytes 983048 | tf_op jit(solution)/shard_map/ppermute | solution.py:558
  27.8 0.9 %shard_map.124.refs_3_.refs_4_ = f32[5,2,2,64,128]{4,3,2,1,0:T(8,128)S(1)} custom-call(s32[32]{0:T(128)S(1)} %copy-done.4, s32[32]{0:T(128)S(1)} %copy-done.5, f32[4,4096]{1,0:T(4,128)S(1)} %copy-done, f32[5,2,64,128]{3,2,1,0:T(8,128)S(1)} %shard_map.120.refs_2_.refs_3_, f32[5,2,64,128]{3,2,1,0:T(8,128)S(1)} %collective-permute-done.1.refs_3_.refs_4_, ...), custom_call_target="tpu_custom_call" | custom-call | flops 524288 | bytes 1 | tf_op jit(solution)/shard_map/pallas_call | solution.py:36
  28.8 3.0 %collective-permute-start.5 = (f32[5,2,2,64,128]{4,3,2,1,0:T(8,128)S(1)}, f32[5,2,2,64,128]{4,3,2,1,0:T(8,128)S(1)}, u32[]{:S(2)}, u32[]{:S(2)}) collective-permute-start(f32[5,2,2,64,128]{4,3,2,1,0:T(8,128)S(1)} %shard_map.124.refs_3_.refs_4_), channel_id=1, source_target_pairs={{1,2},{2,1},{5,6},{6,5},{9,10},{10,9},{13,14},{14,13},{17,18},{18,... | collective-permute-start | bytes 1966088 | tf_op jit(solution)/shard_map/ppermute | solution.py:558
  33.1 1.3 %collective-permute-start.9 = (f32[6,2,88,128]{3,2,1,0:T(8,128)S(1)}, f32[6,2,88,128]{3,2,1,0:T(8,128)S(1)}, u32[]{:S(2)}, u32[]{:S(2)}) collective-permute-start(f32[6,2,88,128]{3,2,1,0:T(8,128)S(1)} %shard_map.126), channel_id=1, source_target_pairs={{0,8},{4,20},{8,0},{12,28},{16,24},{20,4},{24,16},{28,12},{1,9},{5... | collective-permute-start | bytes 1622024 | tf_op jit(solution)/shard_map/ppermute | solution.py:558
  34.4 1.6 %collective-permute-done.11.refs_3_.refs_4_ = f32[5,2,64,128]{3,2,1,0:T(8,128)S(1)} collective-permute-done((f32[5,2,64,128]{3,2,1,0:T(8,128)S(1)}, f32[5,2,64,128]{3,2,1,0:T(8,128)S(1)}, u32[]{:S(2)}, u32[]{:S(2)}) %collective-permute-start.11) | collective-permute-done | bytes 327712 | tf_op jit(solution)/shard_map/ppermute | solution.py:558
  36.7 1.3 %collective-permute-start.12 = (f32[5,2,88,128]{3,2,1,0:T(8,128)S(1)}, f32[5,2,88,128]{3,2,1,0:T(8,128)S(1)}, u32[]{:S(2)}, u32[]{:S(2)}) collective-permute-start(f32[5,2,88,128]{3,2,1,0:T(8,128)S(1)} %shard_map.128), channel_id=1, source_target_pairs={{0,8},{4,20},{8,0},{12,28},{16,24},{20,4},{24,16},{28,12},{1,9},{5... | collective-permute-start | bytes 1351688 | tf_op jit(solution)/shard_map/ppermute | solution.py:558
  38.0 5.2 %collective-permute-done.6.refs_2_ = f32[5,2,2,64,128]{4,3,2,1,0:T(8,128)S(1)} collective-permute-done((f32[5,2,2,64,128]{4,3,2,1,0:T(8,128)S(1)}, f32[5,2,2,64,128]{4,3,2,1,0:T(8,128)S(1)}, u32[]{:S(2)}, u32[]{:S(2)}) %collective-permute-start.6) | collective-permute-done | bytes 655392 | tf_op jit(solution)/shard_map/ppermute | solution.py:558
  43.2 1.9 %collective-permute-done.5.refs_1_ = f32[5,2,2,64,128]{4,3,2,1,0:T(8,128)S(1)} collective-permute-done((f32[5,2,2,64,128]{4,3,2,1,0:T(8,128)S(1)}, f32[5,2,2,64,128]{4,3,2,1,0:T(8,128)S(1)}, u32[]{:S(2)}, u32[]{:S(2)}) %collective-permute-start.5) | collective-permute-done | bytes 655392 | tf_op jit(solution)/shard_map/ppermute | solution.py:558
  45.1 0.8 %shard_map.125 = (f32[5,2,2,32,128]{4,3,2,1,0:T(8,128)S(1)}, f32[5,2,2,32,128]{4,3,2,1,0:T(8,128)S(1)}) custom-call(s32[32]{0:T(128)S(1)} %copy-done.6, f32[5,2,2,64,128]{4,3,2,1,0:T(8,128)S(1)} %collective-permute-done.5.refs_1_, f32[5,2,2,64,128]{4,3,2,1,0:T(8,128)S(1)} %collective-permute-done.6.refs_2_, ...), custom_call_target="tpu_custom_call" | custom-call | flops 524288 | bytes 1 | tf_op jit(solution)/shard_map/pallas_call | solution.py:36
  45.9 2.8 %collective-permute-start.7 = (f32[5,2,2,32,128]{4,3,2,1,0:T(8,128)S(1)}, f32[5,2,2,32,128]{4,3,2,1,0:T(8,128)S(1)}, u32[]{:S(2)}, u32[]{:S(2)}) collective-permute-start(f32[5,2,2,32,128]{4,3,2,1,0:T(8,128)S(1)} %get-tuple-element.18), channel_id=1, source_target_pairs={{0,4},{4,0},{8,12},{12,8},{16,20},{20,16},{24,28},{28,24},{1,5},{5... | collective-permute-start | bytes 983048 | tf_op jit(solution)/shard_map/ppermute | solution.py:558
  48.7 0.9 %shard_map.127 = (f32[6,2,2,32,128]{4,3,2,1,0:T(8,128)S(1)}, f32[6,2,2,32,128]{4,3,2,1,0:T(8,128)S(1)}) custom-call(s32[32]{0:T(128)S(1)} %copy-done.4, s32[32]{0:T(128)S(1)} %copy-done.5, f32[4,4096]{1,0:T(4,128)S(1)} %copy-done, f32[6,2,64,128]{3,2,1,0:T(8,128)S(1)} %shard_map.122.refs_6_.refs_2_.refs_3_, ...), custom_call_target="tpu_custom_call" | custom-call | flops 1 | bytes 1 | tf_op jit(solution)/shard_map/pallas_call | solution.py:36
  49.7 0.9 %shard_map.129 = (f32[5,2,2,32,128]{4,3,2,1,0:T(8,128)S(1)}, f32[5,2,2,32,128]{4,3,2,1,0:T(8,128)S(1)}) custom-call(s32[32]{0:T(128)S(1)} %copy-done.4, s32[32]{0:T(128)S(1)} %copy-done.5, f32[4,4096]{1,0:T(4,128)S(1)} %copy-done, f32[5,2,64,128]{3,2,1,0:T(8,128)S(1)} %shard_map.123.refs_7_.refs_2_.refs_3_, ...), custom_call_target="tpu_custom_call" | custom-call | flops 1 | bytes 1 | tf_op jit(solution)/shard_map/pallas_call | solution.py:36
  51.1 0.9 %shard_map.130.refs_8_ = f32[32,2,8192]{2,1,0:T(2,128)S(1)} custom-call(bf16[768,256]{1,0:T(8,128)(2,1)S(1)} %copy-done.2, bf16[768,256]{1,0:T(8,128)(2,1)S(1)} %copy-done.1, f32[5,2,2,32,128]{4,3,2,1,0:T(8,128)S(1)} %get-tuple-element.17.refs_2_, f32[5,2,2,32,128]{4,3,2,1,0:T(8,128)S(1)} %collective-permute-done.7.refs_3_), custom_call_target="tpu_custom_call" | custom-call | flops 3145728000 | bytes 1 | tf_op jit(solution)/shard_map/pallas_call | solution.py:36
  52.3 3.3 %shard_map.131 = f32[32,2,8192]{2,1,0:T(2,128)} custom-call(bf16[768,256]{1,0:T(8,128)(2,1)S(1)} %copy-done.2, bf16[768,256]{1,0:T(8,128)(2,1)S(1)} %copy-done.1, f32[5,2,2,32,128]{4,3,2,1,0:T(8,128)S(1)} %get-tuple-element.17.refs_2_, f32[5,2,2,32,128]{4,3,2,1,0:T(8,128)S(1)} %collective-permute-done.7.refs_3_, ...), custom_call_target="tpu_custom_call" | custom-call | flops 1 | bytes 1 | tf_op jit(solution)/shard_map/pallas_call | solution.py:36
  (34 shorter events, 5.7 us)
Async XLA Ops:
  0.0 3.2 %copy-start.7 = (s32[32]{0:T(128)S(1)}, s32[32]{0:T(128)}, u32[]{:S(2)}) copy-start(s32[32]{0:T(128)} %refs_0_.16) | copy-start | bytes 388
  0.0 3.2 %collective-permute-start = (f32[32,2,4096]{2,1,0:T(2,128)}, f32[32,2,4096]{2,1,0:T(2,128)S(1)}, u32[]{:S(2)}, u32[]{:S(2)}) collective-permute-start(f32[32,2,4096]{2,1,0:T(2,128)} %refs_2_.4), channel_id=1, source_target_pairs={{0,4},{4,0},{8,12},{12,8},{16,20},{20,16},{24,28},{28,24},{1,5},{5... | collective-permute-start | bytes 3145736 | tf_op jit(solution)/shard_map/ppermute | solution.py:558
  4.3 17.4 %collective-permute-start.4 = (f32[11,128,128]{2,1,0:T(8,128)S(1)}, f32[11,128,128]{2,1,0:T(8,128)S(1)}, u32[]{:S(2)}, u32[]{:S(2)}) collective-permute-start(f32[11,128,128]{2,1,0:T(8,128)S(1)} %shard_map.119.refs_4_.refs_3_), channel_id=1, source_target_pairs={{0,1},{1,0},{2,3},{3,2},{4,5},{5,4},{6,7},{7,6},{8,9},{9,8},{10,11... | collective-permute-start | bytes 2162696 | tf_op jit(solution)/shard_map/ppermute | solution.py:558
  4.6 20.2 %collective-permute-start.3 = (f32[11,128,128]{2,1,0:T(8,128)S(1)}, f32[11,128,128]{2,1,0:T(8,128)S(1)}, u32[]{:S(2)}, u32[]{:S(2)}) collective-permute-start(f32[11,128,128]{2,1,0:T(8,128)S(1)} %shard_map.119.refs_4_.refs_3_), channel_id=1, source_target_pairs={{1,2},{2,1},{5,6},{6,5},{9,10},{10,9},{13,14},{14,13},{17,18},{18,... | collective-permute-start | bytes 2162696 | tf_op jit(solution)/shard_map/ppermute | solution.py:558
  8.9 7.5 %copy-start.4 = (s32[32]{0:T(128)S(1)}, s32[32]{0:T(128)}, u32[]{:S(2)}) copy-start(s32[32]{0:T(128)} %refs_0_.25) | copy-start | bytes 388
  8.9 7.5 %copy-start.5 = (s32[32]{0:T(128)S(1)}, s32[32]{0:T(128)}, u32[]{:S(2)}) copy-start(s32[32]{0:T(128)} %refs_1_.15) | copy-start | bytes 388
  8.9 15.8 %copy-start.3 = (f32[2,4096]{1,0:T(2,128)S(1)}, f32[2,4096]{1,0:T(2,128)}, u32[]{:S(2)}) copy-start(f32[2,4096]{1,0:T(2,128)} %refs_4_.5) | copy-start | bytes 98308
  8.9 15.8 %copy-start.6 = (s32[32]{0:T(128)S(1)}, s32[32]{0:T(128)}, u32[]{:S(2)}) copy-start(s32[32]{0:T(128)} %refs_0_.21) | copy-start | bytes 388
  10.1 6.3 %collective-permute-start.1 = (f32[5,2,64,128]{3,2,1,0:T(8,128)S(1)}, f32[5,2,64,128]{3,2,1,0:T(8,128)S(1)}, u32[]{:S(2)}, u32[]{:S(2)}) collective-permute-start(f32[5,2,64,128]{3,2,1,0:T(8,128)S(1)} %shard_map.120.refs_2_.refs_3_), channel_id=1, source_target_pairs={{0,16},{4,12},{8,24},{12,4},{16,0},{20,28},{24,8},{28,20},{1,17},{... | collective-permute-start | bytes 983048 | tf_op jit(solution)/shard_map/ppermute | solution.py:558
  17.0 10.8 %collective-permute-start.2 = (f32[5,2,88,128]{3,2,1,0:T(8,128)S(1)}, f32[5,2,88,128]{3,2,1,0:T(8,128)S(1)}, u32[]{:S(2)}, u32[]{:S(2)}) collective-permute-start(f32[5,2,88,128]{3,2,1,0:T(8,128)S(1)} %shard_map.121.refs_5_), channel_id=1, source_target_pairs={{0,8},{4,20},{8,0},{12,28},{16,24},{20,4},{24,16},{28,12},{1,9},{5... | collective-permute-start | bytes 1351688 | tf_op jit(solution)/shard_map/ppermute | solution.py:558
  25.5 2.3 %copy-start = (f32[4,4096]{1,0:T(4,128)S(1)}, f32[4,4096]{1,0:T(4,128)}, u32[]{:S(2)}) copy-start(f32[4,4096]{1,0:T(4,128)} %refs_2_.7) | copy-start | bytes 196612
  25.5 7.0 %collective-permute-start.8 = (f32[6,2,64,128]{3,2,1,0:T(8,128)S(1)}, f32[6,2,64,128]{3,2,1,0:T(8,128)S(1)}, u32[]{:S(2)}, u32[]{:S(2)}) collective-permute-start(f32[6,2,64,128]{3,2,1,0:T(8,128)S(1)} %shard_map.122.refs_6_.refs_2_.refs_3_), channel_id=1, source_target_pairs={{0,16},{4,12},{8,24},{12,4},{16,0},{20,28},{24,8},{28,20},{1,17},{... | collective-permute-start | bytes 1179656 | tf_op jit(solution)/shard_map/ppermute | solution.py:558
  26.5 9.5 %collective-permute-start.11 = (f32[5,2,64,128]{3,2,1,0:T(8,128)S(1)}, f32[5,2,64,128]{3,2,1,0:T(8,128)S(1)}, u32[]{:S(2)}, u32[]{:S(2)}) collective-permute-start(f32[5,2,64,128]{3,2,1,0:T(8,128)S(1)} %shard_map.123.refs_7_.refs_2_.refs_3_), channel_id=1, source_target_pairs={{0,16},{4,12},{8,24},{12,4},{16,0},{20,28},{24,8},{28,20},{1,17},{... | collective-permute-start | bytes 983048 | tf_op jit(solution)/shard_map/ppermute | solution.py:558
  28.7 14.5 %collective-permute-start.6 = (f32[5,2,2,64,128]{4,3,2,1,0:T(8,128)S(1)}, f32[5,2,2,64,128]{4,3,2,1,0:T(8,128)S(1)}, u32[]{:S(2)}, u32[]{:S(2)}) collective-permute-start(f32[5,2,2,64,128]{4,3,2,1,0:T(8,128)S(1)} %shard_map.124.refs_3_.refs_4_), channel_id=1, source_target_pairs={{0,1},{1,0},{2,3},{3,2},{4,5},{5,4},{6,7},{7,6},{8,9},{9,8},{10,11... | collective-permute-start | bytes 1966088 | tf_op jit(solution)/shard_map/ppermute | solution.py:558
  28.8 16.3 %collective-permute-start.5 = (f32[5,2,2,64,128]{4,3,2,1,0:T(8,128)S(1)}, f32[5,2,2,64,128]{4,3,2,1,0:T(8,128)S(1)}, u32[]{:S(2)}, u32[]{:S(2)}) collective-permute-start(f32[5,2,2,64,128]{4,3,2,1,0:T(8,128)S(1)} %shard_map.124.refs_3_.refs_4_), channel_id=1, source_target_pairs={{1,2},{2,1},{5,6},{6,5},{9,10},{10,9},{13,14},{14,13},{17,18},{18,... | collective-permute-start | bytes 1966088 | tf_op jit(solution)/shard_map/ppermute | solution.py:558
  33.1 15.5 %collective-permute-start.9 = (f32[6,2,88,128]{3,2,1,0:T(8,128)S(1)}, f32[6,2,88,128]{3,2,1,0:T(8,128)S(1)}, u32[]{:S(2)}, u32[]{:S(2)}) collective-permute-start(f32[6,2,88,128]{3,2,1,0:T(8,128)S(1)} %shard_map.126), channel_id=1, source_target_pairs={{0,8},{4,20},{8,0},{12,28},{16,24},{20,4},{24,16},{28,12},{1,9},{5... | collective-permute-start | bytes 1622024 | tf_op jit(solution)/shard_map/ppermute | solution.py:558
  36.6 14.4 %copy-start.1 = (bf16[768,256]{1,0:T(8,128)(2,1)S(1)}, bf16[768,256]{1,0:T(8,128)(2,1)}, u32[]{:S(2)}) copy-start(bf16[768,256]{1,0:T(8,128)(2,1)} %constant.5.clone.refs_1_) | copy-start | bytes 1179652
  36.6 14.4 %copy-start.2 = (bf16[768,256]{1,0:T(8,128)(2,1)S(1)}, bf16[768,256]{1,0:T(8,128)(2,1)}, u32[]{:S(2)}) copy-start(bf16[768,256]{1,0:T(8,128)(2,1)} %constant.4.clone.refs_0_) | copy-start | bytes 1179652
  36.7 13.0 %collective-permute-start.12 = (f32[5,2,88,128]{3,2,1,0:T(8,128)S(1)}, f32[5,2,88,128]{3,2,1,0:T(8,128)S(1)}, u32[]{:S(2)}, u32[]{:S(2)}) collective-permute-start(f32[5,2,88,128]{3,2,1,0:T(8,128)S(1)} %shard_map.128), channel_id=1, source_target_pairs={{0,8},{4,20},{8,0},{12,28},{16,24},{20,4},{24,16},{28,12},{1,9},{5... | collective-permute-start | bytes 1351688 | tf_op jit(solution)/shard_map/ppermute | solution.py:558
  45.9 5.2 %collective-permute-start.7 = (f32[5,2,2,32,128]{4,3,2,1,0:T(8,128)S(1)}, f32[5,2,2,32,128]{4,3,2,1,0:T(8,128)S(1)}, u32[]{:S(2)}, u32[]{:S(2)}) collective-permute-start(f32[5,2,2,32,128]{4,3,2,1,0:T(8,128)S(1)} %get-tuple-element.18), channel_id=1, source_target_pairs={{0,4},{4,0},{8,12},{12,8},{16,20},{20,16},{24,28},{28,24},{1,5},{5... | collective-permute-start | bytes 983048 | tf_op jit(solution)/shard_map/ppermute | solution.py:558
  49.6 2.8 %collective-permute-start.10 = (f32[6,2,2,32,128]{4,3,2,1,0:T(8,128)S(1)}, f32[6,2,2,32,128]{4,3,2,1,0:T(8,128)S(1)}, u32[]{:S(2)}, u32[]{:S(2)}) collective-permute-start(f32[6,2,2,32,128]{4,3,2,1,0:T(8,128)S(1)} %get-tuple-element.20), channel_id=1, source_target_pairs={{0,4},{4,0},{8,12},{12,8},{16,20},{20,16},{24,28},{28,24},{1,5},{5... | collective-permute-start | bytes 1179656 | tf_op jit(solution)/shard_map/ppermute | solution.py:558
  50.5 1.8 %collective-permute-start.13 = (f32[5,2,2,32,128]{4,3,2,1,0:T(8,128)S(1)}, f32[5,2,2,32,128]{4,3,2,1,0:T(8,128)S(1)}, u32[]{:S(2)}, u32[]{:S(2)}) collective-permute-start(f32[5,2,2,32,128]{4,3,2,1,0:T(8,128)S(1)} %get-tuple-element.22), channel_id=1, source_target_pairs={{0,4},{4,0},{8,12},{12,8},{16,20},{20,16},{24,28},{28,24},{1,5},{5... | collective-permute-start | bytes 983048 | tf_op jit(solution)/shard_map/ppermute | solution.py:558

commit v8 on v7

--- a/solution.py
+++ b/solution.py
@@ -215,33 +215,35 @@
     )[0]
 
 
-def rows_body(group, held, tiles, offset_ref, odd_ref, even_ref, own_ref, weights_ref, out_ref, stack):
+def rows_body(group, held, tiles, offset_ref, odd_ref, even_ref, own_ref, weights_ref, out_ref):
     count, height = out_ref.shape[0], own_ref.shape[1]
     views = height // 2
     _, core = position()
     begin = tile_of(0, group, tiles, core) - tile_of(0, held, tiles, core)
-    after = lax.axis_index("row") % 2 == 0
-    even_at = pl.multiple_of(jnp.where(after, 2 * height, 0), 8)
-    odd_at = pl.multiple_of(jnp.where(after, 0, 2 * height), 8)
-
-    def step(index, slot):
-        tile = tile_of(index, group, tiles, core)
-        offset = offset_ref[tile]
-        stack[slot, pl.ds(even_at, height)] = even_ref[begin + index]
-        stack[slot, pl.ds(odd_at, height)] = odd_ref[begin + index]
-        stack[slot, height : 2 * height] = own_ref[begin + index]
-        weights = weights_ref[:, pl.ds(pl.multiple_of(tile * LANES, LANES), LANES)]
-
-        def picked(row):
-            lifted = row + 2
-            first = lifted // 2 * height + lifted % 2
-            return stack[slot, pl.ds(first, views, stride=2), :]
-
-        terms = [picked(row + offset) for row in range(3)]
-        for row in range(2):
-            out_ref[index, row] = weights[0:1] * terms[row] + weights[1:2] * terms[row + 1]
-
-    unrolled(step, count)
+
+    def run(before, after):
+        def step(index, slot):
+            tile = tile_of(index, group, tiles, core)
+            offset = offset_ref[tile]
+            weights = weights_ref[:, pl.ds(pl.multiple_of(tile * LANES, LANES), LANES)]
+            lines = [
+                ref[begin + index, pl.ds(row, views, stride=2), :]
+                for ref in (before, own_ref, after)
+                for row in range(2)
+            ]
+            terms = []
+            for row in range(3):
+                low = jnp.where(offset == -2, lines[row], lines[row + 1])
+                high = jnp.where(offset == 0, lines[row + 2], lines[row + 3])
+                terms.append(jnp.where(offset < 0, low, high))
+            for row in range(2):
+                out_ref[index, row] = weights[0:1] * terms[row] + weights[1:2] * terms[row + 1]
+
+        unrolled(step, count)
+
+    beside = lax.axis_index("row") % 2
+    pl.when(beside == 0)(lambda: run(odd_ref, even_ref))
+    pl.when(beside == 1)(lambda: run(even_ref, odd_ref))
 
 
 def interpolate_rows(group, held, tiles, offset, even, odd, own, weights, after, cost):
@@ -249,7 +251,7 @@
     return call(
         functools.partial(rows_body, group, held, tiles),
         [f32(group[1], 2, height // 2, LANES)],
-        [pltpu.VMEM((2, 3 * height + 8, LANES), jnp.float32)],
+        [],
         (offset, odd, even, own, weights),
         cost,
         after,
@@ -548,7 +550,7 @@
         scratch,
         args,
         out=ANY if number else VMEM,
-        cost=SHORT if number else cycles(6000),
+        cost=SHORT if number else cycles(3000),
     )[0]
 
 

time: 55.8 us -> 55.7 us (level)
  no operation moved by 1% of the time
where the time goes in v8:
time: 55.7 us; the launch traced here: 55.5 us
  waiting for transfers between devices  22.6 us (41%)
  starting transfers between devices  17.5 us (31%)
  Pallas kernels  15.1 us (27%)
    ppermute x14, waiting for transfers between devices, permuted(): lax.ppermute(value, axis, [(i, j) for i, j in pairs if 0 <= j < count])  22.6 us
    ppermute x14, starting transfers between devices, permuted(): lax.ppermute(value, axis, [(i, j) for i, j in pairs if 0 <= j < count])  17.5 us
    pallas_call x14, Pallas kernels, call(): pl.pallas_call(kernel, out_shape=outs, in_specs=[*specs, *[ANY] * len(aft...  15.1 us
  transfers between devices with their start and end apart: 14, of which 9 were waited for; matrix products, arithmetic and copies ran while one was open for 0% of the time, Pallas kernels for 19%

profile of v8, /device:TPU:11, one launch (start us, length us, event | category | flops | bytes accessed | tf_op | source)
XLA Modules:
  0.0 55.5 jit_solution(7401923075120704006)
XLA Ops:
  0.0 0.7 %collective-permute-start = (f32[32,2,4096]{2,1,0:T(2,128)}, f32[32,2,4096]{2,1,0:T(2,128)S(1)}, u32[]{:S(2)}, u32[]{:S(2)}) collective-permute-start(f32[32,2,4096]{2,1,0:T(2,128)} %refs_2_.4), channel_id=1, source_target_pairs={{0,4},{4,0},{8,12},{12,8},{16,20},{20,16},{24,28},{28,24},{1,5},{5... | collective-permute-start | bytes 3145736 | tf_op jit(solution)/shard_map/ppermute | solution.py:560
  0.7 2.0 %shard_map.118 = (f32[11,64,128]{2,1,0:T(8,128)S(1)}, bf16[16,256,128]{2,1,0:T(8,128)(2,1)S(1)}, f32[32,2,4096]{2,1,0:T(2,128)S(1)}) custom-call(s32[32]{0:T(128)} %refs_0_.16, bf16[32,256,128]{2,1,0:T(8,128)(2,1)} %refs_1_.9, f32[32,2,4096]{2,1,0:T(2,128)} %refs_2_.4), custom_call_target="tpu_custom_call" | custom-call | flops 1 | bytes 1 | tf_op jit(solution)/shard_map/pallas_call | solution.py:36
  3.2 1.1 %shard_map.119.refs_4_.refs_3_ = f32[11,128,128]{2,1,0:T(8,128)S(1)} custom-call(s32[32]{0:T(128)S(1)} %copy-done.7, bf16[16,256,128]{2,1,0:T(8,128)(2,1)S(1)} %get-tuple-element.14.refs_1_, f32[32,2,4096]{2,1,0:T(2,128)S(1)} %collective-permute-done.refs_2_.refs_3_, f32[11,64,128]{2,1,0:T(8,128)S(1)} %get-tuple-element.16.refs_3_), custom_call_target="tpu_custom_call" | custom-call | flops 1 | bytes 1 | tf_op jit(solution)/shard_map/pallas_call | solution.py:36
  4.6 4.3 %collective-permute-start.3 = (f32[11,128,128]{2,1,0:T(8,128)S(1)}, f32[11,128,128]{2,1,0:T(8,128)S(1)}, u32[]{:S(2)}, u32[]{:S(2)}) collective-permute-start(f32[11,128,128]{2,1,0:T(8,128)S(1)} %shard_map.119.refs_4_.refs_3_), channel_id=1, source_target_pairs={{1,2},{2,1},{5,6},{6,5},{9,10},{10,9},{13,14},{14,13},{17,18},{18,... | collective-permute-start | bytes 2162696 | tf_op jit(solution)/shard_map/ppermute | solution.py:560
  8.9 1.1 %shard_map.120.refs_2_.refs_3_ = f32[5,2,64,128]{3,2,1,0:T(8,128)S(1)} custom-call(s32[32]{0:T(128)S(1)} %copy-done.7, bf16[16,256,128]{2,1,0:T(8,128)(2,1)S(1)} %get-tuple-element.14.refs_1_, f32[32,2,4096]{2,1,0:T(2,128)S(1)} %get-tuple-element.15.refs_2_, f32[32,2,4096]{2,1,0:T(2,128)S(1)} %collective-permute-done.refs_2_.refs_3_, ...), custom_call_target="tpu_custom_call" | custom-call | flops 2097152000 | bytes 1 | tf_op jit(solution)/shard_map/pallas_call | solution.py:36
  10.4 6.0 %collective-permute-done.1.refs_3_.refs_4_ = f32[5,2,64,128]{3,2,1,0:T(8,128)S(1)} collective-permute-done((f32[5,2,64,128]{3,2,1,0:T(8,128)S(1)}, f32[5,2,64,128]{3,2,1,0:T(8,128)S(1)}, u32[]{:S(2)}, u32[]{:S(2)}) %collective-permute-start.1) | collective-permute-done | bytes 327712 | tf_op jit(solution)/shard_map/ppermute | solution.py:560
  17.0 1.3 %collective-permute-start.2 = (f32[5,2,88,128]{3,2,1,0:T(8,128)S(1)}, f32[5,2,88,128]{3,2,1,0:T(8,128)S(1)}, u32[]{:S(2)}, u32[]{:S(2)}) collective-permute-start(f32[5,2,88,128]{3,2,1,0:T(8,128)S(1)} %shard_map.121.refs_5_), channel_id=1, source_target_pairs={{0,8},{4,20},{8,0},{12,28},{16,24},{20,4},{24,16},{28,12},{1,9},{5... | collective-permute-start | bytes 1351688 | tf_op jit(solution)/shard_map/ppermute | solution.py:560
  18.3 3.4 %collective-permute-done.4.refs_2_ = f32[11,128,128]{2,1,0:T(8,128)S(1)} collective-permute-done((f32[11,128,128]{2,1,0:T(8,128)S(1)}, f32[11,128,128]{2,1,0:T(8,128)S(1)}, u32[]{:S(2)}, u32[]{:S(2)}) %collective-permute-start.4) | collective-permute-done | bytes 720928 | tf_op jit(solution)/shard_map/ppermute | solution.py:560
  21.7 3.0 %collective-permute-done.3.refs_1_ = f32[11,128,128]{2,1,0:T(8,128)S(1)} collective-permute-done((f32[11,128,128]{2,1,0:T(8,128)S(1)}, f32[11,128,128]{2,1,0:T(8,128)S(1)}, u32[]{:S(2)}, u32[]{:S(2)}) %collective-permute-start.3) | collective-permute-done | bytes 720928 | tf_op jit(solution)/shard_map/ppermute | solution.py:560
  26.4 1.3 %collective-permute-start.11 = (f32[5,2,64,128]{3,2,1,0:T(8,128)S(1)}, f32[5,2,64,128]{3,2,1,0:T(8,128)S(1)}, u32[]{:S(2)}, u32[]{:S(2)}) collective-permute-start(f32[5,2,64,128]{3,2,1,0:T(8,128)S(1)} %shard_map.123.refs_7_.refs_2_.refs_3_), channel_id=1, source_target_pairs={{0,16},{4,12},{8,24},{12,4},{16,0},{20,28},{24,8},{28,20},{1,17},{... | collective-permute-start | bytes 983048 | tf_op jit(solution)/shard_map/ppermute | solution.py:560
  27.7 0.9 %shard_map.124.refs_3_.refs_4_ = f32[5,2,2,64,128]{4,3,2,1,0:T(8,128)S(1)} custom-call(s32[32]{0:T(128)S(1)} %copy-done.4, s32[32]{0:T(128)S(1)} %copy-done.5, f32[4,4096]{1,0:T(4,128)S(1)} %copy-done, f32[5,2,64,128]{3,2,1,0:T(8,128)S(1)} %shard_map.120.refs_2_.refs_3_, f32[5,2,64,128]{3,2,1,0:T(8,128)S(1)} %collective-permute-done.1.refs_3_.refs_4_, ...), custom_call_target="tpu_custom_call" | custom-call | flops 524288 | bytes 1 | tf_op jit(solution)/shard_map/pallas_call | solution.py:36
  28.7 3.0 %collective-permute-start.5 = (f32[5,2,2,64,128]{4,3,2,1,0:T(8,128)S(1)}, f32[5,2,2,64,128]{4,3,2,1,0:T(8,128)S(1)}, u32[]{:S(2)}, u32[]{:S(2)}) collective-permute-start(f32[5,2,2,64,128]{4,3,2,1,0:T(8,128)S(1)} %shard_map.124.refs_3_.refs_4_), channel_id=1, source_target_pairs={{1,2},{2,1},{5,6},{6,5},{9,10},{10,9},{13,14},{14,13},{17,18},{18,... | collective-permute-start | bytes 1966088 | tf_op jit(solution)/shard_map/ppermute | solution.py:560
  31.7 0.7 %collective-permute-done.8.refs_3_.refs_4_ = f32[6,2,64,128]{3,2,1,0:T(8,128)S(1)} collective-permute-done((f32[6,2,64,128]{3,2,1,0:T(8,128)S(1)}, f32[6,2,64,128]{3,2,1,0:T(8,128)S(1)}, u32[]{:S(2)}, u32[]{:S(2)}) %collective-permute-start.8) | collective-permute-done | bytes 393248 | tf_op jit(solution)/shard_map/ppermute | solution.py:560
  33.1 1.3 %collective-permute-start.9 = (f32[6,2,88,128]{3,2,1,0:T(8,128)S(1)}, f32[6,2,88,128]{3,2,1,0:T(8,128)S(1)}, u32[]{:S(2)}, u32[]{:S(2)}) collective-permute-start(f32[6,2,88,128]{3,2,1,0:T(8,128)S(1)} %shard_map.126), channel_id=1, source_target_pairs={{0,8},{4,20},{8,0},{12,28},{16,24},{20,4},{24,16},{28,12},{1,9},{5... | collective-permute-start | bytes 1622024 | tf_op jit(solution)/shard_map/ppermute | solution.py:560
  34.4 1.6 %collective-permute-done.11.refs_3_.refs_4_ = f32[5,2,64,128]{3,2,1,0:T(8,128)S(1)} collective-permute-done((f32[5,2,64,128]{3,2,1,0:T(8,128)S(1)}, f32[5,2,64,128]{3,2,1,0:T(8,128)S(1)}, u32[]{:S(2)}, u32[]{:S(2)}) %collective-permute-start.11) | collective-permute-done | bytes 327712 | tf_op jit(solution)/shard_map/ppermute | solution.py:560
  36.6 1.3 %collective-permute-start.12 = (f32[5,2,88,128]{3,2,1,0:T(8,128)S(1)}, f32[5,2,88,128]{3,2,1,0:T(8,128)S(1)}, u32[]{:S(2)}, u32[]{:S(2)}) collective-permute-start(f32[5,2,88,128]{3,2,1,0:T(8,128)S(1)} %shard_map.128), channel_id=1, source_target_pairs={{0,8},{4,20},{8,0},{12,28},{16,24},{20,4},{24,16},{28,12},{1,9},{5... | collective-permute-start | bytes 1351688 | tf_op jit(solution)/shard_map/ppermute | solution.py:560
  37.9 5.2 %collective-permute-done.6.refs_2_ = f32[5,2,2,64,128]{4,3,2,1,0:T(8,128)S(1)} collective-permute-done((f32[5,2,2,64,128]{4,3,2,1,0:T(8,128)S(1)}, f32[5,2,2,64,128]{4,3,2,1,0:T(8,128)S(1)}, u32[]{:S(2)}, u32[]{:S(2)}) %collective-permute-start.6) | collective-permute-done | bytes 655392 | tf_op jit(solution)/shard_map/ppermute | solution.py:560
  43.1 1.9 %collective-permute-done.5.refs_1_ = f32[5,2,2,64,128]{4,3,2,1,0:T(8,128)S(1)} collective-permute-done((f32[5,2,2,64,128]{4,3,2,1,0:T(8,128)S(1)}, f32[5,2,2,64,128]{4,3,2,1,0:T(8,128)S(1)}, u32[]{:S(2)}, u32[]{:S(2)}) %collective-permute-start.5) | collective-permute-done | bytes 655392 | tf_op jit(solution)/shard_map/ppermute | solution.py:560
  45.0 0.8 %shard_map.125 = (f32[5,2,2,32,128]{4,3,2,1,0:T(8,128)S(1)}, f32[5,2,2,32,128]{4,3,2,1,0:T(8,128)S(1)}) custom-call(s32[32]{0:T(128)S(1)} %copy-done.6, f32[5,2,2,64,128]{4,3,2,1,0:T(8,128)S(1)} %collective-permute-done.5.refs_1_, f32[5,2,2,64,128]{4,3,2,1,0:T(8,128)S(1)} %collective-permute-done.6.refs_2_, ...), custom_call_target="tpu_custom_call" | custom-call | flops 524288 | bytes 1 | tf_op jit(solution)/shard_map/pallas_call | solution.py:36
  45.8 2.8 %collective-permute-start.7 = (f32[5,2,2,32,128]{4,3,2,1,0:T(8,128)S(1)}, f32[5,2,2,32,128]{4,3,2,1,0:T(8,128)S(1)}, u32[]{:S(2)}, u32[]{:S(2)}) collective-permute-start(f32[5,2,2,32,128]{4,3,2,1,0:T(8,128)S(1)} %get-tuple-element.18), channel_id=1, source_target_pairs={{0,4},{4,0},{8,12},{12,8},{16,20},{20,16},{24,28},{28,24},{1,5},{5... | collective-permute-start | bytes 983048 | tf_op jit(solution)/shard_map/ppermute | solution.py:560
  48.6 0.9 %shard_map.127 = (f32[6,2,2,32,128]{4,3,2,1,0:T(8,128)S(1)}, f32[6,2,2,32,128]{4,3,2,1,0:T(8,128)S(1)}) custom-call(s32[32]{0:T(128)S(1)} %copy-done.4, s32[32]{0:T(128)S(1)} %copy-done.5, f32[4,4096]{1,0:T(4,128)S(1)} %copy-done, f32[6,2,64,128]{3,2,1,0:T(8,128)S(1)} %shard_map.122.refs_6_.refs_2_.refs_3_, ...), custom_call_target="tpu_custom_call" | custom-call | flops 1 | bytes 1 | tf_op jit(solution)/shard_map/pallas_call | solution.py:36
  49.6 0.9 %shard_map.129 = (f32[5,2,2,32,128]{4,3,2,1,0:T(8,128)S(1)}, f32[5,2,2,32,128]{4,3,2,1,0:T(8,128)S(1)}) custom-call(s32[32]{0:T(128)S(1)} %copy-done.4, s32[32]{0:T(128)S(1)} %copy-done.5, f32[4,4096]{1,0:T(4,128)S(1)} %copy-done, f32[5,2,64,128]{3,2,1,0:T(8,128)S(1)} %shard_map.123.refs_7_.refs_2_.refs_3_, ...), custom_call_target="tpu_custom_call" | custom-call | flops 1 | bytes 1 | tf_op jit(solution)/shard_map/pallas_call | solution.py:36
  51.0 0.9 %shard_map.130.refs_8_ = f32[32,2,8192]{2,1,0:T(2,128)S(1)} custom-call(bf16[768,256]{1,0:T(8,128)(2,1)S(1)} %copy-done.2, bf16[768,256]{1,0:T(8,128)(2,1)S(1)} %copy-done.1, f32[5,2,2,32,128]{4,3,2,1,0:T(8,128)S(1)} %get-tuple-element.17.refs_2_, f32[5,2,2,32,128]{4,3,2,1,0:T(8,128)S(1)} %collective-permute-done.7.refs_3_), custom_call_target="tpu_custom_call" | custom-call | flops 1572864000 | bytes 1 | tf_op jit(solution)/shard_map/pallas_call | solution.py:36
  52.2 3.3 %shard_map.131 = f32[32,2,8192]{2,1,0:T(2,128)} custom-call(bf16[768,256]{1,0:T(8,128)(2,1)S(1)} %copy-done.2, bf16[768,256]{1,0:T(8,128)(2,1)S(1)} %copy-done.1, f32[5,2,2,32,128]{4,3,2,1,0:T(8,128)S(1)} %get-tuple-element.17.refs_2_, f32[5,2,2,32,128]{4,3,2,1,0:T(8,128)S(1)} %collective-permute-done.7.refs_3_, ...), custom_call_target="tpu_custom_call" | custom-call | flops 1 | bytes 1 | tf_op jit(solution)/shard_map/pallas_call | solution.py:36
  (34 shorter events, 5.6 us)
Async XLA Ops:
  0.0 3.2 %copy-start.7 = (s32[32]{0:T(128)S(1)}, s32[32]{0:T(128)}, u32[]{:S(2)}) copy-start(s32[32]{0:T(128)} %refs_0_.16) | copy-start | bytes 388
  0.0 3.2 %collective-permute-start = (f32[32,2,4096]{2,1,0:T(2,128)}, f32[32,2,4096]{2,1,0:T(2,128)S(1)}, u32[]{:S(2)}, u32[]{:S(2)}) collective-permute-start(f32[32,2,4096]{2,1,0:T(2,128)} %refs_2_.4), channel_id=1, source_target_pairs={{0,4},{4,0},{8,12},{12,8},{16,20},{20,16},{24,28},{28,24},{1,5},{5... | collective-permute-start | bytes 3145736 | tf_op jit(solution)/shard_map/ppermute | solution.py:560
  4.3 17.4 %collective-permute-start.4 = (f32[11,128,128]{2,1,0:T(8,128)S(1)}, f32[11,128,128]{2,1,0:T(8,128)S(1)}, u32[]{:S(2)}, u32[]{:S(2)}) collective-permute-start(f32[11,128,128]{2,1,0:T(8,128)S(1)} %shard_map.119.refs_4_.refs_3_), channel_id=1, source_target_pairs={{0,1},{1,0},{2,3},{3,2},{4,5},{5,4},{6,7},{7,6},{8,9},{9,8},{10,11... | collective-permute-start | bytes 2162696 | tf_op jit(solution)/shard_map/ppermute | solution.py:560
  4.6 20.2 %collective-permute-start.3 = (f32[11,128,128]{2,1,0:T(8,128)S(1)}, f32[11,128,128]{2,1,0:T(8,128)S(1)}, u32[]{:S(2)}, u32[]{:S(2)}) collective-permute-start(f32[11,128,128]{2,1,0:T(8,128)S(1)} %shard_map.119.refs_4_.refs_3_), channel_id=1, source_target_pairs={{1,2},{2,1},{5,6},{6,5},{9,10},{10,9},{13,14},{14,13},{17,18},{18,... | collective-permute-start | bytes 2162696 | tf_op jit(solution)/shard_map/ppermute | solution.py:560
  8.9 7.5 %copy-start.4 = (s32[32]{0:T(128)S(1)}, s32[32]{0:T(128)}, u32[]{:S(2)}) copy-start(s32[32]{0:T(128)} %refs_0_.25) | copy-start | bytes 388
  8.9 7.5 %copy-start.5 = (s32[32]{0:T(128)S(1)}, s32[32]{0:T(128)}, u32[]{:S(2)}) copy-start(s32[32]{0:T(128)} %refs_1_.15) | copy-start | bytes 388
  8.9 15.8 %copy-start.3 = (f32[2,4096]{1,0:T(2,128)S(1)}, f32[2,4096]{1,0:T(2,128)}, u32[]{:S(2)}) copy-start(f32[2,4096]{1,0:T(2,128)} %refs_4_.5) | copy-start | bytes 98308
  8.9 15.8 %copy-start.6 = (s32[32]{0:T(128)S(1)}, s32[32]{0:T(128)}, u32[]{:S(2)}) copy-start(s32[32]{0:T(128)} %refs_0_.21) | copy-start | bytes 388
  10.1 6.3 %collective-permute-start.1 = (f32[5,2,64,128]{3,2,1,0:T(8,128)S(1)}, f32[5,2,64,128]{3,2,1,0:T(8,128)S(1)}, u32[]{:S(2)}, u32[]{:S(2)}) collective-permute-start(f32[5,2,64,128]{3,2,1,0:T(8,128)S(1)} %shard_map.120.refs_2_.refs_3_), channel_id=1, source_target_pairs={{0,16},{4,12},{8,24},{12,4},{16,0},{20,28},{24,8},{28,20},{1,17},{... | collective-permute-start | bytes 983048 | tf_op jit(solution)/shard_map/ppermute | solution.py:560
  17.0 10.7 %collective-permute-start.2 = (f32[5,2,88,128]{3,2,1,0:T(8,128)S(1)}, f32[5,2,88,128]{3,2,1,0:T(8,128)S(1)}, u32[]{:S(2)}, u32[]{:S(2)}) collective-permute-start(f32[5,2,88,128]{3,2,1,0:T(8,128)S(1)} %shard_map.121.refs_5_), channel_id=1, source_target_pairs={{0,8},{4,20},{8,0},{12,28},{16,24},{20,4},{24,16},{28,12},{1,9},{5... | collective-permute-start | bytes 1351688 | tf_op jit(solution)/shard_map/ppermute | solution.py:560
  25.4 2.3 %copy-start = (f32[4,4096]{1,0:T(4,128)S(1)}, f32[4,4096]{1,0:T(4,128)}, u32[]{:S(2)}) copy-start(f32[4,4096]{1,0:T(4,128)} %refs_2_.7) | copy-start | bytes 196612
  25.5 7.0 %collective-permute-start.8 = (f32[6,2,64,128]{3,2,1,0:T(8,128)S(1)}, f32[6,2,64,128]{3,2,1,0:T(8,128)S(1)}, u32[]{:S(2)}, u32[]{:S(2)}) collective-permute-start(f32[6,2,64,128]{3,2,1,0:T(8,128)S(1)} %shard_map.122.refs_6_.refs_2_.refs_3_), channel_id=1, source_target_pairs={{0,16},{4,12},{8,24},{12,4},{16,0},{20,28},{24,8},{28,20},{1,17},{... | collective-permute-start | bytes 1179656 | tf_op jit(solution)/shard_map/ppermute | solution.py:560
  26.4 9.5 %collective-permute-start.11 = (f32[5,2,64,128]{3,2,1,0:T(8,128)S(1)}, f32[5,2,64,128]{3,2,1,0:T(8,128)S(1)}, u32[]{:S(2)}, u32[]{:S(2)}) collective-permute-start(f32[5,2,64,128]{3,2,1,0:T(8,128)S(1)} %shard_map.123.refs_7_.refs_2_.refs_3_), channel_id=1, source_target_pairs={{0,16},{4,12},{8,24},{12,4},{16,0},{20,28},{24,8},{28,20},{1,17},{... | collective-permute-start | bytes 983048 | tf_op jit(solution)/shard_map/ppermute | solution.py:560
  28.6 14.5 %collective-permute-start.6 = (f32[5,2,2,64,128]{4,3,2,1,0:T(8,128)S(1)}, f32[5,2,2,64,128]{4,3,2,1,0:T(8,128)S(1)}, u32[]{:S(2)}, u32[]{:S(2)}) collective-permute-start(f32[5,2,2,64,128]{4,3,2,1,0:T(8,128)S(1)} %shard_map.124.refs_3_.refs_4_), channel_id=1, source_target_pairs={{0,1},{1,0},{2,3},{3,2},{4,5},{5,4},{6,7},{7,6},{8,9},{9,8},{10,11... | collective-permute-start | bytes 1966088 | tf_op jit(solution)/shard_map/ppermute | solution.py:560
  28.7 16.3 %collective-permute-start.5 = (f32[5,2,2,64,128]{4,3,2,1,0:T(8,128)S(1)}, f32[5,2,2,64,128]{4,3,2,1,0:T(8,128)S(1)}, u32[]{:S(2)}, u32[]{:S(2)}) collective-permute-start(f32[5,2,2,64,128]{4,3,2,1,0:T(8,128)S(1)} %shard_map.124.refs_3_.refs_4_), channel_id=1, source_target_pairs={{1,2},{2,1},{5,6},{6,5},{9,10},{10,9},{13,14},{14,13},{17,18},{18,... | collective-permute-start | bytes 1966088 | tf_op jit(solution)/shard_map/ppermute | solution.py:560
  33.1 15.5 %collective-permute-start.9 = (f32[6,2,88,128]{3,2,1,0:T(8,128)S(1)}, f32[6,2,88,128]{3,2,1,0:T(8,128)S(1)}, u32[]{:S(2)}, u32[]{:S(2)}) collective-permute-start(f32[6,2,88,128]{3,2,1,0:T(8,128)S(1)} %shard_map.126), channel_id=1, source_target_pairs={{0,8},{4,20},{8,0},{12,28},{16,24},{20,4},{24,16},{28,12},{1,9},{5... | collective-permute-start | bytes 1622024 | tf_op jit(solution)/shard_map/ppermute | solution.py:560
  36.6 14.4 %copy-start.1 = (bf16[768,256]{1,0:T(8,128)(2,1)S(1)}, bf16[768,256]{1,0:T(8,128)(2,1)}, u32[]{:S(2)}) copy-start(bf16[768,256]{1,0:T(8,128)(2,1)} %constant.5.clone.refs_1_) | copy-start | bytes 1179652
  36.6 14.4 %copy-start.2 = (bf16[768,256]{1,0:T(8,128)(2,1)S(1)}, bf16[768,256]{1,0:T(8,128)(2,1)}, u32[]{:S(2)}) copy-start(bf16[768,256]{1,0:T(8,128)(2,1)} %constant.4.clone.refs_0_) | copy-start | bytes 1179652
  36.6 12.9 %collective-permute-start.12 = (f32[5,2,88,128]{3,2,1,0:T(8,128)S(1)}, f32[5,2,88,128]{3,2,1,0:T(8,128)S(1)}, u32[]{:S(2)}, u32[]{:S(2)}) collective-permute-start(f32[5,2,88,128]{3,2,1,0:T(8,128)S(1)} %shard_map.128), channel_id=1, source_target_pairs={{0,8},{4,20},{8,0},{12,28},{16,24},{20,4},{24,16},{28,12},{1,9},{5... | collective-permute-start | bytes 1351688 | tf_op jit(solution)/shard_map/ppermute | solution.py:560
  45.8 5.2 %collective-permute-start.7 = (f32[5,2,2,32,128]{4,3,2,1,0:T(8,128)S(1)}, f32[5,2,2,32,128]{4,3,2,1,0:T(8,128)S(1)}, u32[]{:S(2)}, u32[]{:S(2)}) collective-permute-start(f32[5,2,2,32,128]{4,3,2,1,0:T(8,128)S(1)} %get-tuple-element.18), channel_id=1, source_target_pairs={{0,4},{4,0},{8,12},{12,8},{16,20},{20,16},{24,28},{28,24},{1,5},{5... | collective-permute-start | bytes 983048 | tf_op jit(solution)/shard_map/ppermute | solution.py:560
  49.5 2.8 %collective-permute-start.10 = (f32[6,2,2,32,128]{4,3,2,1,0:T(8,128)S(1)}, f32[6,2,2,32,128]{4,3,2,1,0:T(8,128)S(1)}, u32[]{:S(2)}, u32[]{:S(2)}) collective-permute-start(f32[6,2,2,32,128]{4,3,2,1,0:T(8,128)S(1)} %get-tuple-element.20), channel_id=1, source_target_pairs={{0,4},{4,0},{8,12},{12,8},{16,20},{20,16},{24,28},{28,24},{1,5},{5... | collective-permute-start | bytes 1179656 | tf_op jit(solution)/shard_map/ppermute | solution.py:560
  50.4 1.8 %collective-permute-start.13 = (f32[5,2,2,32,128]{4,3,2,1,0:T(8,128)S(1)}, f32[5,2,2,32,128]{4,3,2,1,0:T(8,128)S(1)}, u32[]{:S(2)}, u32[]{:S(2)}) collective-permute-start(f32[5,2,2,32,128]{4,3,2,1,0:T(8,128)S(1)} %get-tuple-element.22), channel_id=1, source_target_pairs={{0,4},{4,0},{8,12},{12,8},{16,20},{20,16},{24,28},{28,24},{1,5},{5... | collective-permute-start | bytes 983048 | tf_op jit(solution)/shard_map/ppermute | solution.py:560

commit v9 on v8

--- a/solution.py
+++ b/solution.py
@@ -11,7 +11,7 @@
 
 KR = 256
 LAST_COST = 1
-GROUPS = ((0, 5), (5, 6), (11, 5))
+GROUPS = ((0, 5), (5, 5), (10, 6))
 LANES = 128
 WINDOW = 3 * LANES
 SLOTS = 88

time: 55.7 us -> 55.7 us (level)
  no operation moved by 1% of the time
where the time goes in v9:
time: 55.7 us; the launch traced here: 55.5 us
  waiting for transfers between devices  22.6 us (41%)
  starting transfers between devices  17.5 us (31%)
  Pallas kernels  15.1 us (27%)
    ppermute x14, waiting for transfers between devices, permuted(): lax.ppermute(value, axis, [(i, j) for i, j in pairs if 0 <= j < count])  22.6 us
    ppermute x14, starting transfers between devices, permuted(): lax.ppermute(value, axis, [(i, j) for i, j in pairs if 0 <= j < count])  17.5 us
    pallas_call x14, Pallas kernels, call(): pl.pallas_call(kernel, out_shape=outs, in_specs=[*specs, *[ANY] * len(aft...  15.1 us
  transfers between devices with their start and end apart: 14, of which 9 were waited for; matrix products, arithmetic and copies ran while one was open for 0% of the time, Pallas kernels for 19%

profile of v9, /device:TPU:11, one launch (start us, length us, event | category | flops | bytes accessed | tf_op | source)
XLA Modules:
  0.0 55.5 jit_solution(9250373690149201870)
XLA Ops:
  0.0 0.7 %collective-permute-start = (f32[32,2,4096]{2,1,0:T(2,128)}, f32[32,2,4096]{2,1,0:T(2,128)S(1)}, u32[]{:S(2)}, u32[]{:S(2)}) collective-permute-start(f32[32,2,4096]{2,1,0:T(2,128)} %refs_2_.4), channel_id=1, source_target_pairs={{0,4},{4,0},{8,12},{12,8},{16,20},{20,16},{24,28},{28,24},{1,5},{5... | collective-permute-start | bytes 3145736 | tf_op jit(solution)/shard_map/ppermute | solution.py:560
  0.7 2.1 %shard_map.118 = (f32[11,64,128]{2,1,0:T(8,128)S(1)}, bf16[16,256,128]{2,1,0:T(8,128)(2,1)S(1)}, f32[32,2,4096]{2,1,0:T(2,128)S(1)}) custom-call(s32[32]{0:T(128)} %refs_0_.16, bf16[32,256,128]{2,1,0:T(8,128)(2,1)} %refs_1_.9, f32[32,2,4096]{2,1,0:T(2,128)} %refs_2_.4), custom_call_target="tpu_custom_call" | custom-call | flops 1 | bytes 1 | tf_op jit(solution)/shard_map/pallas_call | solution.py:36
  3.2 1.2 %shard_map.119.refs_4_.refs_3_ = f32[11,128,128]{2,1,0:T(8,128)S(1)} custom-call(s32[32]{0:T(128)S(1)} %copy-done.7, bf16[16,256,128]{2,1,0:T(8,128)(2,1)S(1)} %get-tuple-element.14.refs_1_, f32[32,2,4096]{2,1,0:T(2,128)S(1)} %collective-permute-done.refs_2_.refs_3_, f32[11,64,128]{2,1,0:T(8,128)S(1)} %get-tuple-element.16.refs_3_), custom_call_target="tpu_custom_call" | custom-call | flops 1 | bytes 1 | tf_op jit(solution)/shard_map/pallas_call | solution.py:36
  4.6 4.3 %collective-permute-start.3 = (f32[11,128,128]{2,1,0:T(8,128)S(1)}, f32[11,128,128]{2,1,0:T(8,128)S(1)}, u32[]{:S(2)}, u32[]{:S(2)}) collective-permute-start(f32[11,128,128]{2,1,0:T(8,128)S(1)} %shard_map.119.refs_4_.refs_3_), channel_id=1, source_target_pairs={{1,2},{2,1},{5,6},{6,5},{9,10},{10,9},{13,14},{14,13},{17,18},{18,... | collective-permute-start | bytes 2162696 | tf_op jit(solution)/shard_map/ppermute | solution.py:560
  8.9 1.1 %shard_map.120.refs_2_.refs_3_ = f32[5,2,64,128]{3,2,1,0:T(8,128)S(1)} custom-call(s32[32]{0:T(128)S(1)} %copy-done.7, bf16[16,256,128]{2,1,0:T(8,128)(2,1)S(1)} %get-tuple-element.14.refs_1_, f32[32,2,4096]{2,1,0:T(2,128)S(1)} %get-tuple-element.15.refs_2_, f32[32,2,4096]{2,1,0:T(2,128)S(1)} %collective-permute-done.refs_2_.refs_3_, ...), custom_call_target="tpu_custom_call" | custom-call | flops 2097152000 | bytes 1 | tf_op jit(solution)/shard_map/pallas_call | solution.py:36
  10.4 6.0 %collective-permute-done.1.refs_3_.refs_4_ = f32[5,2,64,128]{3,2,1,0:T(8,128)S(1)} collective-permute-done((f32[5,2,64,128]{3,2,1,0:T(8,128)S(1)}, f32[5,2,64,128]{3,2,1,0:T(8,128)S(1)}, u32[]{:S(2)}, u32[]{:S(2)}) %collective-permute-start.1) | collective-permute-done | bytes 327712 | tf_op jit(solution)/shard_map/ppermute | solution.py:560
  17.0 1.3 %collective-permute-start.2 = (f32[5,2,88,128]{3,2,1,0:T(8,128)S(1)}, f32[5,2,88,128]{3,2,1,0:T(8,128)S(1)}, u32[]{:S(2)}, u32[]{:S(2)}) collective-permute-start(f32[5,2,88,128]{3,2,1,0:T(8,128)S(1)} %shard_map.121.refs_5_), channel_id=1, source_target_pairs={{0,8},{4,20},{8,0},{12,28},{16,24},{20,4},{24,16},{28,12},{1,9},{5... | collective-permute-start | bytes 1351688 | tf_op jit(solution)/shard_map/ppermute | solution.py:560
  18.3 3.4 %collective-permute-done.4.refs_2_ = f32[11,128,128]{2,1,0:T(8,128)S(1)} collective-permute-done((f32[11,128,128]{2,1,0:T(8,128)S(1)}, f32[11,128,128]{2,1,0:T(8,128)S(1)}, u32[]{:S(2)}, u32[]{:S(2)}) %collective-permute-start.4) | collective-permute-done | bytes 720928 | tf_op jit(solution)/shard_map/ppermute | solution.py:560
  21.7 3.0 %collective-permute-done.3.refs_1_ = f32[11,128,128]{2,1,0:T(8,128)S(1)} collective-permute-done((f32[11,128,128]{2,1,0:T(8,128)S(1)}, f32[11,128,128]{2,1,0:T(8,128)S(1)}, u32[]{:S(2)}, u32[]{:S(2)}) %collective-permute-start.3) | collective-permute-done | bytes 720928 | tf_op jit(solution)/shard_map/ppermute | solution.py:560
  26.4 1.3 %collective-permute-start.8 = (f32[5,2,64,128]{3,2,1,0:T(8,128)S(1)}, f32[5,2,64,128]{3,2,1,0:T(8,128)S(1)}, u32[]{:S(2)}, u32[]{:S(2)}) collective-permute-start(f32[5,2,64,128]{3,2,1,0:T(8,128)S(1)} %shard_map.122.refs_6_.refs_2_.refs_3_), channel_id=1, source_target_pairs={{0,16},{4,12},{8,24},{12,4},{16,0},{20,28},{24,8},{28,20},{1,17},{... | collective-permute-start | bytes 983048 | tf_op jit(solution)/shard_map/ppermute | solution.py:560
  27.7 0.9 %shard_map.124.refs_3_.refs_4_ = f32[5,2,2,64,128]{4,3,2,1,0:T(8,128)S(1)} custom-call(s32[32]{0:T(128)S(1)} %copy-done.4, s32[32]{0:T(128)S(1)} %copy-done.5, f32[4,4096]{1,0:T(4,128)S(1)} %copy-done, f32[5,2,64,128]{3,2,1,0:T(8,128)S(1)} %shard_map.120.refs_2_.refs_3_, f32[5,2,64,128]{3,2,1,0:T(8,128)S(1)} %collective-permute-done.1.refs_3_.refs_4_, ...), custom_call_target="tpu_custom_call" | custom-call | flops 524288 | bytes 1 | tf_op jit(solution)/shard_map/pallas_call | solution.py:36
  28.7 3.0 %collective-permute-start.5 = (f32[5,2,2,64,128]{4,3,2,1,0:T(8,128)S(1)}, f32[5,2,2,64,128]{4,3,2,1,0:T(8,128)S(1)}, u32[]{:S(2)}, u32[]{:S(2)}) collective-permute-start(f32[5,2,2,64,128]{4,3,2,1,0:T(8,128)S(1)} %shard_map.124.refs_3_.refs_4_), channel_id=1, source_target_pairs={{1,2},{2,1},{5,6},{6,5},{9,10},{10,9},{13,14},{14,13},{17,18},{18,... | collective-permute-start | bytes 1966088 | tf_op jit(solution)/shard_map/ppermute | solution.py:560
  31.7 0.7 %collective-permute-done.11.refs_3_.refs_4_ = f32[6,2,64,128]{3,2,1,0:T(8,128)S(1)} collective-permute-done((f32[6,2,64,128]{3,2,1,0:T(8,128)S(1)}, f32[6,2,64,128]{3,2,1,0:T(8,128)S(1)}, u32[]{:S(2)}, u32[]{:S(2)}) %collective-permute-start.11) | collective-permute-done | bytes 393248 | tf_op jit(solution)/shard_map/ppermute | solution.py:560
  33.1 1.3 %collective-permute-start.12 = (f32[6,2,88,128]{3,2,1,0:T(8,128)S(1)}, f32[6,2,88,128]{3,2,1,0:T(8,128)S(1)}, u32[]{:S(2)}, u32[]{:S(2)}) collective-permute-start(f32[6,2,88,128]{3,2,1,0:T(8,128)S(1)} %shard_map.128), channel_id=1, source_target_pairs={{0,8},{4,20},{8,0},{12,28},{16,24},{20,4},{24,16},{28,12},{1,9},{5... | collective-permute-start | bytes 1622024 | tf_op jit(solution)/shard_map/ppermute | solution.py:560
  34.4 1.6 %collective-permute-done.8.refs_3_.refs_4_ = f32[5,2,64,128]{3,2,1,0:T(8,128)S(1)} collective-permute-done((f32[5,2,64,128]{3,2,1,0:T(8,128)S(1)}, f32[5,2,64,128]{3,2,1,0:T(8,128)S(1)}, u32[]{:S(2)}, u32[]{:S(2)}) %collective-permute-start.8) | collective-permute-done | bytes 327712 | tf_op jit(solution)/shard_map/ppermute | solution.py:560
  36.6 1.3 %collective-permute-start.9 = (f32[5,2,88,128]{3,2,1,0:T(8,128)S(1)}, f32[5,2,88,128]{3,2,1,0:T(8,128)S(1)}, u32[]{:S(2)}, u32[]{:S(2)}) collective-permute-start(f32[5,2,88,128]{3,2,1,0:T(8,128)S(1)} %shard_map.126), channel_id=1, source_target_pairs={{0,8},{4,20},{8,0},{12,28},{16,24},{20,4},{24,16},{28,12},{1,9},{5... | collective-permute-start | bytes 1351688 | tf_op jit(solution)/shard_map/ppermute | solution.py:560
  37.9 5.2 %collective-permute-done.6.refs_2_ = f32[5,2,2,64,128]{4,3,2,1,0:T(8,128)S(1)} collective-permute-done((f32[5,2,2,64,128]{4,3,2,1,0:T(8,128)S(1)}, f32[5,2,2,64,128]{4,3,2,1,0:T(8,128)S(1)}, u32[]{:S(2)}, u32[]{:S(2)}) %collective-permute-start.6) | collective-permute-done | bytes 655392 | tf_op jit(solution)/shard_map/ppermute | solution.py:560
  43.1 1.9 %collective-permute-done.5.refs_1_ = f32[5,2,2,64,128]{4,3,2,1,0:T(8,128)S(1)} collective-permute-done((f32[5,2,2,64,128]{4,3,2,1,0:T(8,128)S(1)}, f32[5,2,2,64,128]{4,3,2,1,0:T(8,128)S(1)}, u32[]{:S(2)}, u32[]{:S(2)}) %collective-permute-start.5) | collective-permute-done | bytes 655392 | tf_op jit(solution)/shard_map/ppermute | solution.py:560
  45.0 0.8 %shard_map.125 = (f32[5,2,2,32,128]{4,3,2,1,0:T(8,128)S(1)}, f32[5,2,2,32,128]{4,3,2,1,0:T(8,128)S(1)}) custom-call(s32[32]{0:T(128)S(1)} %copy-done.6, f32[5,2,2,64,128]{4,3,2,1,0:T(8,128)S(1)} %collective-permute-done.5.refs_1_, f32[5,2,2,64,128]{4,3,2,1,0:T(8,128)S(1)} %collective-permute-done.6.refs_2_, ...), custom_call_target="tpu_custom_call" | custom-call | flops 524288 | bytes 1 | tf_op jit(solution)/shard_map/pallas_call | solution.py:36
  45.8 2.8 %collective-permute-start.7 = (f32[5,2,2,32,128]{4,3,2,1,0:T(8,128)S(1)}, f32[5,2,2,32,128]{4,3,2,1,0:T(8,128)S(1)}, u32[]{:S(2)}, u32[]{:S(2)}) collective-permute-start(f32[5,2,2,32,128]{4,3,2,1,0:T(8,128)S(1)} %get-tuple-element.18), channel_id=1, source_target_pairs={{0,4},{4,0},{8,12},{12,8},{16,20},{20,16},{24,28},{28,24},{1,5},{5... | collective-permute-start | bytes 983048 | tf_op jit(solution)/shard_map/ppermute | solution.py:560
  48.6 0.9 %shard_map.129 = (f32[6,2,2,32,128]{4,3,2,1,0:T(8,128)S(1)}, f32[6,2,2,32,128]{4,3,2,1,0:T(8,128)S(1)}) custom-call(s32[32]{0:T(128)S(1)} %copy-done.4, s32[32]{0:T(128)S(1)} %copy-done.5, f32[4,4096]{1,0:T(4,128)S(1)} %copy-done, f32[6,2,64,128]{3,2,1,0:T(8,128)S(1)} %shard_map.123.refs_7_.refs_2_.refs_3_, ...), custom_call_target="tpu_custom_call" | custom-call | flops 1 | bytes 1 | tf_op jit(solution)/shard_map/pallas_call | solution.py:36
  49.6 0.9 %shard_map.127 = (f32[5,2,2,32,128]{4,3,2,1,0:T(8,128)S(1)}, f32[5,2,2,32,128]{4,3,2,1,0:T(8,128)S(1)}) custom-call(s32[32]{0:T(128)S(1)} %copy-done.4, s32[32]{0:T(128)S(1)} %copy-done.5, f32[4,4096]{1,0:T(4,128)S(1)} %copy-done, f32[5,2,64,128]{3,2,1,0:T(8,128)S(1)} %shard_map.122.refs_6_.refs_2_.refs_3_, ...), custom_call_target="tpu_custom_call" | custom-call | flops 1 | bytes 1 | tf_op jit(solution)/shard_map/pallas_call | solution.py:36
  51.0 0.9 %shard_map.130.refs_8_ = f32[32,2,8192]{2,1,0:T(2,128)S(1)} custom-call(bf16[768,256]{1,0:T(8,128)(2,1)S(1)} %copy-done.2, bf16[768,256]{1,0:T(8,128)(2,1)S(1)} %copy-done.1, f32[5,2,2,32,128]{4,3,2,1,0:T(8,128)S(1)} %get-tuple-element.17.refs_2_, f32[5,2,2,32,128]{4,3,2,1,0:T(8,128)S(1)} %collective-permute-done.7.refs_3_), custom_call_target="tpu_custom_call" | custom-call | flops 1572864000 | bytes 1 | tf_op jit(solution)/shard_map/pallas_call | solution.py:36
  52.2 3.3 %shard_map.131 = f32[32,2,8192]{2,1,0:T(2,128)} custom-call(bf16[768,256]{1,0:T(8,128)(2,1)S(1)} %copy-done.2, bf16[768,256]{1,0:T(8,128)(2,1)S(1)} %copy-done.1, f32[5,2,2,32,128]{4,3,2,1,0:T(8,128)S(1)} %get-tuple-element.17.refs_2_, f32[5,2,2,32,128]{4,3,2,1,0:T(8,128)S(1)} %collective-permute-done.7.refs_3_, ...), custom_call_target="tpu_custom_call" | custom-call | flops 1 | bytes 1 | tf_op jit(solution)/shard_map/pallas_call | solution.py:36
  (34 shorter events, 5.6 us)
Async XLA Ops:
  0.0 3.2 %copy-start.7 = (s32[32]{0:T(128)S(1)}, s32[32]{0:T(128)}, u32[]{:S(2)}) copy-start(s32[32]{0:T(128)} %refs_0_.16) | copy-start | bytes 388
  0.0 3.2 %collective-permute-start = (f32[32,2,4096]{2,1,0:T(2,128)}, f32[32,2,4096]{2,1,0:T(2,128)S(1)}, u32[]{:S(2)}, u32[]{:S(2)}) collective-permute-start(f32[32,2,4096]{2,1,0:T(2,128)} %refs_2_.4), channel_id=1, source_target_pairs={{0,4},{4,0},{8,12},{12,8},{16,20},{20,16},{24,28},{28,24},{1,5},{5... | collective-permute-start | bytes 3145736 | tf_op jit(solution)/shard_map/ppermute | solution.py:560
  4.3 17.4 %collective-permute-start.4 = (f32[11,128,128]{2,1,0:T(8,128)S(1)}, f32[11,128,128]{2,1,0:T(8,128)S(1)}, u32[]{:S(2)}, u32[]{:S(2)}) collective-permute-start(f32[11,128,128]{2,1,0:T(8,128)S(1)} %shard_map.119.refs_4_.refs_3_), channel_id=1, source_target_pairs={{0,1},{1,0},{2,3},{3,2},{4,5},{5,4},{6,7},{7,6},{8,9},{9,8},{10,11... | collective-permute-start | bytes 2162696 | tf_op jit(solution)/shard_map/ppermute | solution.py:560
  4.6 20.2 %collective-permute-start.3 = (f32[11,128,128]{2,1,0:T(8,128)S(1)}, f32[11,128,128]{2,1,0:T(8,128)S(1)}, u32[]{:S(2)}, u32[]{:S(2)}) collective-permute-start(f32[11,128,128]{2,1,0:T(8,128)S(1)} %shard_map.119.refs_4_.refs_3_), channel_id=1, source_target_pairs={{1,2},{2,1},{5,6},{6,5},{9,10},{10,9},{13,14},{14,13},{17,18},{18,... | collective-permute-start | bytes 2162696 | tf_op jit(solution)/shard_map/ppermute | solution.py:560
  8.9 7.5 %copy-start.4 = (s32[32]{0:T(128)S(1)}, s32[32]{0:T(128)}, u32[]{:S(2)}) copy-start(s32[32]{0:T(128)} %refs_0_.25) | copy-start | bytes 388
  8.9 7.5 %copy-start.5 = (s32[32]{0:T(128)S(1)}, s32[32]{0:T(128)}, u32[]{:S(2)}) copy-start(s32[32]{0:T(128)} %refs_1_.15) | copy-start | bytes 388
  8.9 15.9 %copy-start.3 = (f32[2,4096]{1,0:T(2,128)S(1)}, f32[2,4096]{1,0:T(2,128)}, u32[]{:S(2)}) copy-start(f32[2,4096]{1,0:T(2,128)} %refs_4_.5) | copy-start | bytes 98308
  8.9 15.8 %copy-start.6 = (s32[32]{0:T(128)S(1)}, s32[32]{0:T(128)}, u32[]{:S(2)}) copy-start(s32[32]{0:T(128)} %refs_0_.21) | copy-start | bytes 388
  10.1 6.3 %collective-permute-start.1 = (f32[5,2,64,128]{3,2,1,0:T(8,128)S(1)}, f32[5,2,64,128]{3,2,1,0:T(8,128)S(1)}, u32[]{:S(2)}, u32[]{:S(2)}) collective-permute-start(f32[5,2,64,128]{3,2,1,0:T(8,128)S(1)} %shard_map.120.refs_2_.refs_3_), channel_id=1, source_target_pairs={{0,16},{4,12},{8,24},{12,4},{16,0},{20,28},{24,8},{28,20},{1,17},{... | collective-permute-start | bytes 983048 | tf_op jit(solution)/shard_map/ppermute | solution.py:560
  17.0 10.7 %collective-permute-start.2 = (f32[5,2,88,128]{3,2,1,0:T(8,128)S(1)}, f32[5,2,88,128]{3,2,1,0:T(8,128)S(1)}, u32[]{:S(2)}, u32[]{:S(2)}) collective-permute-start(f32[5,2,88,128]{3,2,1,0:T(8,128)S(1)} %shard_map.121.refs_5_), channel_id=1, source_target_pairs={{0,8},{4,20},{8,0},{12,28},{16,24},{20,4},{24,16},{28,12},{1,9},{5... | collective-permute-start | bytes 1351688 | tf_op jit(solution)/shard_map/ppermute | solution.py:560
  25.4 2.3 %copy-start = (f32[4,4096]{1,0:T(4,128)S(1)}, f32[4,4096]{1,0:T(4,128)}, u32[]{:S(2)}) copy-start(f32[4,4096]{1,0:T(4,128)} %refs_2_.7) | copy-start | bytes 196612
  25.5 7.0 %collective-permute-start.11 = (f32[6,2,64,128]{3,2,1,0:T(8,128)S(1)}, f32[6,2,64,128]{3,2,1,0:T(8,128)S(1)}, u32[]{:S(2)}, u32[]{:S(2)}) collective-permute-start(f32[6,2,64,128]{3,2,1,0:T(8,128)S(1)} %shard_map.123.refs_7_.refs_2_.refs_3_), channel_id=1, source_target_pairs={{0,16},{4,12},{8,24},{12,4},{16,0},{20,28},{24,8},{28,20},{1,17},{... | collective-permute-start | bytes 1179656 | tf_op jit(solution)/shard_map/ppermute | solution.py:560
  26.4 9.5 %collective-permute-start.8 = (f32[5,2,64,128]{3,2,1,0:T(8,128)S(1)}, f32[5,2,64,128]{3,2,1,0:T(8,128)S(1)}, u32[]{:S(2)}, u32[]{:S(2)}) collective-permute-start(f32[5,2,64,128]{3,2,1,0:T(8,128)S(1)} %shard_map.122.refs_6_.refs_2_.refs_3_), channel_id=1, source_target_pairs={{0,16},{4,12},{8,24},{12,4},{16,0},{20,28},{24,8},{28,20},{1,17},{... | collective-permute-start | bytes 983048 | tf_op jit(solution)/shard_map/ppermute | solution.py:560
  28.6 14.5 %collective-permute-start.6 = (f32[5,2,2,64,128]{4,3,2,1,0:T(8,128)S(1)}, f32[5,2,2,64,128]{4,3,2,1,0:T(8,128)S(1)}, u32[]{:S(2)}, u32[]{:S(2)}) collective-permute-start(f32[5,2,2,64,128]{4,3,2,1,0:T(8,128)S(1)} %shard_map.124.refs_3_.refs_4_), channel_id=1, source_target_pairs={{0,1},{1,0},{2,3},{3,2},{4,5},{5,4},{6,7},{7,6},{8,9},{9,8},{10,11... | collective-permute-start | bytes 1966088 | tf_op jit(solution)/shard_map/ppermute | solution.py:560
  28.7 16.4 %collective-permute-start.5 = (f32[5,2,2,64,128]{4,3,2,1,0:T(8,128)S(1)}, f32[5,2,2,64,128]{4,3,2,1,0:T(8,128)S(1)}, u32[]{:S(2)}, u32[]{:S(2)}) collective-permute-start(f32[5,2,2,64,128]{4,3,2,1,0:T(8,128)S(1)} %shard_map.124.refs_3_.refs_4_), channel_id=1, source_target_pairs={{1,2},{2,1},{5,6},{6,5},{9,10},{10,9},{13,14},{14,13},{17,18},{18,... | collective-permute-start | bytes 1966088 | tf_op jit(solution)/shard_map/ppermute | solution.py:560
  33.1 15.5 %collective-permute-start.12 = (f32[6,2,88,128]{3,2,1,0:T(8,128)S(1)}, f32[6,2,88,128]{3,2,1,0:T(8,128)S(1)}, u32[]{:S(2)}, u32[]{:S(2)}) collective-permute-start(f32[6,2,88,128]{3,2,1,0:T(8,128)S(1)} %shard_map.128), channel_id=1, source_target_pairs={{0,8},{4,20},{8,0},{12,28},{16,24},{20,4},{24,16},{28,12},{1,9},{5... | collective-permute-start | bytes 1622024 | tf_op jit(solution)/shard_map/ppermute | solution.py:560
  36.6 14.4 %copy-start.1 = (bf16[768,256]{1,0:T(8,128)(2,1)S(1)}, bf16[768,256]{1,0:T(8,128)(2,1)}, u32[]{:S(2)}) copy-start(bf16[768,256]{1,0:T(8,128)(2,1)} %constant.5.clone.refs_1_) | copy-start | bytes 1179652
  36.6 14.4 %copy-start.2 = (bf16[768,256]{1,0:T(8,128)(2,1)S(1)}, bf16[768,256]{1,0:T(8,128)(2,1)}, u32[]{:S(2)}) copy-start(bf16[768,256]{1,0:T(8,128)(2,1)} %constant.4.clone.refs_0_) | copy-start | bytes 1179652
  36.6 12.9 %collective-permute-start.9 = (f32[5,2,88,128]{3,2,1,0:T(8,128)S(1)}, f32[5,2,88,128]{3,2,1,0:T(8,128)S(1)}, u32[]{:S(2)}, u32[]{:S(2)}) collective-permute-start(f32[5,2,88,128]{3,2,1,0:T(8,128)S(1)} %shard_map.126), channel_id=1, source_target_pairs={{0,8},{4,20},{8,0},{12,28},{16,24},{20,4},{24,16},{28,12},{1,9},{5... | collective-permute-start | bytes 1351688 | tf_op jit(solution)/shard_map/ppermute | solution.py:560
  45.8 5.2 %collective-permute-start.7 = (f32[5,2,2,32,128]{4,3,2,1,0:T(8,128)S(1)}, f32[5,2,2,32,128]{4,3,2,1,0:T(8,128)S(1)}, u32[]{:S(2)}, u32[]{:S(2)}) collective-permute-start(f32[5,2,2,32,128]{4,3,2,1,0:T(8,128)S(1)} %get-tuple-element.18), channel_id=1, source_target_pairs={{0,4},{4,0},{8,12},{12,8},{16,20},{20,16},{24,28},{28,24},{1,5},{5... | collective-permute-start | bytes 983048 | tf_op jit(solution)/shard_map/ppermute | solution.py:560
  49.5 2.8 %collective-permute-start.13 = (f32[6,2,2,32,128]{4,3,2,1,0:T(8,128)S(1)}, f32[6,2,2,32,128]{4,3,2,1,0:T(8,128)S(1)}, u32[]{:S(2)}, u32[]{:S(2)}) collective-permute-start(f32[6,2,2,32,128]{4,3,2,1,0:T(8,128)S(1)} %get-tuple-element.22), channel_id=1, source_target_pairs={{0,4},{4,0},{8,12},{12,8},{16,20},{20,16},{24,28},{28,24},{1,5},{5... | collective-permute-start | bytes 1179656 | tf_op jit(solution)/shard_map/ppermute | solution.py:560
  50.4 1.8 %collective-permute-start.10 = (f32[5,2,2,32,128]{4,3,2,1,0:T(8,128)S(1)}, f32[5,2,2,32,128]{4,3,2,1,0:T(8,128)S(1)}, u32[]{:S(2)}, u32[]{:S(2)}) collective-permute-start(f32[5,2,2,32,128]{4,3,2,1,0:T(8,128)S(1)} %get-tuple-element.20), channel_id=1, source_target_pairs={{0,4},{4,0},{8,12},{12,8},{16,20},{20,16},{24,28},{28,24},{1,5},{5... | collective-permute-start | bytes 983048 | tf_op jit(solution)/shard_map/ppermute | solution.py:560
